TPU v7x, 32 devices: a whole 2x2x4 slice. The times are simulated.
32 devices in a mesh: parts: 2 (over y), row: 8 (over z, x), col: 2 (over core).
Axes of the slice: x: 2, y: 2, z: 4, core: 2. Of those that a mesh axis runs over, the one named last changes fastest.
Arguments:
- cells: bfloat16 [8, 8192], P(None, ('parts', 'row', 'col')), parts along dimension 1, may hold values from -6 to 6
- basis_t: bfloat16 [64, 32, 128], P(('parts', 'row', 'col')), parts along dimension 0, may hold values from -0.5 to 0.5
- near_blocks: bfloat16 [3072, 128, 128], P(('parts', 'row', 'col')), parts along dimension 0, may hold values from -0.0546875 to 0.0546875
- near_owner: int32 [3072, 1], P(('parts', 'row', 'col')), parts along dimension 0, may hold values from 0 to 7; in each aligned block of 96 rows (0 to 95, 96 to 191, ...) at most 24 rows name the same one
- near_col: int32 [3072, 1], P(('parts', 'row', 'col')), parts along dimension 0, may hold values from 0 to 3
- near_row: int32 [3072, 1], P(('parts', 'row', 'col')), parts along dimension 0, may hold values from 0 to 3
- far_row: int32 [4096, 1], P(('parts', 'row', 'col')), parts along dimension 0, may hold values from 0 to 31
- far_col: int32 [4096, 1], P(('parts', 'row', 'col')), parts along dimension 0, may hold values from 0 to 31
- coupling: bfloat16 [4096, 1024], P(('parts', 'row', 'col')), parts along dimension 0, may hold values from -0.09375 to 0.09375
Outputs:
- product: float32 [8, 8192], P(None, ('parts', 'row', 'col')), parts along dimension 1
There are 2 independent parts, one for each index of `parts`. A program takes and returns all parts, laid end to end along the dimension named above; each array names one. Nothing has to cross between parts.
Inputs may be any that keep to these rules, and one draw needn't show every extreme that they name: `near_owner`: in the 96 rows of one device no value appears more than 24 times; in some device one value appears exactly 24 times.
All inputs are finite; a program needn't handle non-finite values.
Results may differ from a plain program's by a relative error of at most 0.0003.
Values may be sent and summed in bfloat16 or wider, within the bound.
No kernel may reach another device: no remote copies, remote signals or barrier semaphores. Data moves between devices by JAX's collectives and lax.ppermute only.
A program may use at most 64 MiB of HBM per device.

v0:
```python
import jax
import jax.numpy as jnp
from jax import lax
from jax.sharding import PartitionSpec as P


def shards(cells, basis_t, near_blocks, near_owner, near_col, near_row, far_row, far_col, coupling):
    highest = lax.Precision.HIGHEST
    row_count = lax.axis_size("row")
    col_count = lax.axis_size("col")
    sides = cells.shape[0]
    owned = basis_t.shape[0]
    width = basis_t.shape[2]
    rank_size = basis_t.shape[1]
    row_clusters = owned * col_count
    all_clusters = row_clusters * row_count
    pairs = near_blocks.shape[0]
    capacity = 2 * ((pairs + row_count - 1) // row_count)
    slots = row_count * capacity
    row_cells = lax.all_gather(cells, "col", axis=1, tiled=True)
    row_view = row_cells.reshape(sides, row_clusters, width)
    owners = near_owner[:, 0]
    targets = near_col[:, 0]
    sources = near_row[:, 0]
    owner_hot = (owners[:, None] == jnp.arange(row_count, dtype=jnp.int32)[None, :]).astype(
        jnp.int32
    )
    earlier = jnp.sum((jnp.cumsum(owner_hot, axis=0) - owner_hot) * owner_hot, axis=1)
    position = owners * capacity + earlier
    placing = position[:, None] == jnp.arange(slots, dtype=jnp.int32)[None, :]
    wanted = jnp.sum(jnp.where(placing, targets[:, None] + 1, 0), axis=0)
    asked = lax.all_to_all(
        wanted.reshape(row_count, capacity), "row", split_axis=0, concat_axis=0, tiled=True
    )
    asked_hot = (
        asked.reshape(slots)[:, None] - 1 == jnp.arange(row_clusters, dtype=jnp.int32)[None, :]
    )
    source_hot = sources[:, None] == jnp.arange(row_clusters, dtype=jnp.int32)[None, :]
    reply = jnp.einsum(
        "ql,slb->qsb", asked_hot.astype(jnp.bfloat16), row_view, preferred_element_type=jnp.float32
    ).astype(jnp.bfloat16)
    arrived = lax.all_to_all(
        reply.reshape(row_count, capacity, sides, width),
        "row",
        split_axis=0,
        concat_axis=0,
        tiled=True,
    )
    far_cells = jnp.einsum(
        "pq,qsb->psb",
        placing.astype(jnp.bfloat16),
        arrived.reshape(slots, sides, width),
        preferred_element_type=jnp.float32,
    ).astype(jnp.bfloat16)
    mine_cells = jnp.einsum(
        "pl,slb->psb", source_hot.astype(jnp.bfloat16), row_view, preferred_element_type=jnp.float32
    ).astype(jnp.bfloat16)
    direct = jnp.einsum("pab,psb->psa", near_blocks, far_cells, preferred_element_type=jnp.float32)
    mirrored = jnp.einsum(
        "pab,psa->psb", near_blocks, mine_cells, preferred_element_type=jnp.float32
    )
    outgoing = jnp.einsum("pq,psb->qsb", placing.astype(jnp.float32), mirrored, precision=highest)
    incoming = lax.all_to_all(
        outgoing.reshape(row_count, capacity, sides, width),
        "row",
        split_axis=0,
        concat_axis=0,
        tiled=True,
    )
    row_total = jnp.einsum("pl,psb->slb", source_hot.astype(jnp.float32), direct, precision=highest)
    row_total = row_total + jnp.einsum(
        "ql,qsb->slb",
        asked_hot.astype(jnp.float32),
        incoming.reshape(slots, sides, width),
        precision=highest,
    )
    near_own = lax.psum_scatter(
        row_total.reshape(sides, row_clusters * width), "col", scatter_dimension=1, tiled=True
    )
    moments = jnp.einsum(
        "krb,skb->ksr",
        basis_t,
        cells.reshape(sides, owned, width),
        preferred_element_type=jnp.float32,
    )
    moments_every = lax.all_gather(
        moments.reshape(owned, sides * rank_size), ("row", "col"), axis=0, tiled=True
    )
    moments_every = moments_every.reshape(all_clusters, sides, rank_size)
    matrices = coupling.astype(jnp.float32).reshape(coupling.shape[0], rank_size, rank_size)
    first = far_row[:, 0]
    second = far_col[:, 0]
    to_first = jnp.einsum("qsk,qrk->qsr", moments_every[second], matrices, precision=highest)
    to_second = jnp.einsum("qsr,qrk->qsk", moments_every[first], matrices, precision=highest)
    spread = (
        jnp.zeros((all_clusters, sides, rank_size), jnp.float32)
        .at[first]
        .add(to_first)
        .at[second]
        .add(to_second)
    )
    spread = spread.reshape(all_clusters, sides * rank_size)
    coupled = lax.psum_scatter(spread, ("row", "col"), scatter_dimension=0, tiled=True)
    far_own = jnp.einsum(
        "krb,ksr->skb",
        basis_t.astype(jnp.float32),
        coupled.reshape(owned, sides, rank_size),
        precision=highest,
    )
    return near_own + far_own.reshape(sides, owned * width)


def solution(mesh):
    return jax.shard_map(
        shards,
        mesh=mesh,
        in_specs=(
            P(None, ("parts", "row", "col")),
            P(("parts", "row", "col"), None, None),
            P(("parts", "row", "col"), None, None),
            P(("parts", "row", "col"), None),
            P(("parts", "row", "col"), None),
            P(("parts", "row", "col"), None),
            P(("parts", "row", "col"), None),
            P(("parts", "row", "col"), None),
            P(("parts", "row", "col"), None),
        ),
        out_specs=P(None, ("parts", "row", "col")),
        check_vma=False,
    )
```

profile of v0, /device:TPU:0, one launch (start us, length us, event | category | flops | bytes accessed | tf_op | source)
XLA Modules:
  0.0 189.8 jit_solution(16351871974274225806)
XLA Ops:
  9.9 7.3 %all-to-all-start = ((s32[8,1,24]{2,1,0:T(1,128)}), s32[8,1,24]{2,1,0:T(1,128)S(1)}, u32[]{:S(2)}, u32[]{:S(2)}) async-start(s32[8,1,24]{2,1,0:T(1,128)} %all_to_all.12), calls=%async_computation | async-start | bytes 8192 | tf_op jit(solution)/shard_map/all_to_all | solution.py:32
  17.1 1.9 %all_gather.6 = bf16[8,512]{1,0:T(8,128)(2,1)S(1)} all-gather(bf16[8,256]{1,0:T(8,128)(2,1)} %param.9), channel_id=1, replica_groups=mesh['parts'=2,'row'=8,'col'=2] {'col'}, dimensions={1}, use_global_device_ids=true | all-gather | bytes 12288 | tf_op jit(solution)/shard_map/all_gather | solution.py:20
  20.9 1.4 fusion.2
  22.3 1.2 all-to-all-done
  24.8 4.8 %all-to-all-start.1 = ((bf16[8,24,8,128]{3,1,2,0:T(8,128)(2,1)}), bf16[8,24,8,128]{3,1,2,0:T(8,128)(2,1)S(1)}, u32[]{:S(2)}, u32[]{:S(2)}) async-start(bf16[8,24,8,128]{3,1,2,0:T(8,128)(2,1)} %copy.13), calls=%async_computation.1 | async-start | bytes 786432 | tf_op jit(solution)/shard_map/all_to_all | solution.py:42
  29.6 1.4 fusion.16
  31.0 2.1 %copy.20 = f32[8,24,8,128]{3,1,2,0:T(8,128)} copy(f32[8,24,8,128]{3,1,0,2:T(8,128)} %bitcast.61) | data formatting | bytes 1572864 | tf_op jit(solution)/shard_map/reshape | solution.py:64
  33.1 1.4 reshape.99
  37.5 4.1 %all-to-all-done.1 = bf16[8,24,8,128]{3,1,2,0:T(8,128)(2,1)S(1)} async-done(((bf16[8,24,8,128]{3,1,2,0:T(8,128)(2,1)}), bf16[8,24,8,128]{3,1,2,0:T(8,128)(2,1)S(1)}, u32[]{:S(2)}, u32[]{:S(2)}) %all-to-all-start.1) | async-done | bytes 393248 | tf_op jit(solution)/shard_map/all_to_all | solution.py:42
  41.6 4.2 %all-to-all-start.2 = ((f32[8,24,8,128]{3,1,2,0:T(8,128)}), f32[8,24,8,128]{3,1,2,0:T(8,128)}, u32[]{:S(2)}, u32[]{:S(2)}) async-start(f32[8,24,8,128]{3,1,2,0:T(8,128)} %copy.20), calls=%async_computation.2 | async-start | bytes 1572864 | tf_op jit(solution)/shard_map/all_to_all | solution.py:63
  45.9 29.3 %all-gather = f32[16,2,256]{2,1,0:T(2,128)} all-gather(f32[1,2,256]{2,1,0:T(2,128)} %reshape.99), channel_id=1, replica_groups=mesh['parts'=2,'row'=8,'col'=2] {'row','col'}, dimensions={0}, use_global_device_ids=true | all-gather | bytes 34816 | tf_op jit(solution)/shard_map/all_gather | solution.py:86
  76.1 1.1 copy.22
  77.2 2.3 %copy.23 = bf16[128,32,32]{2,1,0:T(8,128)(2,1)} copy(bf16[128,32,32]{0,2,1:T(8,128)(2,1)S(1)} %bitcast.65) | data formatting | bytes 524288 | tf_op jit(solution)/shard_map/reshape | solution.py:90
  79.5 1.8 gather_fusion
  81.3 1.7 gather_fusion.1
  83.0 3.9 %fusion.31 = f32[128,8,32]{2,1,0:T(8,128)} fusion(f32[128,8,32]{2,1,0:T(8,128)} %gather_fusion, bf16[128,32,32]{2,1,0:T(8,128)(2,1)} %copy.23), kind=kOutput, calls=%fused_computation.49 | convolution fusion | flops 12582912 | bytes 524288 | tf_op jit(solution)/shard_map/qsk,qrk->qsr/dot_general | solution.py:93
  87.0 9.5 %scatter_fusion = f32[32,8,32]{2,1,0:T(8,128)S(1)} fusion(f32[32,8,32]{2,1,0:T(8,128)S(1)} %broadcast_in_dim.29, s32[128]{0:T(128)S(1)} %copy-done.11, f32[128,8,32]{2,1,0:T(8,128)} %fusion.31), kind=kCustom, calls=%fused_computation.2 | custom fusion | flops 32768 | bytes 393728 | tf_op jit(solution)/shard_map/scatter-add | solution.py:98
  96.5 3.1 %fusion.32 = f32[128,8,32]{2,1,0:T(8,128)} fusion(f32[128,8,32]{2,1,0:T(8,128)} %gather_fusion.1, bf16[128,32,32]{2,1,0:T(8,128)(2,1)} %copy.23), kind=kOutput, calls=%fused_computation.50 | convolution fusion | flops 12582912 | bytes 524288 | tf_op jit(solution)/shard_map/qsr,qrk->qsk/dot_general | solution.py:94
  99.6 9.5 %scatter_fusion.1 = f32[32,8,32]{2,1,0:T(8,128)S(1)} fusion(f32[32,8,32]{2,1,0:T(8,128)S(1)} %scatter_fusion, s32[128]{0:T(128)S(1)} %copy-done.9, f32[128,8,32]{2,1,0:T(8,128)} %fusion.32), kind=kCustom, calls=%fused_computation.3 | custom fusion | flops 32768 | bytes 393728 | tf_op jit(solution)/shard_map/scatter-add | solution.py:100
  110.5 60.6 %all-reduce = f32[32,256]{1,0:T(8,128)S(1)} all-reduce(f32[32,256]{1,0:T(8,128)S(1)} %reshape.64), channel_id=3, replica_groups=mesh['parts'=2,'row'=8,'col'=2] {'row','col'}, use_global_device_ids=true, to_apply=%region_6.7.clone | all-reduce | flops 8192 | bytes 65536
  172.5 1.7 fusion.8
  174.5 1.2 copy.21
  176.8 4.7 %reduce-scatter.2.cloned.1.call-done = f32[8,256]{1,0:T(8,128)} async-done(((f32[8,512]{1,0:T(8,128)}), f32[8,256]{1,0:T(8,128)}) %reduce-scatter.2.cloned.1.call-update) | async-done | bytes 8208 | tf_op jit(solution)/shard_map/reduce_scatter | solution.py:77
  181.5 1.4 fusion.1
  (57 shorter events, 13.8 us)
Async XLA Ops:
  6.5 13.5 %copy-start = (bf16[96,128,128]{2,1,0:T(8,128)(2,1)S(1)}, bf16[96,128,128]{2,1,0:T(8,128)(2,1)}, u32[]{:S(2)}) copy-start(bf16[96,128,128]{2,1,0:T(8,128)(2,1)} %param.11) | copy-start | bytes 9437188
  9.1 15.7 %copy-start.5 = (s32[96]{0:T(128)}, s32[96]{0:T(128)S(1)}, u32[]{:S(2)}) copy-start(s32[96]{0:T(128)S(1)} %get-tuple-element.5) | copy-start | bytes 1156
  9.9 13.6 %all-to-all-start = ((s32[8,1,24]{2,1,0:T(1,128)}), s32[8,1,24]{2,1,0:T(1,128)S(1)}, u32[]{:S(2)}, u32[]{:S(2)}) async-start(s32[8,1,24]{2,1,0:T(1,128)} %all_to_all.12), calls=%async_computation | async-start | bytes 8192 | tf_op jit(solution)/shard_map/all_to_all | solution.py:32
  20.0 9.6 %copy-start.2 = (bf16[2,32,128]{2,1,0:T(8,128)(2,1)S(1)}, bf16[2,32,128]{2,1,0:T(8,128)(2,1)}, u32[]{:S(2)}) copy-start(bf16[2,32,128]{2,1,0:T(8,128)(2,1)} %param.10) | copy-start | bytes 49156
  23.6 1.1 copy-start.3
  24.8 16.9 %all-to-all-start.1 = ((bf16[8,24,8,128]{3,1,2,0:T(8,128)(2,1)}), bf16[8,24,8,128]{3,1,2,0:T(8,128)(2,1)S(1)}, u32[]{:S(2)}, u32[]{:S(2)}) async-start(bf16[8,24,8,128]{3,1,2,0:T(8,128)(2,1)} %copy.13), calls=%async_computation.1 | async-start | bytes 786432 | tf_op jit(solution)/shard_map/all_to_all | solution.py:42
  35.1 1.3 copy-start.8
  36.4 0.6 copy-start.10
  41.6 4.3 %copy-start.1 = (bf16[8,24,8,128]{3,1,2,0:T(8,128)(2,1)}, bf16[8,24,8,128]{3,1,2,0:T(8,128)(2,1)S(1)}, u32[]{:S(2)}) copy-start(bf16[8,24,8,128]{3,1,2,0:T(8,128)(2,1)S(1)} %all-to-all-done.1) | copy-start | bytes 1179652
  41.6 132.9 %all-to-all-start.2 = ((f32[8,24,8,128]{3,1,2,0:T(8,128)}), f32[8,24,8,128]{3,1,2,0:T(8,128)}, u32[]{:S(2)}, u32[]{:S(2)}) async-start(f32[8,24,8,128]{3,1,2,0:T(8,128)} %copy.20), calls=%async_computation.2 | async-start | bytes 1572864 | tf_op jit(solution)/shard_map/all_to_all | solution.py:63
  45.8 135.7 %reduce-scatter.2.cloned.1.call-start = ((), (), s32[]{:S(2)}) async-start(), calls=%async_computation.4 | async-start | bytes 24576 | tf_op jit(solution)/shard_map/reduce_scatter | solution.py:77
  79.5 7.4 %copy-start.11 = (s32[128]{0:T(128)S(1)}, s32[128]{0:T(128)}, u32[]{:S(2)}) copy-start(s32[128]{0:T(128)} %copy-done.10) | copy-start | bytes 1540
  83.0 16.6 %copy-start.9 = (s32[128]{0:T(128)S(1)}, s32[128]{0:T(128)}, u32[]{:S(2)}) copy-start(s32[128]{0:T(128)} %copy-done.8) | copy-start | bytes 1540
  86.9 22.3 %copy-start.12 = (u32[32]{0:T(128)S(1)}, u32[32]{0:T(128)}, u32[]{:S(2)}) copy-start(u32[32]{0:T(128)} %constant.21) | copy-start | bytes 388
  87.0 85.2 %copy-start.6 = (s32[96]{0:T(128)S(1)}, s32[96]{0:T(128)}, u32[]{:S(2)}) copy-start(s32[96]{0:T(128)} %copy-done.5) | copy-start | bytes 1156
  99.6 74.6 %copy-start.7 = (s32[96,1]{0,1:T(1,128)S(1)}, s32[96,1]{0,1:T(1,128)}, u32[]{:S(2)}) copy-start(s32[96,1]{0,1:T(1,128)} %param.14) | copy-start | bytes 1156
  172.2 3.5 %copy-start.4 = (s32[192]{0:T(256)S(1)}, s32[192]{0:T(256)}, u32[]{:S(2)}) copy-start(s32[192]{0:T(256)} %copy-done.3) | copy-start | bytes 2308
Sparse Core Ops, SparseCore 0:
  176.8 4.6 reduce-scatter.1
where the time goes:
time: 191 us; the launch traced here: 190 us
  blocking collectives  91.9 us (48%)
  other arithmetic  24.2 us (13%)
  local copies, waits for them, and re-layouts  17 us (9%)
  starting transfers between devices  16.3 us (9%)
  matrix products  16.1 us (8%)
  between operations  14.3 us (7%)
  waiting for transfers between devices  10 us (5%)
    unnamed x1, blocking collectives  60.6 us
    all_gather x1, blocking collectives, shards(): lax.all_gather(moments.reshape(owned, sides * rank_size), ('row', 'col'),...  29.3 us
    scatter-add x2, other arithmetic, shards(): spread = jnp.zeros((all_clusters, sides, rank_size), jnp.float32).at[firs...  19.1 us
    all_to_all x1, starting transfers between devices, shards(): lax.all_to_all(wanted.reshape(row_count, capacity), 'row', split_axis=0,...  7.25 us
    all_to_all x1, starting transfers between devices, shards(): lax.all_to_all(reply.reshape(row_count, capacity, sides, width), 'row', s...  4.8 us
    reduce_scatter x1, waiting for transfers between devices, shards(): lax.psum_scatter(row_total.reshape(sides, row_clusters * width), 'col', s...  4.74 us
    unnamed x31, local copies, waits for them, and re-layouts  4.29 us
    all_to_all x1, starting transfers between devices, shards(): lax.all_to_all(outgoing.reshape(row_count, capacity, sides, width), 'row'...  4.2 us
  transfers between devices with their start and end apart: 4, of which 3 were waited for; matrix products, arithmetic and copies ran while one was open for 26% of the time, Pallas kernels for 0%

commit v1 on v0

v1 whole, which is shorter than its diff:
```python
import jax
import jax.numpy as jnp
from jax import lax
from jax.experimental import pallas as pl
from jax.experimental.pallas import tpu as pltpu
from jax.sharding import PartitionSpec as P

f32 = jnp.float32
bf16 = jnp.bfloat16
LAST = (((1,), (1,)), ((), ()))
PLAIN = (((1,), (0,)), ((), ()))
FIRST = (((0,), (0,)), ((), ()))


def dot(left, right, dims):
    return lax.dot_general(left, right, dims, preferred_element_type=f32)


def halves(value):
    high = value.astype(bf16)
    return high, (value - high.astype(f32)).astype(bf16)


def side_mask(sides, rank):
    row = lax.broadcasted_iota(jnp.int32, (sides, sides * rank), 0)
    lane = lax.broadcasted_iota(jnp.int32, (sides, sides * rank), 1)
    return lane // rank == row


def pack_kernel(cells_ref, basis_ref, out_ref):
    sides = cells_ref.shape[0]
    owned, rank, width = basis_ref.shape
    mask = side_mask(sides, rank)
    high, low = [], []
    for k in range(owned):
        tiled = jnp.concatenate([basis_ref[k]] * sides, axis=0)
        every = dot(cells_ref[:, k * width : (k + 1) * width], tiled, LAST)
        flat = jnp.sum(jnp.where(mask, every, 0.0), axis=0, keepdims=True)
        part = flat.astype(bf16).astype(f32)
        high.append(part)
        low.append(flat - part)
    rest = jnp.zeros((out_ref.shape[1] - sides - 2 * owned, owned * width), f32)
    packed = jnp.concatenate([cells_ref[...].astype(f32)] + high + low + [rest], axis=0)
    packed = packed.astype(bf16)

    def store(d, _):
        out_ref[d] = packed
        return 0

    lax.fori_loop(0, out_ref.shape[0], store, 0, unroll=min(16, out_ref.shape[0]))


def turn_kernel(coupling_ref, by_row_ref, by_col_ref):
    count, size = coupling_ref.shape
    rank = round(size**0.5)
    for t in range(0, size, 128):
        by_row_ref[t : t + 128, :] = coupling_ref[:, t : t + 128].astype(f32).T
    for k in range(rank):
        by_col_ref[k * rank : (k + 1) * rank, :] = by_row_ref[pl.ds(k, rank, stride=rank), :]


def work_kernel(
    index_ref, first_ref, second_ref, every_ref, blocks_ref, by_row_ref, by_col_ref,
    out_ref, row_ref, left_ref, right_ref, to_first_ref, to_second_ref, *, unroll,
):
    devices, lines, lanes = every_ref.shape
    pairs, width, _ = blocks_ref.shape
    sides = out_ref.shape[1]
    count = first_ref.shape[1]
    rank = lanes // sides
    row_clusters = row_ref.shape[0]
    out_ref[...] = jnp.zeros(out_ref.shape, f32)
    row_ref[...] = jnp.zeros(row_ref.shape, f32)
    base = index_ref[2, 0]

    def place(c):
        return c >> 1, pl.ds(pl.multiple_of((c & 1) * width, width), width)

    def group(g, _):
        done = []
        for u in range(unroll):
            p = g * unroll + u
            block = blocks_ref[p]
            i = index_ref[0, p]
            j = index_ref[1, p]
            dj, lj = place(j)
            di, li = place(i + base)
            direct = dot(every_ref[dj, :, lj], block, LAST)
            mirrored = dot(every_ref[di, :, li], block, PLAIN)
            done.append((i, dj, lj, direct, mirrored))
        for i, dj, lj, direct, mirrored in done:
            row_ref[i] += direct[:sides]
            out_ref[dj, :, lj] += mirrored[:sides]
        return 0

    lax.fori_loop(0, pairs // unroll, group, 0)
    for i in range(row_clusters):
        d, l = place(base + i)
        out_ref[d, :, l] += row_ref[i]

    line = lax.broadcasted_iota(jnp.int32, (devices * lines, count), 0)
    hot = []
    for ref in (first_ref, second_ref):
        c = ref[...]
        at = (c >> 1) * lines + sides + (c & 1)
        hot.append(((line == at) | (line == at + 2)).astype(f32).astype(bf16))
    flat = every_ref[...].reshape(devices * lines, lanes)
    left_ref[...] = dot(flat, hot[0], FIRST)
    right_ref[...] = dot(flat, hot[1], FIRST)

    def couple(matrix_ref, moment_ref, result_ref):
        def step(r, sums):
            matrix = matrix_ref[pl.ds(pl.multiple_of(r * rank, rank), rank), :]
            return tuple(
                total + moment_ref[pl.ds(s * rank + r, 1), :] * matrix
                for s, total in enumerate(sums)
            )

        sums = tuple(jnp.zeros((rank, count), f32) for _ in range(sides))
        for s, total in enumerate(lax.fori_loop(0, rank, step, sums, unroll=4)):
            result_ref[s * rank : (s + 1) * rank, :] = total

    couple(by_col_ref, right_ref, to_first_ref)
    couple(by_row_ref, left_ref, to_second_ref)

    line = lax.broadcasted_iota(jnp.int32, (devices * sides, count), 0)
    within = line % sides
    cluster = jnp.where(within < 4, 2 * (line // sides) + within // 2, -1)
    hot_first = (cluster == first_ref[...]).astype(f32).astype(bf16)
    hot_second = (cluster == second_ref[...]).astype(f32).astype(bf16)
    hots = jnp.concatenate([hot_first, hot_first, hot_second, hot_second], axis=1)
    sums = jnp.concatenate(halves(to_first_ref[...]) + halves(to_second_ref[...]), axis=1)
    spread = dot(hots, sums, LAST)
    half = lanes // 2
    odd = lax.broadcasted_iota(jnp.int32, (devices * sides, half), 0) % 2 == 1
    spread = jnp.where(odd, spread[:, half:], spread[:, :half])
    out_ref[:, :, lanes : lanes + half] = spread.reshape(devices, sides, half)


def finish_kernel(parts_ref, basis_ref, out_ref):
    devices, sides, _ = parts_ref.shape
    owned, rank, width = basis_ref.shape
    lanes = owned * width
    half = lanes // 2

    def add(d, total):
        return total + parts_ref[d]

    total = lax.fori_loop(1, devices, add, parts_ref[0], unroll=min(15, devices - 1))
    mask = side_mask(sides, rank)
    for k in range(owned):
        flat = jnp.concatenate(
            [total[2 * k : 2 * k + 1, lanes:], total[2 * k + 1 : 2 * k + 2, lanes:]], axis=1
        )
        high, low = halves(jnp.where(mask, flat, 0.0))
        tiled = jnp.concatenate([basis_ref[k]] * sides, axis=0)
        far = dot(high, tiled, PLAIN) + dot(low, tiled, PLAIN)
        out_ref[:, k * width : (k + 1) * width] = total[:, k * width : (k + 1) * width] + far


def vmem(count):
    return [pl.BlockSpec(memory_space=pltpu.VMEM)] * count


def shards(cells, basis_t, near_blocks, near_owner, near_col, near_row, far_row, far_col, coupling):
    devices = lax.axis_size("row") * lax.axis_size("col")
    sides, lanes = cells.shape
    owned, rank, width = basis_t.shape
    row_clusters = owned * lax.axis_size("col")
    pairs = near_blocks.shape[0]
    count = coupling.shape[0]
    params = pltpu.CompilerParams(vmem_limit_bytes=16 * 1024 * 1024)
    packed = pl.pallas_call(
        pack_kernel,
        out_shape=jax.ShapeDtypeStruct((devices, 16, lanes), bf16),
        in_specs=vmem(2),
        out_specs=pl.BlockSpec(memory_space=pltpu.VMEM),
        compiler_params=params,
        name="pack",
    )(cells, basis_t)
    every = lax.all_to_all(packed, ("row", "col"), split_axis=0, concat_axis=0, tiled=True)
    by_row, by_col = pl.pallas_call(
        turn_kernel,
        out_shape=[jax.ShapeDtypeStruct((rank * rank, count), f32)] * 2,
        in_specs=vmem(1),
        out_specs=vmem(2),
        compiler_params=params,
        cost_estimate=pl.CostEstimate(flops=10**6, bytes_accessed=2 * 10**6, transcendentals=0),
        name="turn",
    )(coupling)
    base = lax.axis_index("row") * row_clusters
    index = jnp.stack(
        [
            near_row[:, 0],
            near_owner[:, 0] * row_clusters + near_col[:, 0],
            jnp.full((pairs,), base, jnp.int32),
        ]
    )
    partial = pl.pallas_call(
        lambda *refs: work_kernel(*refs, unroll=8),
        out_shape=jax.ShapeDtypeStruct((devices, sides, lanes + lanes // 2), f32),
        in_specs=[pl.BlockSpec(memory_space=pltpu.SMEM)] + vmem(6),
        out_specs=pl.BlockSpec(memory_space=pltpu.VMEM),
        scratch_shapes=[
            pltpu.VMEM((row_clusters, sides, width), f32),
            pltpu.VMEM((sides * rank, count), f32),
            pltpu.VMEM((sides * rank, count), f32),
            pltpu.VMEM((sides * rank, count), f32),
            pltpu.VMEM((sides * rank, count), f32),
        ],
        compiler_params=params,
        name="work",
    )(
        index,
        far_row.reshape(1, count),
        far_col.reshape(1, count),
        every,
        near_blocks,
        by_row,
        by_col,
    )
    parts = lax.all_to_all(partial, ("row", "col"), split_axis=0, concat_axis=0, tiled=True)
    return pl.pallas_call(
        finish_kernel,
        out_shape=jax.ShapeDtypeStruct((sides, lanes), f32),
        in_specs=vmem(2),
        out_specs=pl.BlockSpec(memory_space=pltpu.VMEM),
        compiler_params=params,
        name="finish",
    )(parts, basis_t)


def solution(mesh):
    split = ("parts", "row", "col")
    return jax.shard_map(
        shards,
        mesh=mesh,
        in_specs=(
            P(None, split),
            P(split, None, None),
            P(split, None, None),
            P(split, None),
            P(split, None),
            P(split, None),
            P(split, None),
            P(split, None),
            P(split, None),
        ),
        out_specs=P(None, split),
        check_vma=False,
    )
```

time: 191 us -> 39.3 us (0.21)
  blocking collectives: 91.9 us -> 11.6 us
  other arithmetic: 24.2 us -> 1.41 us
  matrix products: 16.1 us -> 0 us
  between operations: 14.3 us -> 0.04 us
  local copies, waits for them, and re-layouts: 17 us -> 5.63 us
  starting transfers between devices: 16.3 us -> 7.36 us
  Pallas kernels: 0 us -> 7.82 us
  waiting for transfers between devices: 10 us -> 5.03 us
    unnamed x1 -> x0, blocking collectives: 60.6 us -> none
    all_gather x2 -> x0, blocking collectives: 31.2 us -> none  [the longest x1 29.3 us: shards(): lax.all_gather(moments.reshape(owned, sides * rank_size), ('row', 'col'),...]
    scatter-add x2 -> x0, other arithmetic: 19.1 us -> none  [shards(): spread = jnp.zeros((all_clusters, sides, rank_size), jnp.float32).at[firs...]
    dot_general x12 -> x0, matrix products: 16.1 us -> none  [the longest x1 3.93 us: shards(): jnp.einsum('qsk,qrk->qsr', moments_every[second], matrices, precision=hig...]
    all_to_all x0 -> x1, blocking collectives: none -> 11.6 us  [shards(): lax.all_to_all(partial, ('row', 'col'), split_axis=0, concat_axis=0, tile...]
    all_to_all x3 -> x1, starting transfers between devices: 16.3 us -> 7.36 us  [shards(): lax.all_to_all(packed, ('row', 'col'), split_axis=0, concat_axis=0, tiled...]
    pallas_call x0 -> x4, Pallas kernels: none -> 7.82 us  [the longest x1 5.79 us: shards(): pl.pallas_call(lambda *refs: work_kernel(*refs, unroll=8), out_shape=jax....]
    reshape x7 -> x0, local copies, waits for them, and re-layouts: 6.27 us -> none  [the longest x1 2.32 us: shards(): coupling.astype(jnp.float32)]
  transfers between devices with their start and end apart: 4 -> 1, of which waited for: 3 -> 1; matrix products, arithmetic and copies ran while one was open for 26% -> 4% of each run, Pallas kernels for 0% -> 1%
where the time goes in v1:
time: 39.3 us; the launch traced here: 38.9 us
  blocking collectives  11.6 us (30%)
  Pallas kernels  7.82 us (20%)
  starting transfers between devices  7.36 us (19%)
  local copies, waits for them, and re-layouts  5.63 us (14%)
  waiting for transfers between devices  5.03 us (13%)
  other arithmetic  1.41 us (4%)
    all_to_all x1, blocking collectives, shards(): lax.all_to_all(partial, ('row', 'col'), split_axis=0, concat_axis=0, tile...  11.6 us
    all_to_all x1, starting transfers between devices, shards(): lax.all_to_all(packed, ('row', 'col'), split_axis=0, concat_axis=0, tiled...  7.36 us
    pallas_call x1, Pallas kernels, shards(): pl.pallas_call(lambda *refs: work_kernel(*refs, unroll=8), out_shape=jax....  5.79 us
    unnamed x14, local copies, waits for them, and re-layouts  5.56 us
    all_to_all x1, waiting for transfers between devices, shards(): lax.all_to_all(packed, ('row', 'col'), split_axis=0, concat_axis=0, tiled...  5.03 us
    pallas_call x1, Pallas kernels, shards(): pl.pallas_call(pack_kernel, out_shape=jax.ShapeDtypeStruct((devices, 16,...  0.81 us
  transfers between devices with their start and end apart: 1, of which 1 were waited for; matrix products, arithmetic and copies ran while one was open for 4% of the time, Pallas kernels for 1%

profile of v1, /device:TPU:0, one launch (start us, length us, event | category | flops | bytes accessed | tf_op | source)
XLA Modules:
  0.0 38.9 jit_solution(8233058716507461421)
XLA Ops:
  0.0 0.0 copy-start.2
  0.0 0.7 %copy-done.2 = bf16[2,32,128]{2,1,0:T(8,128)(2,1)S(1)} copy-done((bf16[2,32,128]{2,1,0:T(8,128)(2,1)S(1)}, bf16[2,32,128]{2,1,0:T(8,128)(2,1)}, u32[]{:S(2)}) %copy-start.2) | copy-done | bytes 16408
  0.7 0.0 copy-start.4
  0.7 0.7 %copy-done.4 = bf16[8,256]{1,0:T(8,128)(2,1)S(1)} copy-done((bf16[8,256]{1,0:T(8,128)(2,1)S(1)}, bf16[8,256]{1,0:T(8,128)(2,1)}, u32[]{:S(2)}) %copy-start.4) | copy-done | bytes 4120
  1.4 0.0 copy-start.3
  1.4 0.8 %pack.1 = bf16[16,16,256]{2,1,0:T(8,128)(2,1)} custom-call(bf16[8,256]{1,0:T(8,128)(2,1)S(1)} %copy-done.4, bf16[2,32,128]{2,1,0:T(8,128)(2,1)S(1)} %copy-done.2), custom_call_target="tpu_custom_call" | custom-call | tf_op jit(solution)/shard_map/pack/pallas_call | solution.py:173
  2.2 7.4 %all-to-all-start = ((bf16[16,16,256]{2,1,0:T(8,128)(2,1)}), bf16[16,16,256]{2,1,0:T(8,128)(2,1)S(1)}, u32[]{:S(2)}, u32[]{:S(2)}) async-start(bf16[16,16,256]{2,1,0:T(8,128)(2,1)} %pack.1), calls=%async_computation | async-start | bytes 262144 | tf_op jit(solution)/shard_map/all_to_all | solution.py:181
  9.6 0.7 %add_bitcast_fusion = s32[1,96]{1,0:T(1,128)S(1)} fusion(s32[96,1]{0,1:T(1,128)} %param.13, s32[96,1]{0,1:T(1,128)} %param.12), kind=kLoop, calls=%fused_computation.1 | loop fusion | flops 192 | bytes 1152 | tf_op jit(solution)/shard_map/add | solution.py:195
  10.3 0.1 pad.2.clone
  10.3 0.0 copy-start.1
  10.3 0.9 %copy-done.1 = bf16[128,1024]{1,0:T(8,128)(2,1)S(1)} copy-done((bf16[128,1024]{1,0:T(8,128)(2,1)S(1)}, bf16[128,1024]{1,0:T(8,128)(2,1)}, u32[]{:S(2)}) %copy-start.1) | copy-done | bytes 262168
  11.3 0.5 %turn.1 = (f32[1024,128]{1,0:T(8,128)S(1)}, f32[1024,128]{1,0:T(8,128)S(1)}) custom-call(bf16[128,1024]{1,0:T(8,128)(2,1)S(1)} %copy-done.1), custom_call_target="tpu_custom_call" | custom-call | flops 1000000 | bytes 2000000 | tf_op jit(solution)/shard_map/turn/pallas_call | solution.py:182
  11.8 0.7 %add_add_fusion.refs_0_ = s32[3,96]{1,0:T(4,128)S(1)} fusion(s32[1,96]{1,0:T(1,128)S(1)} %add_bitcast_fusion, s32[1,96]{1,0:T(1,128)} %bitcast.8, s32[3]{0:T(128)S(1)} %pad.2.clone), kind=kLoop, calls=%fused_computation | loop fusion | flops 576 | bytes 1932 | tf_op jit(solution)/shard_map/stack | solution.py:192
  12.5 5.0 %all-to-all-done.refs_3_ = bf16[16,16,256]{2,1,0:T(8,128)(2,1)S(1)} async-done(((bf16[16,16,256]{2,1,0:T(8,128)(2,1)}), bf16[16,16,256]{2,1,0:T(8,128)(2,1)S(1)}, u32[]{:S(2)}, u32[]{:S(2)}) %all-to-all-start) | async-done | bytes 131104 | tf_op jit(solution)/shard_map/all_to_all | solution.py:181
  17.5 0.0 copy-start
  17.5 1.9 %copy-done = bf16[96,128,128]{2,1,0:T(8,128)(2,1)S(1)} copy-done((bf16[96,128,128]{2,1,0:T(8,128)(2,1)S(1)}, bf16[96,128,128]{2,1,0:T(8,128)(2,1)}, u32[]{:S(2)}) %copy-start) | copy-done | bytes 3145752
  19.4 0.0 copy-start.5
  19.4 0.7 %copy-done.5 = s32[128,1]{0,1:T(1,128)S(1)} copy-done((s32[128,1]{0,1:T(1,128)S(1)}, s32[128,1]{0,1:T(1,128)}, u32[]{:S(2)}) %copy-start.5) | copy-done | bytes 536
  20.1 0.0 copy-start.6
  20.1 0.7 %copy-done.6 = s32[128,1]{0,1:T(1,128)S(1)} copy-done((s32[128,1]{0,1:T(1,128)S(1)}, s32[128,1]{0,1:T(1,128)}, u32[]{:S(2)}) %copy-start.6) | copy-done | bytes 536
  20.7 5.8 %work.1 = f32[16,8,384]{2,1,0:T(8,128)S(1)} custom-call(s32[3,96]{1,0:T(4,128)S(1)} %add_add_fusion.refs_0_, s32[1,128]{1,0:T(1,128)S(1)} %bitcast.6, s32[1,128]{1,0:T(1,128)S(1)} %bitcast.7, bf16[16,16,256]{2,1,0:T(8,128)(2,1)S(1)} %all-to-all-done.refs_3_, bf16[96,128,128]{2,1,0:T(8,128)(2,1)S(1)} %copy-done, f32[1024,128]{1,0:T(8,128)S(1)} %get-tuple-element.7.refs_5_, ...), custom_call_target="tpu_custom_call" | custom-call | tf_op jit(solution)/shard_map/work/pallas_call | solution.py:199
  26.5 11.6 %all_to_all.10.parts_ref = f32[16,8,384]{2,1,0:T(8,128)S(1)} all-to-all(f32[16,8,384]{2,1,0:T(8,128)S(1)} %work.1), channel_id=1, replica_groups=mesh['parts'=2,'row'=8,'col'=2] {'row','col'}, dimensions={0} | all-to-all | bytes 393216 | tf_op jit(solution)/shard_map/all_to_all | solution.py:222
  38.1 0.0 copy-done.3
  38.1 0.8 %finish.1 = f32[8,256]{1,0:T(8,128)} custom-call(f32[16,8,384]{2,1,0:T(8,128)S(1)} %all_to_all.10.parts_ref, bf16[2,32,128]{2,1,0:T(8,128)(2,1)S(1)} %copy-done.3), custom_call_target="tpu_custom_call" | custom-call | tf_op jit(solution)/shard_map/finish/pallas_call | solution.py:223
Async XLA Ops:
  0.0 0.7 %copy-start.2 = (bf16[2,32,128]{2,1,0:T(8,128)(2,1)S(1)}, bf16[2,32,128]{2,1,0:T(8,128)(2,1)}, u32[]{:S(2)}) copy-start(bf16[2,32,128]{2,1,0:T(8,128)(2,1)} %basis_ref.3) | copy-start | bytes 49156
  0.7 0.7 %copy-start.4 = (bf16[8,256]{1,0:T(8,128)(2,1)S(1)}, bf16[8,256]{1,0:T(8,128)(2,1)}, u32[]{:S(2)}) copy-start(bf16[8,256]{1,0:T(8,128)(2,1)} %cells_ref.1) | copy-start | bytes 12292
  1.4 36.7 %copy-start.3 = (bf16[2,32,128]{2,1,0:T(8,128)(2,1)S(1)}, bf16[2,32,128]{2,1,0:T(8,128)(2,1)}, u32[]{:S(2)}) copy-start(bf16[2,32,128]{2,1,0:T(8,128)(2,1)} %basis_ref.3) | copy-start | bytes 49156
  2.2 15.3 %all-to-all-start = ((bf16[16,16,256]{2,1,0:T(8,128)(2,1)}), bf16[16,16,256]{2,1,0:T(8,128)(2,1)S(1)}, u32[]{:S(2)}, u32[]{:S(2)}) async-start(bf16[16,16,256]{2,1,0:T(8,128)(2,1)} %pack.1), calls=%async_computation | async-start | bytes 262144 | tf_op jit(solution)/shard_map/all_to_all | solution.py:181
  10.3 0.9 %copy-start.1 = (bf16[128,1024]{1,0:T(8,128)(2,1)S(1)}, bf16[128,1024]{1,0:T(8,128)(2,1)}, u32[]{:S(2)}) copy-start(bf16[128,1024]{1,0:T(8,128)(2,1)} %coupling_ref.1) | copy-start | bytes 786436
  17.5 1.9 %copy-start = (bf16[96,128,128]{2,1,0:T(8,128)(2,1)S(1)}, bf16[96,128,128]{2,1,0:T(8,128)(2,1)}, u32[]{:S(2)}) copy-start(bf16[96,128,128]{2,1,0:T(8,128)(2,1)} %refs_4_.1) | copy-start | bytes 9437188
  19.4 0.7 %copy-start.5 = (s32[128,1]{0,1:T(1,128)S(1)}, s32[128,1]{0,1:T(1,128)}, u32[]{:S(2)}) copy-start(s32[128,1]{0,1:T(1,128)} %param.15) | copy-start | bytes 1540
  20.1 0.7 %copy-start.6 = (s32[128,1]{0,1:T(1,128)S(1)}, s32[128,1]{0,1:T(1,128)}, u32[]{:S(2)}) copy-start(s32[128,1]{0,1:T(1,128)} %param.16) | copy-start | bytes 1540

commit v2 on v1

v2 whole, which is shorter than its diff:
```python
import jax
import jax.numpy as jnp
from jax import lax
from jax.experimental import pallas as pl
from jax.experimental.pallas import tpu as pltpu
from jax.sharding import PartitionSpec as P

f32 = jnp.float32
bf16 = jnp.bfloat16
LAST = (((1,), (1,)), ((), ()))
PLAIN = (((1,), (0,)), ((), ()))
FIRST = (((0,), (0,)), ((), ()))
HBM = pl.BlockSpec(memory_space=pltpu.HBM)
VMEM = pl.BlockSpec(memory_space=pltpu.VMEM)
CHUNKS = 4
UNROLL = 8


def dot(left, right, dims):
    return lax.dot_general(left, right, dims, preferred_element_type=f32)


def halves(value):
    high = value.astype(bf16)
    return high, (value - high.astype(f32)).astype(bf16)


def one_hot(match):
    return match.astype(f32).astype(bf16)


def side_mask(sides, rank):
    row = lax.broadcasted_iota(jnp.int32, (sides, sides * rank), 0)
    lane = lax.broadcasted_iota(jnp.int32, (sides, sides * rank), 1)
    return lane // rank == row


def start(source, target, sem):
    copy = pltpu.make_async_copy(source, target, sem)
    copy.start()
    return copy


def in_hbm(array):
    return pltpu.with_memory_space_constraint(array, pltpu.HBM)


def place(cluster, width):
    return cluster >> 1, pl.ds(pl.multiple_of((cluster & 1) * width, width), width)


def pack_kernel(cells_hbm, basis_hbm, out_ref, mine_ref, cells_ref, basis_ref, sems):
    copies = [
        start(cells_hbm, cells_ref, sems.at[0]),
        start(basis_hbm, basis_ref, sems.at[1]),
    ]
    sides = cells_ref.shape[0]
    owned, rank, width = basis_ref.shape
    mask = side_mask(sides, rank)
    for copy in copies:
        copy.wait()
    high, low = [], []
    for k in range(owned):
        tiled = jnp.concatenate([basis_ref[k]] * sides, axis=0)
        every = dot(cells_ref[:, k * width : (k + 1) * width], tiled, LAST)
        flat = jnp.sum(jnp.where(mask, every, 0.0), axis=0, keepdims=True)
        part = flat.astype(bf16).astype(f32)
        high.append(part)
        low.append(flat - part)
    rest = jnp.zeros((mine_ref.shape[0] - sides - 2 * owned, owned * width), f32)
    packed = jnp.concatenate([cells_ref[...].astype(f32)] + high + low + [rest], axis=0)
    packed = packed.astype(bf16)
    mine_ref[...] = packed

    def store(d, _):
        out_ref[d] = packed
        return 0

    lax.fori_loop(0, out_ref.shape[0], store, 0, unroll=min(16, out_ref.shape[0]))


def near_copies(blocks_hbm, blocks_ref, sems, first):
    size = blocks_ref.shape[0] // CHUNKS
    return [
        start(blocks_hbm.at[pl.ds(c * size, size)], blocks_ref.at[pl.ds(c * size, size)], sems.at[first + c])
        for c in range(CHUNKS)
    ]


def near_loop(copies, pairs, body):
    size = pairs // CHUNKS
    for c, copy in enumerate(copies):
        copy.wait()

        def group(g, _, c=c):
            body([c * size + g * UNROLL + u for u in range(UNROLL)])
            return 0

        lax.fori_loop(0, size // UNROLL, group, 0)


def mirror_kernel(
    owner_hbm, col_hbm, row_hbm, first_hbm, second_hbm, coupling_hbm, blocks_hbm, mine_ref, other_ref,
    by_row_ref, by_col_ref, gather_ref, spread_ref, out_ref,
    owner, col, row, far, coupling_ref, blocks_ref, cells_ref, sems,
):
    small = [
        start(owner_hbm, owner, sems.at[0]),
        start(col_hbm, col, sems.at[1]),
        start(row_hbm, row, sems.at[2]),
        start(first_hbm, far.at[0], sems.at[3]),
        start(second_hbm, far.at[1], sems.at[4]),
        start(coupling_hbm, coupling_ref, sems.at[5]),
    ]
    copies = near_copies(blocks_hbm, blocks_ref, sems, 6)
    count, size = coupling_ref.shape
    rank = round(size**0.5)
    devices, sides, _ = out_ref.shape
    lines = gather_ref.shape[0] // devices
    pairs, width, _ = blocks_ref.shape
    row_clusters = 2 * cells_ref.shape[0]
    me = lax.axis_index("col")
    cells_ref[me] = mine_ref[...]
    cells_ref[1 - me] = other_ref[...]
    out_ref[...] = jnp.zeros(out_ref.shape, f32)

    for copy in small:
        copy.wait()
    line = lax.broadcasted_iota(jnp.int32, (devices * lines, count), 0)
    target = lax.broadcasted_iota(jnp.int32, (devices * sides, count), 0)
    within = target % sides
    cluster = jnp.where(within < 4, 2 * (target // sides) + within // 2, -1)
    for n in range(2):
        c = far[n]
        at = (c >> 1) * lines + sides + (c & 1)
        gather_ref[:, n * count : (n + 1) * count] = one_hot((line == at) | (line == at + 2))
        hot = one_hot(cluster == c)
        spread_ref[:, 2 * n * count : (2 * n + 1) * count] = hot
        spread_ref[:, (2 * n + 1) * count : (2 * n + 2) * count] = hot

    for t in range(0, size, 128):
        by_row_ref[t : t + 128, :] = coupling_ref[:, t : t + 128].astype(f32).T
    for k in range(rank):
        by_col_ref[k * rank : (k + 1) * rank, :] = by_row_ref[pl.ds(k, rank, stride=rank), :]

    def body(group):
        done = []
        for p in group:
            d, l = place(row[0, p], width)
            j = owner[0, p] * row_clusters + col[0, p]
            done.append((j, dot(cells_ref[d, :, l], blocks_ref[p], PLAIN)))
        for j, mirrored in done:
            d, l = place(j, width)
            out_ref[d, :, l] += mirrored[:sides]

    near_loop(copies, pairs, body)


def far_kernel(
    every_ref, gather_ref, spread_ref, by_row_ref, by_col_ref, near_ref,
    out_ref, left_ref, right_ref, to_first_ref, to_second_ref,
):
    devices, lines, lanes = every_ref.shape
    sides = out_ref.shape[1]
    count = left_ref.shape[1]
    rank = lanes // sides
    flat = every_ref[...].reshape(devices * lines, lanes)
    moments = dot(flat, gather_ref[...], FIRST)
    left_ref[...] = moments[:, :count]
    right_ref[...] = moments[:, count:]

    def couple(matrix_ref, moment_ref, result_ref):
        def step(r, sums):
            matrix = matrix_ref[pl.ds(pl.multiple_of(r * rank, rank), rank), :]
            return tuple(
                total + moment_ref[pl.ds(s * rank + r, 1), :] * matrix
                for s, total in enumerate(sums)
            )

        sums = tuple(jnp.zeros((rank, count), f32) for _ in range(sides))
        for s, total in enumerate(lax.fori_loop(0, rank, step, sums, unroll=4)):
            result_ref[s * rank : (s + 1) * rank, :] = total

    couple(by_col_ref, right_ref, to_first_ref)
    couple(by_row_ref, left_ref, to_second_ref)
    sums = jnp.concatenate(halves(to_first_ref[...]) + halves(to_second_ref[...]), axis=1)
    spread = dot(spread_ref[...], sums, LAST)
    half = lanes // 2
    odd = lax.broadcasted_iota(jnp.int32, (devices * sides, half), 0) % 2 == 1
    spread = jnp.where(odd, spread[:, half:], spread[:, :half])
    out_ref[:, :, :lanes] = near_ref[...]
    out_ref[:, :, lanes:] = spread.reshape(devices, sides, half)


def direct_kernel(
    owner_hbm, col_hbm, row_hbm, blocks_hbm, every_ref, out_ref, owner, col, row, blocks_ref, sems
):
    small = [
        start(owner_hbm, owner, sems.at[0]),
        start(col_hbm, col, sems.at[1]),
        start(row_hbm, row, sems.at[2]),
    ]
    copies = near_copies(blocks_hbm, blocks_ref, sems, 3)
    pairs, width, _ = blocks_ref.shape
    row_clusters = 2 * out_ref.shape[0]
    sides = out_ref.shape[1]
    out_ref[...] = jnp.zeros(out_ref.shape, f32)
    for copy in small:
        copy.wait()

    def body(group):
        done = []
        for p in group:
            d, l = place(owner[0, p] * row_clusters + col[0, p], width)
            done.append((row[0, p], dot(every_ref[d, :, l], blocks_ref[p], LAST)))
        for i, direct in done:
            d, l = place(i, width)
            out_ref[d, :, l] += direct[:sides]

    near_loop(copies, pairs, body)


def finish_kernel(parts_ref, mine_ref, other_ref, basis_ref, out_ref):
    devices, sides, _ = parts_ref.shape
    owned, rank, width = basis_ref.shape
    lanes = owned * width

    def add(d, total):
        return total + parts_ref[d]

    total = lax.fori_loop(1, devices, add, parts_ref[0], unroll=min(15, devices - 1))
    me = lax.axis_index("col")
    near = total[:, :lanes] + (mine_ref[me] + other_ref[me])
    mask = side_mask(sides, rank)
    for k in range(owned):
        flat = jnp.concatenate(
            [total[2 * k : 2 * k + 1, lanes:], total[2 * k + 1 : 2 * k + 2, lanes:]], axis=1
        )
        high, low = halves(jnp.where(mask, flat, 0.0))
        tiled = jnp.concatenate([basis_ref[k]] * sides, axis=0)
        far = dot(high, tiled, PLAIN) + dot(low, tiled, PLAIN)
        out_ref[:, k * width : (k + 1) * width] = near[:, k * width : (k + 1) * width] + far


def shards(cells, basis_t, near_blocks, near_owner, near_col, near_row, far_row, far_col, coupling):
    everyone = ("row", "col")
    devices = lax.axis_size("row") * lax.axis_size("col")
    sides, lanes = cells.shape
    owned, rank, width = basis_t.shape
    pairs = near_blocks.shape[0]
    count = coupling.shape[0]
    lines = 16
    swap = [(0, 1), (1, 0)]
    params = pltpu.CompilerParams(vmem_limit_bytes=24 * 1024 * 1024)

    def shaped(shape, dtype):
        return jax.ShapeDtypeStruct(shape, dtype)

    def cost(flops, moved):
        return pl.CostEstimate(flops=flops, bytes_accessed=moved, transcendentals=0)

    packed, mine = pl.pallas_call(
        pack_kernel,
        out_shape=[shaped((devices, lines, lanes), bf16), shaped((lines, lanes), bf16)],
        in_specs=[HBM] * 2,
        out_specs=[VMEM] * 2,
        scratch_shapes=[
            pltpu.VMEM(cells.shape, bf16),
            pltpu.VMEM(basis_t.shape, bf16),
            pltpu.SemaphoreType.DMA((2,)),
        ],
        compiler_params=params,
        name="pack",
    )(in_hbm(cells), in_hbm(basis_t))
    every = lax.all_to_all(packed, everyone, split_axis=0, concat_axis=0, tiled=True)
    other = lax.ppermute(mine, "col", swap)
    owner, column, line = [in_hbm(a.reshape(1, pairs)) for a in (near_owner, near_col, near_row)]
    first, second = [in_hbm(a.reshape(1, count)) for a in (far_row, far_col)]
    blocks = in_hbm(near_blocks)
    index_scratch = [pltpu.SMEM((1, pairs), jnp.int32)] * 3
    by_row, by_col, gather, spread, near = pl.pallas_call(
        mirror_kernel,
        out_shape=[
            shaped((rank * rank, count), f32),
            shaped((rank * rank, count), f32),
            shaped((devices * lines, 2 * count), bf16),
            shaped((devices * sides, 4 * count), bf16),
            shaped((devices, sides, lanes), f32),
        ],
        in_specs=[HBM] * 7 + [VMEM] * 2,
        out_specs=[VMEM] * 5,
        scratch_shapes=index_scratch
        + [
            pltpu.VMEM((2, 1, count), jnp.int32),
            pltpu.VMEM(coupling.shape, bf16),
            pltpu.VMEM(near_blocks.shape, bf16),
            pltpu.VMEM((2, lines, lanes), bf16),
            pltpu.SemaphoreType.DMA((6 + CHUNKS,)),
        ],
        compiler_params=params,
        cost_estimate=cost(2 * pairs * 16 * width * width, 10**7),
        name="mirror",
    )(owner, column, line, first, second, in_hbm(coupling), blocks, mine, other)
    partial = pl.pallas_call(
        far_kernel,
        out_shape=shaped((devices, sides, lanes + lanes // 2), f32),
        in_specs=[VMEM] * 6,
        out_specs=VMEM,
        scratch_shapes=[pltpu.VMEM((sides * rank, count), f32)] * 4,
        compiler_params=params,
        name="far",
    )(every, gather, spread, by_row, by_col, near)
    parts = lax.all_to_all(partial, everyone, split_axis=0, concat_axis=0, tiled=True)
    direct = pl.pallas_call(
        direct_kernel,
        out_shape=shaped((2, sides, lanes), f32),
        in_specs=[HBM] * 4 + [VMEM],
        out_specs=VMEM,
        scratch_shapes=index_scratch
        + [pltpu.VMEM(near_blocks.shape, bf16), pltpu.SemaphoreType.DMA((3 + CHUNKS,))],
        compiler_params=params,
        cost_estimate=cost(2 * pairs * 16 * width * width, 10**7),
        name="direct",
    )(owner, column, line, blocks, every)
    others = lax.ppermute(direct, "col", swap)
    return pl.pallas_call(
        finish_kernel,
        out_shape=shaped((sides, lanes), f32),
        in_specs=[VMEM] * 4,
        out_specs=VMEM,
        compiler_params=params,
        name="finish",
    )(parts, direct, others, basis_t)


def solution(mesh):
    split = ("parts", "row", "col")
    return jax.shard_map(
        shards,
        mesh=mesh,
        in_specs=(
            P(None, split),
            P(split, None, None),
            P(split, None, None),
            P(split, None),
            P(split, None),
            P(split, None),
            P(split, None),
            P(split, None),
            P(split, None),
        ),
        out_specs=P(None, split),
        check_vma=False,
    )
```

time: 39.3 us -> 32.5 us (0.83)
  blocking collectives: 11.6 us -> 0 us
  local copies, waits for them, and re-layouts: 5.63 us -> 0.01 us
  Pallas kernels: 7.82 us -> 12.3 us
  starting transfers between devices: 7.36 us -> 11.7 us
  waiting for transfers between devices: 5.03 us -> 7.91 us
  other arithmetic: 1.41 us -> 0 us
    all_to_all x1 -> x0, blocking collectives: 11.6 us -> none  [shards(): lax.all_to_all(partial, ('row', 'col'), split_axis=0, concat_axis=0, tile...]
    unnamed x14 -> x2, local copies, waits for them, and re-layouts: 5.56 us -> 0.01 us
    pallas_call x4 -> x5, Pallas kernels: 7.82 us -> 12.3 us  [the longest x1 4.25 us: shards(): pl.pallas_call(direct_kernel, out_shape=shaped((2, sides, lanes), f32), i...]
    all_to_all x1 -> x2, starting transfers between devices: 7.36 us -> 10.9 us  [the longest x1 7.37 us: shards(): lax.all_to_all(packed, everyone, split_axis=0, concat_axis=0, tiled=True)]
    ppermute x0 -> x2, waiting for transfers between devices: none -> 1.7 us  [the longest x1 0.88 us: shards(): others = lax.ppermute(direct, 'col', swap)]
    all_to_all x1 -> x2, waiting for transfers between devices: 5.03 us -> 6.21 us  [the longest x1 3.46 us: shards(): lax.all_to_all(partial, everyone, split_axis=0, concat_axis=0, tiled=True)]
    ppermute x0 -> x2, starting transfers between devices: none -> 0.78 us  [the longest x1 0.41 us: shards(): other = lax.ppermute(mine, 'col', swap)]
    another operation x1 -> x0, other arithmetic: 0.73 us -> none  [shards(): jnp.stack([near_row[:, 0], near_owner[:, 0] * row_clusters + near_col[:,...]
  transfers between devices with their start and end apart: 1 -> 4, of which waited for: 1 -> 4; matrix products, arithmetic and copies ran while one was open for 4% -> 0% of each run, Pallas kernels for 1% -> 26%
where the time goes in v2:
time: 32.5 us; the launch traced here: 32 us
  Pallas kernels  12.3 us (38%)
  starting transfers between devices  11.7 us (36%)
  waiting for transfers between devices  7.91 us (24%)
    all_to_all x1, starting transfers between devices, shards(): lax.all_to_all(packed, everyone, split_axis=0, concat_axis=0, tiled=True)  7.37 us
    pallas_call x1, Pallas kernels, shards(): pl.pallas_call(direct_kernel, out_shape=shaped((2, sides, lanes), f32), i...  4.25 us
    pallas_call x1, Pallas kernels, shards(): pl.pallas_call(mirror_kernel, out_shape=[shaped((rank * rank, count), f32...  3.92 us
    all_to_all x1, starting transfers between devices, shards(): lax.all_to_all(partial, everyone, split_axis=0, concat_axis=0, tiled=True)  3.52 us
    all_to_all x1, waiting for transfers between devices, shards(): lax.all_to_all(partial, everyone, split_axis=0, concat_axis=0, tiled=True)  3.46 us
    all_to_all x1, waiting for transfers between devices, shards(): lax.all_to_all(packed, everyone, split_axis=0, concat_axis=0, tiled=True)  2.75 us
    pallas_call x1, Pallas kernels, shards(): pl.pallas_call(far_kernel, out_shape=shaped((devices, sides, lanes + lane...  1.84 us
    pallas_call x1, Pallas kernels, shards(): pl.pallas_call(pack_kernel, out_shape=[shaped((devices, lines, lanes), bf...  1.56 us
  transfers between devices with their start and end apart: 4, of which 4 were waited for; matrix products, arithmetic and copies ran while one was open for 0% of the time, Pallas kernels for 26%

profile of v2, /device:TPU:0, one launch (start us, length us, event | category | flops | bytes accessed | tf_op | source)
XLA Modules:
  0.0 32.0 jit_solution(11833041061463565022)
XLA Ops:
  0.0 1.6 %pack.1 = (bf16[16,16,256]{2,1,0:T(8,128)(2,1)}, bf16[16,256]{1,0:T(8,128)(2,1)S(1)}) custom-call(bf16[8,256]{1,0:T(8,128)(2,1)} %cells_hbm.1, bf16[2,32,128]{2,1,0:T(8,128)(2,1)} %basis_ref.1), custom_call_target="tpu_custom_call" | custom-call | tf_op jit(solution)/shard_map/pack/pallas_call | solution.py:262
  1.6 7.4 %all-to-all-start = ((bf16[16,16,256]{2,1,0:T(8,128)(2,1)}), bf16[16,16,256]{2,1,0:T(8,128)(2,1)S(1)}, u32[]{:S(2)}, u32[]{:S(2)}) async-start(bf16[16,16,256]{2,1,0:T(8,128)(2,1)} %get-tuple-element.12), calls=%async_computation | async-start | bytes 262144 | tf_op jit(solution)/shard_map/all_to_all | solution.py:275
  8.9 0.4 %collective-permute-start = (bf16[16,256]{1,0:T(8,128)(2,1)S(1)}, bf16[16,256]{1,0:T(8,128)(2,1)S(1)}, u32[]{:S(2)}, u32[]{:S(2)}) collective-permute-start(bf16[16,256]{1,0:T(8,128)(2,1)S(1)} %get-tuple-element.13.mine_ref), channel_id=1, source_target_pairs={{0,1},{1,0},{2,3},{3,2},{4,5},{5,4},{6,7},{7,6},{8,9},{9,8},{10,11... | collective-permute-start | bytes 24584 | tf_op jit(solution)/shard_map/ppermute | solution.py:276
  9.4 0.8 %collective-permute-done.other_ref = bf16[16,256]{1,0:T(8,128)(2,1)S(1)} collective-permute-done((bf16[16,256]{1,0:T(8,128)(2,1)S(1)}, bf16[16,256]{1,0:T(8,128)(2,1)S(1)}, u32[]{:S(2)}, u32[]{:S(2)}) %collective-permute-start) | collective-permute-done | bytes 8224 | tf_op jit(solution)/shard_map/ppermute | solution.py:276
  10.2 3.9 %mirror.1 = (f32[1024,128]{1,0:T(8,128)S(1)}, f32[1024,128]{1,0:T(8,128)S(1)}, bf16[256,256]{1,0:T(8,128)(2,1)S(1)}, bf16[128,512]{1,0:T(8,128)(2,1)S(1)}, f32[16,8,256]{2,1,0:T(8,128)S(1)}) custom-call(s32[1,96]{1,0:T(1,128)} %bitcast.5, s32[1,96]{1,0:T(1,128)} %bitcast.7, s32[1,96]{1,0:T(1,128)} %bitcast.9, s32[1,128]{1,0:T(1,128)} %bitcast.11, ...), custom_call_target="tpu_custom_call" | custom-call | flops 50331648 | bytes 10000000 | tf_op jit(solution)/shard_map/mirror/pallas_call | solution.py:281
  14.1 0.0 copy-start
  14.1 2.8 %all-to-all-done.every_ref = bf16[16,16,256]{2,1,0:T(8,128)(2,1)S(1)} async-done(((bf16[16,16,256]{2,1,0:T(8,128)(2,1)}), bf16[16,16,256]{2,1,0:T(8,128)(2,1)S(1)}, u32[]{:S(2)}, u32[]{:S(2)}) %all-to-all-start) | async-done | bytes 131104 | tf_op jit(solution)/shard_map/all_to_all | solution.py:275
  16.9 1.8 %far.1 = f32[16,8,384]{2,1,0:T(8,128)} custom-call(bf16[16,16,256]{2,1,0:T(8,128)(2,1)S(1)} %all-to-all-done.every_ref, bf16[256,256]{1,0:T(8,128)(2,1)S(1)} %get-tuple-element.14.gather_ref, bf16[128,512]{1,0:T(8,128)(2,1)S(1)} %get-tuple-element.15.spread_ref, f32[1024,128]{1,0:T(8,128)S(1)} %get-tuple-element.16.by_row_ref, ...), custom_call_target="tpu_custom_call" | custom-call | tf_op jit(solution)/shard_map/far/pallas_call | solution.py:304
  18.7 3.5 %all-to-all-start.1 = ((f32[16,8,384]{2,1,0:T(8,128)}), f32[16,8,384]{2,1,0:T(8,128)S(1)}, u32[]{:S(2)}, u32[]{:S(2)}) async-start(f32[16,8,384]{2,1,0:T(8,128)} %far.1), calls=%async_computation.1 | async-start | bytes 393216 | tf_op jit(solution)/shard_map/all_to_all | solution.py:313
  22.3 4.3 %direct.1.mine_ref = f32[2,8,256]{2,1,0:T(8,128)S(1)} custom-call(s32[1,96]{1,0:T(1,128)} %bitcast.6, s32[1,96]{1,0:T(1,128)} %bitcast.8, s32[1,96]{1,0:T(1,128)} %bitcast.10, bf16[96,128,128]{2,1,0:T(8,128)(2,1)} %blocks_hbm.3, bf16[16,16,256]{2,1,0:T(8,128)(2,1)S(1)} %all-to-all-done.every_ref), custom_call_target="tpu_custom_call" | custom-call | flops 50331648 | bytes 10000000 | tf_op jit(solution)/shard_map/direct/pallas_call | solution.py:314
  26.5 0.4 %collective-permute-start.1 = (f32[2,8,256]{2,1,0:T(8,128)S(1)}, f32[2,8,256]{2,1,0:T(8,128)S(1)}, u32[]{:S(2)}, u32[]{:S(2)}) collective-permute-start(f32[2,8,256]{2,1,0:T(8,128)S(1)} %direct.1.mine_ref), channel_id=1, source_target_pairs={{0,1},{1,0},{2,3},{3,2},{4,5},{5,4},{6,7},{7,6},{8,9},{9,8},{10,11... | collective-permute-start | bytes 49160 | tf_op jit(solution)/shard_map/ppermute | solution.py:325
  26.9 0.9 %collective-permute-done.1.other_ref = f32[2,8,256]{2,1,0:T(8,128)S(1)} collective-permute-done((f32[2,8,256]{2,1,0:T(8,128)S(1)}, f32[2,8,256]{2,1,0:T(8,128)S(1)}, u32[]{:S(2)}, u32[]{:S(2)}) %collective-permute-start.1) | collective-permute-done | bytes 16416 | tf_op jit(solution)/shard_map/ppermute | solution.py:325
  27.8 3.5 %all-to-all-done.1.parts_ref = f32[16,8,384]{2,1,0:T(8,128)S(1)} async-done(((f32[16,8,384]{2,1,0:T(8,128)}), f32[16,8,384]{2,1,0:T(8,128)S(1)}, u32[]{:S(2)}, u32[]{:S(2)}) %all-to-all-start.1) | async-done | bytes 196640 | tf_op jit(solution)/shard_map/all_to_all | solution.py:313
  31.2 0.0 copy-done
  31.2 0.8 %finish.1 = f32[8,256]{1,0:T(8,128)} custom-call(f32[16,8,384]{2,1,0:T(8,128)S(1)} %all-to-all-done.1.parts_ref, f32[2,8,256]{2,1,0:T(8,128)S(1)} %direct.1.mine_ref, f32[2,8,256]{2,1,0:T(8,128)S(1)} %collective-permute-done.1.other_ref, bf16[2,32,128]{2,1,0:T(8,128)(2,1)S(1)} %copy-done), custom_call_target="tpu_custom_call" | custom-call | tf_op jit(solution)/shard_map/finish/pallas_call | solution.py:326
Async XLA Ops:
  1.6 15.3 %all-to-all-start = ((bf16[16,16,256]{2,1,0:T(8,128)(2,1)}), bf16[16,16,256]{2,1,0:T(8,128)(2,1)S(1)}, u32[]{:S(2)}, u32[]{:S(2)}) async-start(bf16[16,16,256]{2,1,0:T(8,128)(2,1)} %get-tuple-element.12), calls=%async_computation | async-start | bytes 262144 | tf_op jit(solution)/shard_map/all_to_all | solution.py:275
  8.9 1.2 %collective-permute-start = (bf16[16,256]{1,0:T(8,128)(2,1)S(1)}, bf16[16,256]{1,0:T(8,128)(2,1)S(1)}, u32[]{:S(2)}, u32[]{:S(2)}) collective-permute-start(bf16[16,256]{1,0:T(8,128)(2,1)S(1)} %get-tuple-element.13.mine_ref), channel_id=1, source_target_pairs={{0,1},{1,0},{2,3},{3,2},{4,5},{5,4},{6,7},{7,6},{8,9},{9,8},{10,11... | collective-permute-start | bytes 24584 | tf_op jit(solution)/shard_map/ppermute | solution.py:276
  14.1 17.1 %copy-start = (bf16[2,32,128]{2,1,0:T(8,128)(2,1)S(1)}, bf16[2,32,128]{2,1,0:T(8,128)(2,1)}, u32[]{:S(2)}) copy-start(bf16[2,32,128]{2,1,0:T(8,128)(2,1)} %basis_ref.1) | copy-start | bytes 49156
  18.7 12.5 %all-to-all-start.1 = ((f32[16,8,384]{2,1,0:T(8,128)}), f32[16,8,384]{2,1,0:T(8,128)S(1)}, u32[]{:S(2)}, u32[]{:S(2)}) async-start(f32[16,8,384]{2,1,0:T(8,128)} %far.1), calls=%async_computation.1 | async-start | bytes 393216 | tf_op jit(solution)/shard_map/all_to_all | solution.py:313
  26.5 1.2 %collective-permute-start.1 = (f32[2,8,256]{2,1,0:T(8,128)S(1)}, f32[2,8,256]{2,1,0:T(8,128)S(1)}, u32[]{:S(2)}, u32[]{:S(2)}) collective-permute-start(f32[2,8,256]{2,1,0:T(8,128)S(1)} %direct.1.mine_ref), channel_id=1, source_target_pairs={{0,1},{1,0},{2,3},{3,2},{4,5},{5,4},{6,7},{7,6},{8,9},{9,8},{10,11... | collective-permute-start | bytes 49160 | tf_op jit(solution)/shard_map/ppermute | solution.py:325

commit v3 on v2

v3 whole, which is shorter than its diff:
```python
import jax
import jax.numpy as jnp
from jax import lax
from jax.experimental import pallas as pl
from jax.experimental.pallas import tpu as pltpu
from jax.sharding import Mesh, PartitionSpec as P

f32 = jnp.float32
bf16 = jnp.bfloat16
LAST = (((1,), (1,)), ((), ()))
PLAIN = (((1,), (0,)), ((), ()))
FIRST = (((0,), (0,)), ((), ()))
HBM = pl.BlockSpec(memory_space=pltpu.HBM)
VMEM = pl.BlockSpec(memory_space=pltpu.VMEM)
CHUNKS = 4
UNROLL = 8
GROUP = ("x", "col", "z")


def dot(left, right, dims):
    return lax.dot_general(left, right, dims, preferred_element_type=f32)


def halves(value):
    high = value.astype(bf16)
    return high, (value - high.astype(f32)).astype(bf16)


def one_hot(match):
    return match.astype(f32).astype(bf16)


def side_mask(sides, rank):
    row = lax.broadcasted_iota(jnp.int32, (sides, sides * rank), 0)
    lane = lax.broadcasted_iota(jnp.int32, (sides, sides * rank), 1)
    return lane // rank == row


def start(source, target, sem):
    copy = pltpu.make_async_copy(source, target, sem)
    copy.start()
    return copy


def in_hbm(array):
    return pltpu.with_memory_space_constraint(array, pltpu.HBM)


def slot_of(cluster, inner):
    depth, width = inner
    device = cluster >> 1
    return lax.rem(device, width) * depth + lax.div(device, width)


def each(count, body):
    if count <= 16:
        for d in range(count):
            body(d)
    else:
        pl.loop(0, count)(body)


def pack_kernel(cells_hbm, basis_hbm, out_hbm, mine_ref, cells_ref, basis_ref, out_ref, sems):
    copies = [
        start(cells_hbm, cells_ref, sems.at[0]),
        start(basis_hbm, basis_ref, sems.at[1]),
    ]
    sides = cells_ref.shape[0]
    owned, rank, width = basis_ref.shape
    mask = side_mask(sides, rank)
    for copy in copies:
        copy.wait()
    mine_ref[...] = cells_ref[...]
    cells = cells_ref[...].astype(f32)
    blocks, lines = [], []
    for k in range(owned):
        part = cells[:, k * width : (k + 1) * width]
        blocks += [part[:4], part[4:]]
        tiled = jnp.concatenate([basis_ref[k]] * sides, axis=0)
        every = dot(cells_ref[:, k * width : (k + 1) * width], tiled, LAST)
        flat = jnp.sum(jnp.where(mask, every, 0.0), axis=0, keepdims=True)
        lines += [flat[:, :128], flat[:, 128:]]
    blocks.append(jnp.concatenate(lines, axis=0))

    def store(d):
        for b, block in enumerate(blocks):
            out_ref[d, b] = block

    each(out_ref.shape[0], store)
    start(out_ref, out_hbm, sems.at[0]).wait()


def near_copies(blocks_hbm, blocks_ref, sems, first):
    size = blocks_ref.shape[0] // CHUNKS
    return [
        start(blocks_hbm.at[pl.ds(c * size, size)], blocks_ref.at[pl.ds(c * size, size)], sems.at[first + c])
        for c in range(CHUNKS)
    ]


def near_loop(copies, pairs, body):
    size = pairs // CHUNKS
    for c, copy in enumerate(copies):
        copy.wait()

        def group(g, _, c=c):
            body([c * size + g * UNROLL + u for u in range(UNROLL)])
            return 0

        lax.fori_loop(0, size // UNROLL, group, 0)


def mirror_kernel(
    owner_hbm, col_hbm, row_hbm, first_hbm, second_hbm, coupling_hbm, blocks_hbm, mine_ref, other_ref,
    by_row_ref, by_col_ref, gather_ref, spread_ref, out_ref,
    owner, col, row, far, coupling_ref, blocks_ref, cells_ref, sums_ref, sems, *, inner,
):
    small = [
        start(owner_hbm, owner, sems.at[0]),
        start(col_hbm, col, sems.at[1]),
        start(row_hbm, row, sems.at[2]),
        start(first_hbm, far.at[0], sems.at[3]),
        start(second_hbm, far.at[1], sems.at[4]),
        start(coupling_hbm, coupling_ref, sems.at[5]),
    ]
    copies = near_copies(blocks_hbm, blocks_ref, sems, 6)
    count, size = coupling_ref.shape
    rank = round(size**0.5)
    devices = out_ref.shape[0]
    pairs, width, _ = blocks_ref.shape
    row_clusters = cells_ref.shape[0]
    me = lax.axis_index("col")
    for k in range(2):
        cells_ref[2 * me + k] = mine_ref[:, k * width : (k + 1) * width].astype(f32)
        cells_ref[2 - 2 * me + k] = other_ref[:, k * width : (k + 1) * width].astype(f32)
    sums_ref[...] = jnp.zeros(sums_ref.shape, f32)

    for copy in small:
        copy.wait()
    line = lax.broadcasted_iota(jnp.int32, (4 * devices, count), 0)
    for n in range(2):
        c = far[n]
        at = 4 * slot_of(c, inner) + 2 * (c & 1)
        low, high = line == at, line == at + 1
        for h, match in enumerate((low, high)):
            hot = one_hot(match)
            column = (2 * n + h) * count
            gather_ref[: 4 * devices, column : column + count] = hot
            gather_ref[4 * devices :, column : column + count] = hot
        hot = one_hot(low | high)
        spread_ref[:, 2 * n * count : (2 * n + 1) * count] = hot
        spread_ref[:, (2 * n + 1) * count : (2 * n + 2) * count] = hot

    for t in range(0, size, 128):
        by_row_ref[t : t + 128, :] = coupling_ref[:, t : t + 128].astype(f32).T
    for k in range(rank):
        by_col_ref[k * rank : (k + 1) * rank, :] = by_row_ref[pl.ds(k, rank, stride=rank), :]

    def body(group):
        done = []
        for p in group:
            j = owner[0, p] * row_clusters + col[0, p]
            at = 2 * slot_of(j, inner) + (j & 1)
            done.append((at, dot(cells_ref[row[0, p]].astype(bf16), blocks_ref[p], PLAIN)))
        for at, mirrored in done:
            sums_ref[at] += mirrored

    near_loop(copies, pairs, body)

    def store(d):
        for k in range(2):
            out_ref[d, 2 * k] = sums_ref[2 * d + k, :4, :]
            out_ref[d, 2 * k + 1] = sums_ref[2 * d + k, 4:, :]

    each(devices, store)


def far_kernel(
    every_ref, gather_ref, spread_ref, by_row_ref, by_col_ref, near_ref,
    out_hbm, moment_ref, left_ref, right_ref, to_first_ref, to_second_ref, lines_ref, far_ref, sems,
):
    near = start(near_ref, out_hbm.at[:, pl.ds(0, 4)], sems.at[0])
    devices = every_ref.shape[0]
    size, count = left_ref.shape
    sides = 8
    rank = size // sides

    def load(d):
        moment_ref[pl.ds(4 * d, 4), :] = every_ref[d, 4]

    each(devices, load)
    moments = dot(jnp.concatenate(halves(moment_ref[...]), axis=0), gather_ref[...], FIRST)
    for h in range(2):
        left_ref[h * 128 : (h + 1) * 128, :] = moments[:, h * count : (h + 1) * count]
        right_ref[h * 128 : (h + 1) * 128, :] = moments[:, (2 + h) * count : (3 + h) * count]

    def couple(matrix_ref, moment_ref, result_ref):
        def step(r, sums):
            matrix = matrix_ref[pl.ds(pl.multiple_of(r * rank, rank), rank), :]
            return tuple(
                total + moment_ref[pl.ds(s * rank + r, 1), :] * matrix
                for s, total in enumerate(sums)
            )

        sums = tuple(jnp.zeros((rank, count), f32) for _ in range(sides))
        for s, total in enumerate(lax.fori_loop(0, rank, step, sums, unroll=4)):
            result_ref[s * rank : (s + 1) * rank, :] = total

    couple(by_col_ref, right_ref, to_first_ref)
    couple(by_row_ref, left_ref, to_second_ref)
    sums = jnp.concatenate(halves(to_first_ref[...]) + halves(to_second_ref[...]), axis=1)
    spread = dot(spread_ref[...], sums, LAST)
    odd = lax.broadcasted_iota(jnp.int32, (4 * devices, 128), 0) % 2 == 1
    lines_ref[...] = jnp.where(odd, spread[:, 128:], spread[:, :128])

    def store(d):
        far_ref[d, 0] = lines_ref[pl.ds(4 * d, 4), :]

    each(devices, store)
    far = start(far_ref, out_hbm.at[:, pl.ds(4, 1)], sems.at[1])
    near.wait()
    far.wait()


def direct_kernel(
    owner_hbm, col_hbm, row_hbm, blocks_hbm, every_ref,
    out_ref, owner, col, row, blocks_ref, cells_ref, sems, *, inner,
):
    small = [
        start(owner_hbm, owner, sems.at[0]),
        start(col_hbm, col, sems.at[1]),
        start(row_hbm, row, sems.at[2]),
    ]
    copies = near_copies(blocks_hbm, blocks_ref, sems, 3)
    pairs = blocks_ref.shape[0]
    row_clusters = out_ref.shape[0]
    out_ref[...] = jnp.zeros(out_ref.shape, f32)

    def load(d):
        for k in range(2):
            cells_ref[2 * d + k] = jnp.concatenate([every_ref[d, 2 * k], every_ref[d, 2 * k + 1]], axis=0)

    each(every_ref.shape[0], load)
    for copy in small:
        copy.wait()

    def body(group):
        done = []
        for p in group:
            j = owner[0, p] * row_clusters + col[0, p]
            at = 2 * slot_of(j, inner) + (j & 1)
            done.append((row[0, p], dot(cells_ref[at].astype(bf16), blocks_ref[p], LAST)))
        for i, direct in done:
            out_ref[i] += direct

    near_loop(copies, pairs, body)


def finish_kernel(parts_ref, mine_ref, other_ref, basis_ref, out_ref):
    devices = parts_ref.shape[0]
    owned, rank, width = basis_ref.shape
    sides = out_ref.shape[0]

    def add(d, totals):
        return tuple(total + parts_ref[d, b] for b, total in enumerate(totals))

    first = tuple(parts_ref[0, b] for b in range(5))
    totals = lax.fori_loop(1, devices, add, first, unroll=min(15, devices - 1))
    me = lax.axis_index("col")
    mask = side_mask(sides, rank)
    for k in range(owned):
        near = jnp.concatenate([totals[2 * k], totals[2 * k + 1]], axis=0)
        near = near + (mine_ref[2 * me + k] + other_ref[2 * me + k])
        flat = jnp.concatenate([totals[4][2 * k : 2 * k + 1], totals[4][2 * k + 1 : 2 * k + 2]], axis=1)
        high, low = halves(jnp.where(mask, flat, 0.0))
        tiled = jnp.concatenate([basis_ref[k]] * sides, axis=0)
        far = dot(high, tiled, PLAIN) + dot(low, tiled, PLAIN)
        out_ref[:, k * width : (k + 1) * width] = near + far


def shards(cells, basis_t, near_blocks, near_owner, near_col, near_row, far_row, far_col, coupling):
    depth = lax.axis_size("z")
    inner = (depth, lax.axis_size("x") * lax.axis_size("col"))
    devices = depth * inner[1]
    sides, lanes = cells.shape
    owned, rank, width = basis_t.shape
    row_clusters = owned * lax.axis_size("col")
    pairs = near_blocks.shape[0]
    count = coupling.shape[0]
    swap = [(0, 1), (1, 0)]
    params = pltpu.CompilerParams(vmem_limit_bytes=24 * 1024 * 1024)

    def shaped(shape, dtype):
        return jax.ShapeDtypeStruct(shape, dtype)

    def exchange(blocks):
        return lax.all_to_all(blocks, GROUP, split_axis=0, concat_axis=0, tiled=True)

    near_cost = pl.CostEstimate(
        flops=2 * pairs * sides * width * width, bytes_accessed=10**7, transcendentals=0
    )
    payload = shaped((devices, 5, 4, 128), f32)
    packed, mine = pl.pallas_call(
        pack_kernel,
        out_shape=[payload, shaped(cells.shape, bf16)],
        in_specs=[HBM] * 2,
        out_specs=[HBM, VMEM],
        scratch_shapes=[
            pltpu.VMEM(cells.shape, bf16),
            pltpu.VMEM(basis_t.shape, bf16),
            pltpu.VMEM(payload.shape, f32),
            pltpu.SemaphoreType.DMA((2,)),
        ],
        compiler_params=params,
        name="pack",
    )(in_hbm(cells), in_hbm(basis_t))
    every = exchange(packed)
    other = lax.ppermute(mine, "col", swap)
    owner, column, line = [in_hbm(a.reshape(1, pairs)) for a in (near_owner, near_col, near_row)]
    first, second = [in_hbm(a.reshape(1, count)) for a in (far_row, far_col)]
    blocks = in_hbm(near_blocks)
    index_scratch = [pltpu.SMEM((1, pairs), jnp.int32)] * 3
    by_row, by_col, gather, spread, near = pl.pallas_call(
        lambda *refs: mirror_kernel(*refs, inner=inner),
        out_shape=[
            shaped((rank * rank, count), f32),
            shaped((rank * rank, count), f32),
            shaped((8 * devices, 4 * count), bf16),
            shaped((4 * devices, 4 * count), bf16),
            shaped((devices, 4, 4, 128), f32),
        ],
        in_specs=[HBM] * 7 + [VMEM] * 2,
        out_specs=[VMEM] * 5,
        scratch_shapes=index_scratch
        + [
            pltpu.VMEM((2, 1, count), jnp.int32),
            pltpu.VMEM(coupling.shape, bf16),
            pltpu.VMEM(near_blocks.shape, bf16),
            pltpu.VMEM((row_clusters, sides, width), f32),
            pltpu.VMEM((2 * devices, sides, width), f32),
            pltpu.SemaphoreType.DMA((6 + CHUNKS,)),
        ],
        compiler_params=params,
        cost_estimate=near_cost,
        name="mirror",
    )(owner, column, line, first, second, in_hbm(coupling), blocks, mine, other)
    partial = pl.pallas_call(
        far_kernel,
        out_shape=payload,
        in_specs=[VMEM] * 6,
        out_specs=HBM,
        scratch_shapes=[pltpu.VMEM((4 * devices, 128), f32)]
        + [pltpu.VMEM((sides * rank, count), f32)] * 4
        + [
            pltpu.VMEM((4 * devices, 128), f32),
            pltpu.VMEM((devices, 1, 4, 128), f32),
            pltpu.SemaphoreType.DMA((2,)),
        ],
        compiler_params=params,
        name="far",
    )(every, gather, spread, by_row, by_col, near)
    parts = exchange(partial)
    direct = pl.pallas_call(
        lambda *refs: direct_kernel(*refs, inner=inner),
        out_shape=shaped((row_clusters, sides, width), f32),
        in_specs=[HBM] * 4 + [VMEM],
        out_specs=VMEM,
        scratch_shapes=index_scratch
        + [
            pltpu.VMEM(near_blocks.shape, bf16),
            pltpu.VMEM((2 * devices, sides, width), f32),
            pltpu.SemaphoreType.DMA((3 + CHUNKS,)),
        ],
        compiler_params=params,
        cost_estimate=near_cost,
        name="direct",
    )(owner, column, line, blocks, every)
    others = lax.ppermute(direct, "col", swap)
    return pl.pallas_call(
        finish_kernel,
        out_shape=shaped((sides, lanes), f32),
        in_specs=[VMEM] * 4,
        out_specs=VMEM,
        compiler_params=params,
        name="finish",
    )(parts, direct, others, basis_t)


def solution(mesh):
    parts, rows, cols = mesh.devices.shape
    x = 2 if rows % 2 == 0 else 1
    mesh = Mesh(mesh.devices.reshape(parts, rows // x, x, cols), ("parts", "z", "x", "col"))
    split = ("parts", "z", "x", "col")
    return jax.shard_map(
        shards,
        mesh=mesh,
        in_specs=(
            P(None, split),
            P(split, None, None),
            P(split, None, None),
            P(split, None),
            P(split, None),
            P(split, None),
            P(split, None),
            P(split, None),
            P(split, None),
        ),
        out_specs=P(None, split),
        check_vma=False,
    )
```

time: 32.5 us -> 30.9 us (0.951)
  waiting for transfers between devices: 7.91 us -> 6.22 us
    all_to_all x2, waiting for transfers between devices: 6.21 us -> 4.56 us  [exchange(): lax.all_to_all(blocks, GROUP, split_axis=0, concat_axis=0, tiled=True)]
  transfers between devices with their start and end apart: 4 -> 4, of which waited for: 4 -> 4; matrix products, arithmetic and copies ran while one was open for 0% -> 0% of each run, Pallas kernels for 26% -> 27%
where the time goes in v3:
time: 30.9 us; the launch traced here: 30.4 us
  Pallas kernels  12.2 us (39%)
  starting transfers between devices  11.9 us (39%)
  waiting for transfers between devices  6.22 us (20%)
    all_to_all x2, starting transfers between devices, exchange(): lax.all_to_all(blocks, GROUP, split_axis=0, concat_axis=0, tiled=True)  11 us
    all_to_all x2, waiting for transfers between devices, exchange(): lax.all_to_all(blocks, GROUP, split_axis=0, concat_axis=0, tiled=True)  4.56 us
    pallas_call x1, Pallas kernels, shards(): pl.pallas_call(lambda *refs: direct_kernel(*refs, inner=inner), out_shape...  4.25 us
    pallas_call x1, Pallas kernels, shards(): pl.pallas_call(lambda *refs: mirror_kernel(*refs, inner=inner), out_shape...  3.84 us
    pallas_call x1, Pallas kernels, shards(): pl.pallas_call(far_kernel, out_shape=payload, in_specs=[VMEM] * 6, out_sp...  1.75 us
    pallas_call x1, Pallas kernels, shards(): pl.pallas_call(pack_kernel, out_shape=[payload, shaped(cells.shape, bf16)...  1.56 us
    ppermute x1, waiting for transfers between devices, shards(): others = lax.ppermute(direct, 'col', swap)  0.84 us
    ppermute x1, waiting for transfers between devices, shards(): other = lax.ppermute(mine, 'col', swap)  0.82 us
  transfers between devices with their start and end apart: 4, of which 4 were waited for; matrix products, arithmetic and copies ran while one was open for 0% of the time, Pallas kernels for 27%

profile of v3, /device:TPU:0, one launch (start us, length us, event | category | flops | bytes accessed | tf_op | source)
XLA Modules:
  0.0 30.4 jit_solution(16684197123674137249)
XLA Ops:
  0.0 1.6 %pack.1 = (f32[16,5,4,128]{3,2,1,0:T(4,128)}, bf16[8,256]{1,0:T(8,128)(2,1)S(1)}) custom-call(bf16[8,256]{1,0:T(8,128)(2,1)} %cells_hbm.1, bf16[2,32,128]{2,1,0:T(8,128)(2,1)} %basis_ref.1), custom_call_target="tpu_custom_call" | custom-call | tf_op jit(solution)/shard_map/pack/pallas_call | solution.py:303
  1.6 7.4 %all-to-all-start = ((f32[16,5,4,128]{3,2,1,0:T(4,128)}), f32[16,5,4,128]{3,2,1,0:T(4,128)S(1)}, u32[]{:S(2)}, u32[]{:S(2)}) async-start(f32[16,5,4,128]{3,2,1,0:T(4,128)} %get-tuple-element.12), calls=%async_computation | async-start | bytes 327680 | tf_op jit(solution)/shard_map/all_to_all | solution.py:297
  8.9 0.4 %collective-permute-start = (bf16[8,256]{1,0:T(8,128)(2,1)S(1)}, bf16[8,256]{1,0:T(8,128)(2,1)S(1)}, u32[]{:S(2)}, u32[]{:S(2)}) collective-permute-start(bf16[8,256]{1,0:T(8,128)(2,1)S(1)} %get-tuple-element.13.refs_7_), channel_id=1, source_target_pairs={{0,1},{1,0},{2,3},{3,2},{4,5},{5,4},{6,7},{7,6},{8,9},{9,8},{10,11... | collective-permute-start | bytes 12296 | tf_op jit(solution)/shard_map/ppermute | solution.py:318
  9.4 0.8 %collective-permute-done.refs_8_ = bf16[8,256]{1,0:T(8,128)(2,1)S(1)} collective-permute-done((bf16[8,256]{1,0:T(8,128)(2,1)S(1)}, bf16[8,256]{1,0:T(8,128)(2,1)S(1)}, u32[]{:S(2)}, u32[]{:S(2)}) %collective-permute-start) | collective-permute-done | bytes 4128 | tf_op jit(solution)/shard_map/ppermute | solution.py:318
  10.2 3.8 %mirror.1 = (f32[1024,128]{1,0:T(8,128)S(1)}, f32[1024,128]{1,0:T(8,128)S(1)}, bf16[128,512]{1,0:T(8,128)(2,1)S(1)}, bf16[64,512]{1,0:T(8,128)(2,1)S(1)}, f32[16,4,4,128]{3,2,1,0:T(4,128)S(1)}) custom-call(s32[1,96]{1,0:T(1,128)} %bitcast.5, s32[1,96]{1,0:T(1,128)} %bitcast.7, s32[1,96]{1,0:T(1,128)} %bitcast.9, s32[1,128]{1,0:T(1,128)} %bitcast.11, ...), custom_call_target="tpu_custom_call" | custom-call | flops 25165824 | bytes 10000000 | tf_op jit(solution)/shard_map/mirror/pallas_call | solution.py:323
  14.0 0.0 copy-start
  14.0 2.5 %all-to-all-done.every_ref.refs_4_ = f32[16,5,4,128]{3,2,1,0:T(4,128)S(1)} async-done(((f32[16,5,4,128]{3,2,1,0:T(4,128)}), f32[16,5,4,128]{3,2,1,0:T(4,128)S(1)}, u32[]{:S(2)}, u32[]{:S(2)}) %all-to-all-start) | async-done | bytes 163872 | tf_op jit(solution)/shard_map/all_to_all | solution.py:297
  16.6 1.8 %far.1 = f32[16,5,4,128]{3,2,1,0:T(4,128)} custom-call(f32[16,5,4,128]{3,2,1,0:T(4,128)S(1)} %all-to-all-done.every_ref.refs_4_, bf16[128,512]{1,0:T(8,128)(2,1)S(1)} %get-tuple-element.14.gather_ref, bf16[64,512]{1,0:T(8,128)(2,1)S(1)} %get-tuple-element.15.spread_ref, f32[1024,128]{1,0:T(8,128)S(1)} %get-tuple-element.16.by_row_ref, ...), custom_call_target="tpu_custom_call" | custom-call | tf_op jit(solution)/shard_map/far/pallas_call | solution.py:347
  18.3 3.7 %all-to-all-start.1 = ((f32[16,5,4,128]{3,2,1,0:T(4,128)}), f32[16,5,4,128]{3,2,1,0:T(4,128)S(1)}, u32[]{:S(2)}, u32[]{:S(2)}) async-start(f32[16,5,4,128]{3,2,1,0:T(4,128)} %far.1), calls=%async_computation.1 | async-start | bytes 327680 | tf_op jit(solution)/shard_map/all_to_all | solution.py:297
  22.0 4.2 %direct.1.mine_ref = f32[4,8,128]{2,1,0:T(8,128)S(1)} custom-call(s32[1,96]{1,0:T(1,128)} %bitcast.6, s32[1,96]{1,0:T(1,128)} %bitcast.8, s32[1,96]{1,0:T(1,128)} %bitcast.10, bf16[96,128,128]{2,1,0:T(8,128)(2,1)} %refs_3_.1, f32[16,5,4,128]{3,2,1,0:T(4,128)S(1)} %all-to-all-done.every_ref.refs_4_), custom_call_target="tpu_custom_call" | custom-call | flops 25165824 | bytes 10000000 | tf_op jit(solution)/shard_map/direct/pallas_call | solution.py:363
  26.3 0.5 %collective-permute-start.1 = (f32[4,8,128]{2,1,0:T(8,128)S(1)}, f32[4,8,128]{2,1,0:T(8,128)S(1)}, u32[]{:S(2)}, u32[]{:S(2)}) collective-permute-start(f32[4,8,128]{2,1,0:T(8,128)S(1)} %direct.1.mine_ref), channel_id=1, source_target_pairs={{0,1},{1,0},{2,3},{3,2},{4,5},{5,4},{6,7},{7,6},{8,9},{9,8},{10,11... | collective-permute-start | bytes 49160 | tf_op jit(solution)/shard_map/ppermute | solution.py:378
  26.7 0.8 %collective-permute-done.1.other_ref = f32[4,8,128]{2,1,0:T(8,128)S(1)} collective-permute-done((f32[4,8,128]{2,1,0:T(8,128)S(1)}, f32[4,8,128]{2,1,0:T(8,128)S(1)}, u32[]{:S(2)}, u32[]{:S(2)}) %collective-permute-start.1) | collective-permute-done | bytes 16416 | tf_op jit(solution)/shard_map/ppermute | solution.py:378
  27.6 2.0 %all-to-all-done.1.parts_ref = f32[16,5,4,128]{3,2,1,0:T(4,128)S(1)} async-done(((f32[16,5,4,128]{3,2,1,0:T(4,128)}), f32[16,5,4,128]{3,2,1,0:T(4,128)S(1)}, u32[]{:S(2)}, u32[]{:S(2)}) %all-to-all-start.1) | async-done | bytes 163872 | tf_op jit(solution)/shard_map/all_to_all | solution.py:297
  29.6 0.0 copy-done
  29.6 0.8 %finish.1 = f32[8,256]{1,0:T(8,128)} custom-call(f32[16,5,4,128]{3,2,1,0:T(4,128)S(1)} %all-to-all-done.1.parts_ref, f32[4,8,128]{2,1,0:T(8,128)S(1)} %direct.1.mine_ref, f32[4,8,128]{2,1,0:T(8,128)S(1)} %collective-permute-done.1.other_ref, bf16[2,32,128]{2,1,0:T(8,128)(2,1)S(1)} %copy-done), custom_call_target="tpu_custom_call" | custom-call | tf_op jit(solution)/shard_map/finish/pallas_call | solution.py:379
Async XLA Ops:
  1.6 15.0 %all-to-all-start = ((f32[16,5,4,128]{3,2,1,0:T(4,128)}), f32[16,5,4,128]{3,2,1,0:T(4,128)S(1)}, u32[]{:S(2)}, u32[]{:S(2)}) async-start(f32[16,5,4,128]{3,2,1,0:T(4,128)} %get-tuple-element.12), calls=%async_computation | async-start | bytes 327680 | tf_op jit(solution)/shard_map/all_to_all | solution.py:297
  8.9 1.2 %collective-permute-start = (bf16[8,256]{1,0:T(8,128)(2,1)S(1)}, bf16[8,256]{1,0:T(8,128)(2,1)S(1)}, u32[]{:S(2)}, u32[]{:S(2)}) collective-permute-start(bf16[8,256]{1,0:T(8,128)(2,1)S(1)} %get-tuple-element.13.refs_7_), channel_id=1, source_target_pairs={{0,1},{1,0},{2,3},{3,2},{4,5},{5,4},{6,7},{7,6},{8,9},{9,8},{10,11... | collective-permute-start | bytes 12296 | tf_op jit(solution)/shard_map/ppermute | solution.py:318
  14.0 15.6 %copy-start = (bf16[2,32,128]{2,1,0:T(8,128)(2,1)S(1)}, bf16[2,32,128]{2,1,0:T(8,128)(2,1)}, u32[]{:S(2)}) copy-start(bf16[2,32,128]{2,1,0:T(8,128)(2,1)} %basis_ref.1) | copy-start | bytes 49156
  18.3 11.3 %all-to-all-start.1 = ((f32[16,5,4,128]{3,2,1,0:T(4,128)}), f32[16,5,4,128]{3,2,1,0:T(4,128)S(1)}, u32[]{:S(2)}, u32[]{:S(2)}) async-start(f32[16,5,4,128]{3,2,1,0:T(4,128)} %far.1), calls=%async_computation.1 | async-start | bytes 327680 | tf_op jit(solution)/shard_map/all_to_all | solution.py:297
  26.3 1.3 %collective-permute-start.1 = (f32[4,8,128]{2,1,0:T(8,128)S(1)}, f32[4,8,128]{2,1,0:T(8,128)S(1)}, u32[]{:S(2)}, u32[]{:S(2)}) collective-permute-start(f32[4,8,128]{2,1,0:T(8,128)S(1)} %direct.1.mine_ref), channel_id=1, source_target_pairs={{0,1},{1,0},{2,3},{3,2},{4,5},{5,4},{6,7},{7,6},{8,9},{9,8},{10,11... | collective-permute-start | bytes 49160 | tf_op jit(solution)/shard_map/ppermute | solution.py:378

commit v4 on v3

--- a/solution.py
+++ b/solution.py
@@ -13,7 +13,7 @@
 HBM = pl.BlockSpec(memory_space=pltpu.HBM)
 VMEM = pl.BlockSpec(memory_space=pltpu.VMEM)
 CHUNKS = 4
-UNROLL = 8
+UNROLL = 24
 GROUP = ("x", "col", "z")
 
 
@@ -71,16 +71,17 @@
     for copy in copies:
         copy.wait()
     mine_ref[...] = cells_ref[...]
-    cells = cells_ref[...].astype(f32)
     blocks, lines = [], []
     for k in range(owned):
-        part = cells[:, k * width : (k + 1) * width]
-        blocks += [part[:4], part[4:]]
+        cells = cells_ref[:, k * width : (k + 1) * width]
+        blocks.append(cells)
         tiled = jnp.concatenate([basis_ref[k]] * sides, axis=0)
-        every = dot(cells_ref[:, k * width : (k + 1) * width], tiled, LAST)
+        every = dot(cells, tiled, LAST)
         flat = jnp.sum(jnp.where(mask, every, 0.0), axis=0, keepdims=True)
         lines += [flat[:, :128], flat[:, 128:]]
-    blocks.append(jnp.concatenate(lines, axis=0))
+    moments = jnp.concatenate(lines, axis=0)
+    high = moments.astype(bf16).astype(f32)
+    blocks.append(jnp.concatenate([high, moments - high], axis=0).astype(bf16))
 
     def store(d):
         for b, block in enumerate(blocks):
@@ -137,19 +138,19 @@
 
     for copy in small:
         copy.wait()
-    line = lax.broadcasted_iota(jnp.int32, (4 * devices, count), 0)
+    source = lax.broadcasted_iota(jnp.int32, (8 * devices, count), 0)
+    target = lax.broadcasted_iota(jnp.int32, (4 * devices, count), 0)
     for n in range(2):
         c = far[n]
-        at = 4 * slot_of(c, inner) + 2 * (c & 1)
-        low, high = line == at, line == at + 1
-        for h, match in enumerate((low, high)):
-            hot = one_hot(match)
-            column = (2 * n + h) * count
-            gather_ref[: 4 * devices, column : column + count] = hot
-            gather_ref[4 * devices :, column : column + count] = hot
-        hot = one_hot(low | high)
-        spread_ref[:, 2 * n * count : (2 * n + 1) * count] = hot
-        spread_ref[:, (2 * n + 1) * count : (2 * n + 2) * count] = hot
+        slot, k = slot_of(c, inner), c & 1
+        for h in range(2):
+            at = 8 * slot + 2 * k + h
+            hot = one_hot((source == at) | (source == at + 4))
+            gather_ref[:, (2 * n + h) * count : (2 * n + h + 1) * count] = hot
+        at = 4 * slot + 2 * k
+        hot = ((target == at) | (target == at + 1)).astype(f32).T.astype(bf16)
+        spread_ref[2 * n * count : (2 * n + 1) * count, :] = hot
+        spread_ref[(2 * n + 1) * count : (2 * n + 2) * count, :] = hot
 
     for t in range(0, size, 128):
         by_row_ref[t : t + 128, :] = coupling_ref[:, t : t + 128].astype(f32).T
@@ -177,7 +178,7 @@
 
 def far_kernel(
     every_ref, gather_ref, spread_ref, by_row_ref, by_col_ref, near_ref,
-    out_hbm, moment_ref, left_ref, right_ref, to_first_ref, to_second_ref, lines_ref, far_ref, sems,
+    out_hbm, left_ref, right_ref, lines_ref, far_ref, sems,
 ):
     near = start(near_ref, out_hbm.at[:, pl.ds(0, 4)], sems.at[0])
     devices = every_ref.shape[0]
@@ -185,33 +186,27 @@
     sides = 8
     rank = size // sides
 
-    def load(d):
-        moment_ref[pl.ds(4 * d, 4), :] = every_ref[d, 4]
-
-    each(devices, load)
-    moments = dot(jnp.concatenate(halves(moment_ref[...]), axis=0), gather_ref[...], FIRST)
+    lines = every_ref[:, 2].astype(f32).reshape(8 * devices, 128).astype(bf16)
+    moments = dot(lines, gather_ref[...], FIRST)
     for h in range(2):
         left_ref[h * 128 : (h + 1) * 128, :] = moments[:, h * count : (h + 1) * count]
         right_ref[h * 128 : (h + 1) * 128, :] = moments[:, (2 + h) * count : (3 + h) * count]
 
-    def couple(matrix_ref, moment_ref, result_ref):
-        def step(r, sums):
-            matrix = matrix_ref[pl.ds(pl.multiple_of(r * rank, rank), rank), :]
-            return tuple(
-                total + moment_ref[pl.ds(s * rank + r, 1), :] * matrix
-                for s, total in enumerate(sums)
-            )
-
-        sums = tuple(jnp.zeros((rank, count), f32) for _ in range(sides))
-        for s, total in enumerate(lax.fori_loop(0, rank, step, sums, unroll=4)):
-            result_ref[s * rank : (s + 1) * rank, :] = total
-
-    couple(by_col_ref, right_ref, to_first_ref)
-    couple(by_row_ref, left_ref, to_second_ref)
-    sums = jnp.concatenate(halves(to_first_ref[...]) + halves(to_second_ref[...]), axis=1)
-    spread = dot(spread_ref[...], sums, LAST)
-    odd = lax.broadcasted_iota(jnp.int32, (4 * devices, 128), 0) % 2 == 1
-    lines_ref[...] = jnp.where(odd, spread[:, 128:], spread[:, :128])
+    lines = []
+    for h in range(2):
+        total = 0.0
+        for n, (matrix_ref, source_ref) in enumerate(((by_col_ref, right_ref), (by_row_ref, left_ref))):
+            sums = [jnp.zeros((rank, count), f32) for _ in range(sides // 2)]
+            for r in range(rank):
+                matrix = matrix_ref[r * rank : (r + 1) * rank, :]
+                for s in range(sides // 2):
+                    at = h * 128 + s * rank + r
+                    sums[s] = sums[s] + source_ref[at : at + 1, :] * matrix
+            pair = jnp.concatenate(halves(jnp.concatenate(sums, axis=0)), axis=1)
+            total = total + dot(pair, spread_ref[2 * n * count : (2 * n + 2) * count, :], PLAIN)
+        lines.append(total)
+    odd = lax.broadcasted_iota(jnp.int32, (128, 4 * devices), 1) % 2 == 1
+    lines_ref[...] = jnp.where(odd, lines[1], lines[0]).T
 
     def store(d):
         far_ref[d, 0] = lines_ref[pl.ds(4 * d, 4), :]
@@ -224,7 +219,7 @@
 
 def direct_kernel(
     owner_hbm, col_hbm, row_hbm, blocks_hbm, every_ref,
-    out_ref, owner, col, row, blocks_ref, cells_ref, sems, *, inner,
+    out_ref, owner, col, row, blocks_ref, sems, *, inner,
 ):
     small = [
         start(owner_hbm, owner, sems.at[0]),
@@ -236,11 +231,6 @@
     row_clusters = out_ref.shape[0]
     out_ref[...] = jnp.zeros(out_ref.shape, f32)
 
-    def load(d):
-        for k in range(2):
-            cells_ref[2 * d + k] = jnp.concatenate([every_ref[d, 2 * k], every_ref[d, 2 * k + 1]], axis=0)
-
-    each(every_ref.shape[0], load)
     for copy in small:
         copy.wait()
 
@@ -248,8 +238,8 @@
         done = []
         for p in group:
             j = owner[0, p] * row_clusters + col[0, p]
-            at = 2 * slot_of(j, inner) + (j & 1)
-            done.append((row[0, p], dot(cells_ref[at].astype(bf16), blocks_ref[p], LAST)))
+            cells = every_ref[slot_of(j, inner), j & 1]
+            done.append((row[0, p], dot(cells, blocks_ref[p], LAST)))
         for i, direct in done:
             out_ref[i] += direct
 
@@ -299,7 +289,7 @@
     near_cost = pl.CostEstimate(
         flops=2 * pairs * sides * width * width, bytes_accessed=10**7, transcendentals=0
     )
-    payload = shaped((devices, 5, 4, 128), f32)
+    payload = shaped((devices, 3, sides, 128), bf16)
     packed, mine = pl.pallas_call(
         pack_kernel,
         out_shape=[payload, shaped(cells.shape, bf16)],
@@ -308,7 +298,7 @@
         scratch_shapes=[
             pltpu.VMEM(cells.shape, bf16),
             pltpu.VMEM(basis_t.shape, bf16),
-            pltpu.VMEM(payload.shape, f32),
+            pltpu.VMEM(payload.shape, bf16),
             pltpu.SemaphoreType.DMA((2,)),
         ],
         compiler_params=params,
@@ -326,7 +316,7 @@
             shaped((rank * rank, count), f32),
             shaped((rank * rank, count), f32),
             shaped((8 * devices, 4 * count), bf16),
-            shaped((4 * devices, 4 * count), bf16),
+            shaped((4 * count, 4 * devices), bf16),
             shaped((devices, 4, 4, 128), f32),
         ],
         in_specs=[HBM] * 7 + [VMEM] * 2,
@@ -346,11 +336,10 @@
     )(owner, column, line, first, second, in_hbm(coupling), blocks, mine, other)
     partial = pl.pallas_call(
         far_kernel,
-        out_shape=payload,
+        out_shape=shaped((devices, 5, 4, 128), f32),
         in_specs=[VMEM] * 6,
         out_specs=HBM,
-        scratch_shapes=[pltpu.VMEM((4 * devices, 128), f32)]
-        + [pltpu.VMEM((sides * rank, count), f32)] * 4
+        scratch_shapes=[pltpu.VMEM((sides * rank, count), f32)] * 2
         + [
             pltpu.VMEM((4 * devices, 128), f32),
             pltpu.VMEM((devices, 1, 4, 128), f32),
@@ -368,7 +357,6 @@
         scratch_shapes=index_scratch
         + [
             pltpu.VMEM(near_blocks.shape, bf16),
-            pltpu.VMEM((2 * devices, sides, width), f32),
             pltpu.SemaphoreType.DMA((3 + CHUNKS,)),
         ],
         compiler_params=params,

time: 30.9 us -> 29.9 us (0.968)
  Pallas kernels: 12.2 us -> 10.1 us
  waiting for transfers between devices: 6.22 us -> 7.59 us
    all_to_all x2, waiting for transfers between devices: 4.56 us -> 5.9 us  [exchange(): lax.all_to_all(blocks, GROUP, split_axis=0, concat_axis=0, tiled=True)]
    pallas_call x1, Pallas kernels: 3.84 us -> 2.85 us  [shards(): pl.pallas_call(lambda *refs: mirror_kernel(*refs, inner=inner), out_shape...]
    pallas_call x1, Pallas kernels: 4.25 us -> 3.31 us  [shards(): pl.pallas_call(lambda *refs: direct_kernel(*refs, inner=inner), out_shape...]
  transfers between devices with their start and end apart: 4 -> 4, of which waited for: 4 -> 4; matrix products, arithmetic and copies ran while one was open for 0% -> 0% of each run, Pallas kernels for 27% -> 21%
where the time goes in v4:
time: 29.9 us; the launch traced here: 29.5 us
  starting transfers between devices  11.7 us (39%)
  Pallas kernels  10.1 us (34%)
  waiting for transfers between devices  7.59 us (25%)
    all_to_all x2, starting transfers between devices, exchange(): lax.all_to_all(blocks, GROUP, split_axis=0, concat_axis=0, tiled=True)  10.9 us
    all_to_all x2, waiting for transfers between devices, exchange(): lax.all_to_all(blocks, GROUP, split_axis=0, concat_axis=0, tiled=True)  5.9 us
    pallas_call x1, Pallas kernels, shards(): pl.pallas_call(lambda *refs: direct_kernel(*refs, inner=inner), out_shape...  3.31 us
    pallas_call x1, Pallas kernels, shards(): pl.pallas_call(lambda *refs: mirror_kernel(*refs, inner=inner), out_shape...  2.85 us
    pallas_call x1, Pallas kernels, shards(): pl.pallas_call(far_kernel, out_shape=shaped((devices, 5, 4, 128), f32), i...  1.63 us
    pallas_call x1, Pallas kernels, shards(): pl.pallas_call(pack_kernel, out_shape=[payload, shaped(cells.shape, bf16)...  1.55 us
    ppermute x1, waiting for transfers between devices, shards(): others = lax.ppermute(direct, 'col', swap)  0.87 us
    ppermute x1, waiting for transfers between devices, shards(): other = lax.ppermute(mine, 'col', swap)  0.82 us
  transfers between devices with their start and end apart: 4, of which 4 were waited for; matrix products, arithmetic and copies ran while one was open for 0% of the time, Pallas kernels for 21%

profile of v4, /device:TPU:0, one launch (start us, length us, event | category | flops | bytes accessed | tf_op | source)
XLA Modules:
  0.0 29.5 jit_solution(12845747236124778737)
XLA Ops:
  0.0 1.5 %pack.1 = (bf16[16,3,8,128]{3,2,1,0:T(8,128)(2,1)}, bf16[8,256]{1,0:T(8,128)(2,1)S(1)}) custom-call(bf16[8,256]{1,0:T(8,128)(2,1)} %cells_hbm.1, bf16[2,32,128]{2,1,0:T(8,128)(2,1)} %basis_ref.1), custom_call_target="tpu_custom_call" | custom-call | tf_op jit(solution)/shard_map/pack/pallas_call | solution.py:293
  1.6 7.4 %all-to-all-start = ((bf16[16,3,8,128]{3,2,1,0:T(8,128)(2,1)}), bf16[16,3,8,128]{3,2,1,0:T(8,128)(2,1)S(1)}, u32[]{:S(2)}, u32[]{:S(2)}) async-start(bf16[16,3,8,128]{3,2,1,0:T(8,128)(2,1)} %get-tuple-element.12), calls=%async_computation | async-start | bytes 196608 | tf_op jit(solution)/shard_map/all_to_all | solution.py:287
  8.9 0.4 %collective-permute-start = (bf16[8,256]{1,0:T(8,128)(2,1)S(1)}, bf16[8,256]{1,0:T(8,128)(2,1)S(1)}, u32[]{:S(2)}, u32[]{:S(2)}) collective-permute-start(bf16[8,256]{1,0:T(8,128)(2,1)S(1)} %get-tuple-element.13.refs_7_), channel_id=1, source_target_pairs={{0,1},{1,0},{2,3},{3,2},{4,5},{5,4},{6,7},{7,6},{8,9},{9,8},{10,11... | collective-permute-start | bytes 12296 | tf_op jit(solution)/shard_map/ppermute | solution.py:308
  9.3 0.8 %collective-permute-done.refs_8_ = bf16[8,256]{1,0:T(8,128)(2,1)S(1)} collective-permute-done((bf16[8,256]{1,0:T(8,128)(2,1)S(1)}, bf16[8,256]{1,0:T(8,128)(2,1)S(1)}, u32[]{:S(2)}, u32[]{:S(2)}) %collective-permute-start) | collective-permute-done | bytes 4128 | tf_op jit(solution)/shard_map/ppermute | solution.py:308
  10.2 2.9 %mirror.1 = (f32[1024,128]{1,0:T(8,128)S(1)}, f32[1024,128]{1,0:T(8,128)S(1)}, bf16[128,512]{1,0:T(8,128)(2,1)S(1)}, bf16[512,64]{1,0:T(8,128)(2,1)S(1)}, f32[16,4,4,128]{3,2,1,0:T(4,128)S(1)}) custom-call(s32[1,96]{1,0:T(1,128)} %bitcast.5, s32[1,96]{1,0:T(1,128)} %bitcast.7, s32[1,96]{1,0:T(1,128)} %bitcast.9, s32[1,128]{1,0:T(1,128)} %bitcast.11, ...), custom_call_target="tpu_custom_call" | custom-call | flops 25165824 | bytes 10000000 | tf_op jit(solution)/shard_map/mirror/pallas_call | solution.py:313
  13.0 0.0 copy-start
  13.0 2.9 %all-to-all-done.every_ref.refs_4_ = bf16[16,3,8,128]{3,2,1,0:T(8,128)(2,1)S(1)} async-done(((bf16[16,3,8,128]{3,2,1,0:T(8,128)(2,1)}), bf16[16,3,8,128]{3,2,1,0:T(8,128)(2,1)S(1)}, u32[]{:S(2)}, u32[]{:S(2)}) %all-to-all-start) | async-done | bytes 98336 | tf_op jit(solution)/shard_map/all_to_all | solution.py:287
  15.9 1.6 %far.1 = f32[16,5,4,128]{3,2,1,0:T(4,128)} custom-call(bf16[16,3,8,128]{3,2,1,0:T(8,128)(2,1)S(1)} %all-to-all-done.every_ref.refs_4_, bf16[128,512]{1,0:T(8,128)(2,1)S(1)} %get-tuple-element.14.gather_ref, bf16[512,64]{1,0:T(8,128)(2,1)S(1)} %get-tuple-element.15.spread_ref, f32[1024,128]{1,0:T(8,128)S(1)} %get-tuple-element.16.by_row_ref, ...), custom_call_target="tpu_custom_call" | custom-call | tf_op jit(solution)/shard_map/far/pallas_call | solution.py:337
  17.6 3.5 %all-to-all-start.1 = ((f32[16,5,4,128]{3,2,1,0:T(4,128)}), f32[16,5,4,128]{3,2,1,0:T(4,128)S(1)}, u32[]{:S(2)}, u32[]{:S(2)}) async-start(f32[16,5,4,128]{3,2,1,0:T(4,128)} %far.1), calls=%async_computation.1 | async-start | bytes 327680 | tf_op jit(solution)/shard_map/all_to_all | solution.py:287
  21.1 3.3 %direct.1.mine_ref = f32[4,8,128]{2,1,0:T(8,128)S(1)} custom-call(s32[1,96]{1,0:T(1,128)} %bitcast.6, s32[1,96]{1,0:T(1,128)} %bitcast.8, s32[1,96]{1,0:T(1,128)} %bitcast.10, bf16[96,128,128]{2,1,0:T(8,128)(2,1)} %refs_3_.1, bf16[16,3,8,128]{3,2,1,0:T(8,128)(2,1)S(1)} %all-to-all-done.every_ref.refs_4_), custom_call_target="tpu_custom_call" | custom-call | flops 25165824 | bytes 10000000 | tf_op jit(solution)/shard_map/direct/pallas_call | solution.py:352
  24.4 0.4 %collective-permute-start.1 = (f32[4,8,128]{2,1,0:T(8,128)S(1)}, f32[4,8,128]{2,1,0:T(8,128)S(1)}, u32[]{:S(2)}, u32[]{:S(2)}) collective-permute-start(f32[4,8,128]{2,1,0:T(8,128)S(1)} %direct.1.mine_ref), channel_id=1, source_target_pairs={{0,1},{1,0},{2,3},{3,2},{4,5},{5,4},{6,7},{7,6},{8,9},{9,8},{10,11... | collective-permute-start | bytes 49160 | tf_op jit(solution)/shard_map/ppermute | solution.py:366
  24.8 0.9 %collective-permute-done.1.other_ref = f32[4,8,128]{2,1,0:T(8,128)S(1)} collective-permute-done((f32[4,8,128]{2,1,0:T(8,128)S(1)}, f32[4,8,128]{2,1,0:T(8,128)S(1)}, u32[]{:S(2)}, u32[]{:S(2)}) %collective-permute-start.1) | collective-permute-done | bytes 16416 | tf_op jit(solution)/shard_map/ppermute | solution.py:366
  25.7 3.0 %all-to-all-done.1.parts_ref = f32[16,5,4,128]{3,2,1,0:T(4,128)S(1)} async-done(((f32[16,5,4,128]{3,2,1,0:T(4,128)}), f32[16,5,4,128]{3,2,1,0:T(4,128)S(1)}, u32[]{:S(2)}, u32[]{:S(2)}) %all-to-all-start.1) | async-done | bytes 163872 | tf_op jit(solution)/shard_map/all_to_all | solution.py:287
  28.7 0.0 copy-done
  28.7 0.8 %finish.1 = f32[8,256]{1,0:T(8,128)} custom-call(f32[16,5,4,128]{3,2,1,0:T(4,128)S(1)} %all-to-all-done.1.parts_ref, f32[4,8,128]{2,1,0:T(8,128)S(1)} %direct.1.mine_ref, f32[4,8,128]{2,1,0:T(8,128)S(1)} %collective-permute-done.1.other_ref, bf16[2,32,128]{2,1,0:T(8,128)(2,1)S(1)} %copy-done), custom_call_target="tpu_custom_call" | custom-call | tf_op jit(solution)/shard_map/finish/pallas_call | solution.py:367
Async XLA Ops:
  1.6 14.4 %all-to-all-start = ((bf16[16,3,8,128]{3,2,1,0:T(8,128)(2,1)}), bf16[16,3,8,128]{3,2,1,0:T(8,128)(2,1)S(1)}, u32[]{:S(2)}, u32[]{:S(2)}) async-start(bf16[16,3,8,128]{3,2,1,0:T(8,128)(2,1)} %get-tuple-element.12), calls=%async_computation | async-start | bytes 196608 | tf_op jit(solution)/shard_map/all_to_all | solution.py:287
  8.9 1.2 %collective-permute-start = (bf16[8,256]{1,0:T(8,128)(2,1)S(1)}, bf16[8,256]{1,0:T(8,128)(2,1)S(1)}, u32[]{:S(2)}, u32[]{:S(2)}) collective-permute-start(bf16[8,256]{1,0:T(8,128)(2,1)S(1)} %get-tuple-element.13.refs_7_), channel_id=1, source_target_pairs={{0,1},{1,0},{2,3},{3,2},{4,5},{5,4},{6,7},{7,6},{8,9},{9,8},{10,11... | collective-permute-start | bytes 12296 | tf_op jit(solution)/shard_map/ppermute | solution.py:308
  13.0 15.7 %copy-start = (bf16[2,32,128]{2,1,0:T(8,128)(2,1)S(1)}, bf16[2,32,128]{2,1,0:T(8,128)(2,1)}, u32[]{:S(2)}) copy-start(bf16[2,32,128]{2,1,0:T(8,128)(2,1)} %basis_ref.1) | copy-start | bytes 49156
  17.6 11.1 %all-to-all-start.1 = ((f32[16,5,4,128]{3,2,1,0:T(4,128)}), f32[16,5,4,128]{3,2,1,0:T(4,128)S(1)}, u32[]{:S(2)}, u32[]{:S(2)}) async-start(f32[16,5,4,128]{3,2,1,0:T(4,128)} %far.1), calls=%async_computation.1 | async-start | bytes 327680 | tf_op jit(solution)/shard_map/all_to_all | solution.py:287
  24.4 1.2 %collective-permute-start.1 = (f32[4,8,128]{2,1,0:T(8,128)S(1)}, f32[4,8,128]{2,1,0:T(8,128)S(1)}, u32[]{:S(2)}, u32[]{:S(2)}) collective-permute-start(f32[4,8,128]{2,1,0:T(8,128)S(1)} %direct.1.mine_ref), channel_id=1, source_target_pairs={{0,1},{1,0},{2,3},{3,2},{4,5},{5,4},{6,7},{7,6},{8,9},{9,8},{10,11... | collective-permute-start | bytes 49160 | tf_op jit(solution)/shard_map/ppermute | solution.py:366

commit v5 on v4

v5 whole, which is shorter than its diff:
```python
import jax
import jax.numpy as jnp
from jax import lax
from jax.experimental import pallas as pl
from jax.experimental.pallas import tpu as pltpu
from jax.sharding import Mesh, PartitionSpec as P

f32 = jnp.float32
bf16 = jnp.bfloat16
LAST = (((1,), (1,)), ((), ()))
PLAIN = (((1,), (0,)), ((), ()))
FIRST = (((0,), (0,)), ((), ()))
HBM = pl.BlockSpec(memory_space=pltpu.HBM)
VMEM = pl.BlockSpec(memory_space=pltpu.VMEM)
CHUNKS = 4
UNROLL = 24
EARLY = 2
GROUP = ("x", "col", "z")


def dot(left, right, dims):
    return lax.dot_general(left, right, dims, preferred_element_type=f32)


def halves(value):
    high = value.astype(bf16)
    return high, (value - high.astype(f32)).astype(bf16)


def one_hot(match):
    return match.astype(f32).astype(bf16)


def side_mask(sides, rank):
    row = lax.broadcasted_iota(jnp.int32, (sides, sides * rank), 0)
    lane = lax.broadcasted_iota(jnp.int32, (sides, sides * rank), 1)
    return lane // rank == row


def start(source, target, sem):
    copy = pltpu.make_async_copy(source, target, sem)
    copy.start()
    return copy


def in_hbm(array):
    return pltpu.with_memory_space_constraint(array, pltpu.HBM)


def slot_of(cluster, inner):
    depth, width = inner
    device = cluster >> 1
    return lax.rem(device, 2 * width) * depth + lax.div(device, 2 * width)


def each(count, body):
    if count <= 16:
        for d in range(count):
            body(d)
    else:
        pl.loop(0, count)(body)


def pack_kernel(
    cells_hbm, basis_hbm, first_hbm, second_hbm, coupling_hbm, blocks_hbm,
    out_hbm, mine_ref, far_ref, coupling_ref, early_ref,
    cells_ref, basis_ref, out_ref, sems, *, inner,
):
    copies = [
        start(cells_hbm, cells_ref, sems.at[0]),
        start(basis_hbm, basis_ref, sems.at[1]),
    ]
    ahead = [
        start(first_hbm, far_ref.at[0], sems.at[2]),
        start(second_hbm, far_ref.at[1], sems.at[3]),
        start(coupling_hbm, coupling_ref, sems.at[4]),
        start(blocks_hbm.at[pl.ds(0, early_ref.shape[0])], early_ref, sems.at[5]),
    ]
    sides = cells_ref.shape[0]
    owned, rank, width = basis_ref.shape
    mask = side_mask(sides, rank)
    for copy in copies:
        copy.wait()
    mine_ref[...] = cells_ref[...]
    blocks, lines = [], []
    for k in range(owned):
        cells = cells_ref[:, k * width : (k + 1) * width]
        blocks.append(cells.astype(f32))
        tiled = jnp.concatenate([basis_ref[k]] * sides, axis=0)
        every = dot(cells, tiled, LAST)
        flat = jnp.sum(jnp.where(mask, every, 0.0), axis=0, keepdims=True)
        lines += [flat[:, :128], flat[:, 128:]]
    moments = jnp.concatenate(lines, axis=0)
    high = moments.astype(bf16).astype(f32)
    moments = jnp.concatenate([high, moments - high], axis=0).astype(bf16)
    for c in range(2):
        half = jnp.concatenate([block[4 * c : 4 * c + 4] for block in blocks], axis=0).astype(bf16)
        for x in range(inner[1]):

            def store(z, c=c, x=x, half=half):
                d = (2 * x + c) * inner[0] + z
                out_ref[d, 0] = half
                out_ref[d, 1] = moments

            each(inner[0], store)
    start(out_ref, out_hbm, sems.at[0]).wait()
    for copy in ahead:
        copy.wait()


def near_copies(blocks_hbm, blocks_ref, sems, first, chunks):
    size = blocks_hbm.shape[0] // CHUNKS
    skipped = CHUNKS - chunks
    return [
        start(
            blocks_hbm.at[pl.ds((skipped + c) * size, size)],
            blocks_ref.at[pl.ds(c * size, size)],
            sems.at[first + c],
        )
        for c in range(chunks)
    ]


def near_loop(first, size, body):
    def group(g, _):
        body([first + g * UNROLL + u for u in range(UNROLL)])
        return 0

    lax.fori_loop(0, size // UNROLL, group, 0)


def mirror_kernel(
    owner_hbm, col_hbm, row_hbm, blocks_hbm, far, coupling_ref, early_ref, mine_ref, other_ref,
    by_row_ref, by_col_ref, gather_ref, spread_ref, keep_ref, give_ref,
    owner, col, row, blocks_ref, cells_ref, sums_ref, sems, *, inner,
):
    small = [
        start(owner_hbm, owner, sems.at[0]),
        start(col_hbm, col, sems.at[1]),
        start(row_hbm, row, sems.at[2]),
    ]
    copies = near_copies(blocks_hbm, blocks_ref, sems, 3, CHUNKS - EARLY)
    count, size = coupling_ref.shape
    rank = round(size**0.5)
    devices = keep_ref.shape[0]
    early, width, _ = early_ref.shape
    chunk = early // EARLY
    row_clusters = cells_ref.shape[0]
    me = lax.axis_index("col")
    for k in range(2):
        cells_ref[2 * me + k] = mine_ref[:, k * width : (k + 1) * width].astype(f32)
        cells_ref[2 - 2 * me + k] = other_ref[:, k * width : (k + 1) * width].astype(f32)
    sums_ref[...] = jnp.zeros(sums_ref.shape, f32)

    source = lax.broadcasted_iota(jnp.int32, (8 * devices, count), 0)
    target = lax.broadcasted_iota(jnp.int32, (4 * devices, count), 0)
    for n in range(2):
        c = far[n]
        slot, k = slot_of(c, inner), c & 1
        for h in range(2):
            at = 8 * slot + 2 * k + h
            hot = one_hot((source == at) | (source == at + 4))
            gather_ref[:, (2 * n + h) * count : (2 * n + h + 1) * count] = hot
        at = 4 * slot + 2 * k
        hot = ((target == at) | (target == at + 1)).astype(f32).T.astype(bf16)
        spread_ref[2 * n * count : (2 * n + 1) * count, :] = hot
        spread_ref[(2 * n + 1) * count : (2 * n + 2) * count, :] = hot

    for t in range(0, size, 128):
        by_row_ref[t : t + 128, :] = coupling_ref[:, t : t + 128].astype(f32).T
    for k in range(rank):
        by_col_ref[k * rank : (k + 1) * rank, :] = by_row_ref[pl.ds(k, rank, stride=rank), :]

    def multiply(source_ref, first):
        def body(group):
            done = []
            for p in group:
                j = owner[0, p] * row_clusters + col[0, p]
                at = 2 * slot_of(j, inner) + (j & 1)
                done.append((at, dot(cells_ref[row[0, p]].astype(bf16), source_ref[p - first], PLAIN)))
            for at, mirrored in done:
                sums_ref[at] += mirrored

        return body

    for copy in small:
        copy.wait()
    near_loop(0, early, multiply(early_ref, 0))
    for c, copy in enumerate(copies):
        copy.wait()
        near_loop(early + c * chunk, chunk, multiply(blocks_ref, early))

    def store(d):
        for k in range(2):
            keep_ref[d, k] = sums_ref[2 * d + k, pl.ds(4 * me, 4), :]
            give_ref[d, k] = sums_ref[2 * d + k, pl.ds(4 - 4 * me, 4), :]

    each(devices, store)


def far_kernel(
    every_ref, gather_ref, spread_ref, by_row_ref, by_col_ref, keep_ref, got_ref,
    out_hbm, near_ref, left_ref, right_ref, lines_ref, far_ref, sems,
):
    near_ref[...] = keep_ref[...] + got_ref[...]
    near = start(near_ref, out_hbm.at[:, pl.ds(0, 2)], sems.at[0])
    devices = every_ref.shape[0]
    size, count = left_ref.shape
    sides = 8
    rank = size // sides

    lines = every_ref[:, 1].astype(f32).reshape(8 * devices, 128).astype(bf16)
    moments = dot(lines, gather_ref[...], FIRST)
    for h in range(2):
        left_ref[h * 128 : (h + 1) * 128, :] = moments[:, h * count : (h + 1) * count]
        right_ref[h * 128 : (h + 1) * 128, :] = moments[:, (2 + h) * count : (3 + h) * count]

    lines = []
    for h in range(2):
        total = 0.0
        for n, (matrix_ref, source_ref) in enumerate(((by_col_ref, right_ref), (by_row_ref, left_ref))):
            sums = [jnp.zeros((rank, count), f32) for _ in range(sides // 2)]
            for r in range(rank):
                matrix = matrix_ref[r * rank : (r + 1) * rank, :]
                for s in range(sides // 2):
                    at = h * 128 + s * rank + r
                    sums[s] = sums[s] + source_ref[at : at + 1, :] * matrix
            pair = jnp.concatenate(halves(jnp.concatenate(sums, axis=0)), axis=1)
            total = total + dot(pair, spread_ref[2 * n * count : (2 * n + 2) * count, :], PLAIN)
        lines.append(total)
    odd = lax.broadcasted_iota(jnp.int32, (128, 4 * devices), 1) % 2 == 1
    lines_ref[...] = jnp.where(odd, lines[1], lines[0]).T

    def store(d):
        far_ref[d, 0] = lines_ref[pl.ds(4 * d, 4), :]

    each(devices, store)
    far = start(far_ref, out_hbm.at[:, pl.ds(2, 1)], sems.at[1])
    near.wait()
    far.wait()


def direct_kernel(
    owner_hbm, col_hbm, row_hbm, blocks_hbm, every_ref, others_ref,
    out_ref, owner, col, row, blocks_ref, cells_ref, sems, *, inner,
):
    small = [
        start(owner_hbm, owner, sems.at[0]),
        start(col_hbm, col, sems.at[1]),
        start(row_hbm, row, sems.at[2]),
    ]
    copies = near_copies(blocks_hbm, blocks_ref, sems, 3, CHUNKS)
    chunk = blocks_ref.shape[0] // CHUNKS
    row_clusters = out_ref.shape[0]
    out_ref[...] = jnp.zeros(out_ref.shape, f32)
    me = lax.axis_index("col")

    def load(d):
        mine, other = every_ref[d, 0].astype(f32), others_ref[d, 0].astype(f32)
        first, second = jnp.where(me == 0, mine, other), jnp.where(me == 0, other, mine)
        for k in range(2):
            cells_ref[d, k] = jnp.concatenate([first[4 * k : 4 * k + 4], second[4 * k : 4 * k + 4]], axis=0)

    each(every_ref.shape[0], load)
    for copy in small:
        copy.wait()

    def body(group):
        done = []
        for p in group:
            j = owner[0, p] * row_clusters + col[0, p]
            cells = cells_ref[slot_of(j, inner), j & 1].astype(bf16)
            done.append((row[0, p], dot(cells, blocks_ref[p], LAST)))
        for i, direct in done:
            out_ref[i] += direct

    for c, copy in enumerate(copies):
        copy.wait()
        near_loop(c * chunk, chunk, body)


def finish_kernel(parts_ref, mine_ref, other_ref, basis_ref, out_ref, *, inner):
    owned, rank, width = basis_ref.shape
    sides = out_ref.shape[0]
    depth = inner[0]
    near, far = [], jnp.zeros((4, 128), f32)
    for c in range(2):
        totals = (jnp.zeros((4, 128), f32), jnp.zeros((4, 128), f32), far)
        for x in range(inner[1]):

            def add(z, totals, first=(2 * x + c) * depth):
                return tuple(total + parts_ref[first + z, b] for b, total in enumerate(totals))

            totals = lax.fori_loop(0, depth, add, totals, unroll=min(8, depth))
        near.append(totals[:2])
        far = totals[2]
    me = lax.axis_index("col")
    mask = side_mask(sides, rank)
    for k in range(owned):
        total = jnp.concatenate([near[0][k], near[1][k]], axis=0)
        total = total + (mine_ref[2 * me + k] + other_ref[2 * me + k])
        flat = jnp.concatenate([far[2 * k : 2 * k + 1], far[2 * k + 1 : 2 * k + 2]], axis=1)
        high, low = halves(jnp.where(mask, flat, 0.0))
        tiled = jnp.concatenate([basis_ref[k]] * sides, axis=0)
        total = total + (dot(high, tiled, PLAIN) + dot(low, tiled, PLAIN))
        out_ref[:, k * width : (k + 1) * width] = total


def shards(cells, basis_t, near_blocks, near_owner, near_col, near_row, far_row, far_col, coupling):
    depth = lax.axis_size("z")
    inner = (depth, lax.axis_size("x"))
    devices = 2 * depth * inner[1]
    sides, lanes = cells.shape
    owned, rank, width = basis_t.shape
    row_clusters = owned * lax.axis_size("col")
    pairs = near_blocks.shape[0]
    count = coupling.shape[0]
    swap = [(0, 1), (1, 0)]
    params = pltpu.CompilerParams(vmem_limit_bytes=24 * 1024 * 1024)

    def shaped(shape, dtype):
        return jax.ShapeDtypeStruct(shape, dtype)

    def exchange(blocks):
        return lax.all_to_all(blocks, GROUP, split_axis=0, concat_axis=0, tiled=True)

    near_cost = pl.CostEstimate(
        flops=2 * pairs * sides * width * width, bytes_accessed=10**7, transcendentals=0
    )
    payload = shaped((devices, 2, sides, 128), bf16)
    owner, column, line = [in_hbm(a.reshape(1, pairs)) for a in (near_owner, near_col, near_row)]
    first, second = [in_hbm(a.reshape(1, count)) for a in (far_row, far_col)]
    blocks = in_hbm(near_blocks)
    early = EARLY * (pairs // CHUNKS)
    packed, mine, far, couplings, early_blocks = pl.pallas_call(
        lambda *refs: pack_kernel(*refs, inner=inner),
        out_shape=[
            payload,
            shaped(cells.shape, bf16),
            shaped((2, 1, count), jnp.int32),
            shaped(coupling.shape, bf16),
            shaped((early,) + near_blocks.shape[1:], bf16),
        ],
        in_specs=[HBM] * 6,
        out_specs=[HBM] + [VMEM] * 4,
        scratch_shapes=[
            pltpu.VMEM(cells.shape, bf16),
            pltpu.VMEM(basis_t.shape, bf16),
            pltpu.VMEM(payload.shape, bf16),
            pltpu.SemaphoreType.DMA((6,)),
        ],
        compiler_params=params,
        name="pack",
    )(in_hbm(cells), in_hbm(basis_t), first, second, in_hbm(coupling), blocks)
    every = exchange(packed)
    other = lax.ppermute(mine, "col", swap)
    index_scratch = [pltpu.SMEM((1, pairs), jnp.int32)] * 3
    by_row, by_col, gather, spread, keep, give = pl.pallas_call(
        lambda *refs: mirror_kernel(*refs, inner=inner),
        out_shape=[
            shaped((rank * rank, count), f32),
            shaped((rank * rank, count), f32),
            shaped((8 * devices, 4 * count), bf16),
            shaped((4 * count, 4 * devices), bf16),
            shaped((devices, 2, 4, 128), f32),
            shaped((devices, 2, 4, 128), f32),
        ],
        in_specs=[HBM] * 4 + [VMEM] * 5,
        out_specs=[VMEM] * 6,
        scratch_shapes=index_scratch
        + [
            pltpu.VMEM((pairs - early,) + near_blocks.shape[1:], bf16),
            pltpu.VMEM((row_clusters, sides, width), f32),
            pltpu.VMEM((2 * devices, sides, width), f32),
            pltpu.SemaphoreType.DMA((3 + CHUNKS,)),
        ],
        compiler_params=params,
        cost_estimate=near_cost,
        name="mirror",
    )(owner, column, line, blocks, far, couplings, early_blocks, mine, other)
    got = lax.ppermute(give, "col", swap)
    partial = pl.pallas_call(
        far_kernel,
        out_shape=shaped((devices, 3, 4, 128), f32),
        in_specs=[VMEM] * 7,
        out_specs=HBM,
        scratch_shapes=[pltpu.VMEM(keep.shape, f32)]
        + [pltpu.VMEM((sides * rank, count), f32)] * 2
        + [
            pltpu.VMEM((4 * devices, 128), f32),
            pltpu.VMEM((devices, 1, 4, 128), f32),
            pltpu.SemaphoreType.DMA((2,)),
        ],
        compiler_params=params,
        name="far",
    )(every, gather, spread, by_row, by_col, keep, got)
    parts = exchange(partial)
    every_other = lax.ppermute(every, "col", swap)
    direct = pl.pallas_call(
        lambda *refs: direct_kernel(*refs, inner=inner),
        out_shape=shaped((row_clusters, sides, width), f32),
        in_specs=[HBM] * 4 + [VMEM] * 2,
        out_specs=VMEM,
        scratch_shapes=index_scratch
        + [
            pltpu.VMEM(near_blocks.shape, bf16),
            pltpu.VMEM(payload.shape, f32),
            pltpu.SemaphoreType.DMA((3 + CHUNKS,)),
        ],
        compiler_params=params,
        cost_estimate=near_cost,
        name="direct",
    )(owner, column, line, blocks, every, every_other)
    others = lax.ppermute(direct, "col", swap)
    return pl.pallas_call(
        lambda *refs: finish_kernel(*refs, inner=inner),
        out_shape=shaped((sides, lanes), f32),
        in_specs=[VMEM] * 4,
        out_specs=VMEM,
        compiler_params=params,
        name="finish",
    )(parts, direct, others, basis_t)


def solution(mesh):
    parts, rows, cols = mesh.devices.shape
    x = 2 if rows % 2 == 0 else 1
    mesh = Mesh(mesh.devices.reshape(parts, rows // x, x, cols), ("parts", "z", "x", "col"))
    split = ("parts", "z", "x", "col")
    return jax.shard_map(
        shards,
        mesh=mesh,
        in_specs=(
            P(None, split),
            P(split, None, None),
            P(split, None, None),
            P(split, None),
            P(split, None),
            P(split, None),
            P(split, None),
            P(split, None),
            P(split, None),
        ),
        out_specs=P(None, split),
        check_vma=False,
    )
```

time: 29.9 us -> 29.4 us (0.983)
  starting transfers between devices: 11.7 us -> 13 us
  waiting for transfers between devices: 7.59 us -> 6.53 us
  Pallas kernels: 10.1 us -> 9.45 us
    all_to_all x2, waiting for transfers between devices: 5.9 us -> 3.05 us  [exchange(): lax.all_to_all(blocks, GROUP, split_axis=0, concat_axis=0, tiled=True)]
    ppermute x0 -> x2, waiting for transfers between devices: none -> 1.82 us  [the longest x1 0.91 us: shards(): got = lax.ppermute(give, 'col', swap)]
    ppermute x0 -> x2, starting transfers between devices: none -> 0.82 us  [the longest x1 0.41 us: shards(): every_other = lax.ppermute(every, 'col', swap)]
    pallas_call x1, Pallas kernels: 2.85 us -> 2.13 us  [shards(): pl.pallas_call(lambda *refs: mirror_kernel(*refs, inner=inner), out_shape...]
    all_to_all x2, starting transfers between devices: 10.9 us -> 11.4 us  [exchange(): lax.all_to_all(blocks, GROUP, split_axis=0, concat_axis=0, tiled=True)]
  transfers between devices with their start and end apart: 4 -> 6, of which waited for: 4 -> 6; matrix products, arithmetic and copies ran while one was open for 0% -> 0% of each run, Pallas kernels for 21% -> 19%
where the time goes in v5:
time: 29.4 us; the launch traced here: 29.1 us
  starting transfers between devices  13 us (44%)
  Pallas kernels  9.45 us (32%)
  waiting for transfers between devices  6.53 us (22%)
    all_to_all x2, starting transfers between devices, exchange(): lax.all_to_all(blocks, GROUP, split_axis=0, concat_axis=0, tiled=True)  11.4 us
    pallas_call x1, Pallas kernels, shards(): pl.pallas_call(lambda *refs: direct_kernel(*refs, inner=inner), out_shape...  3.31 us
    all_to_all x2, waiting for transfers between devices, exchange(): lax.all_to_all(blocks, GROUP, split_axis=0, concat_axis=0, tiled=True)  3.05 us
    pallas_call x1, Pallas kernels, shards(): pl.pallas_call(lambda *refs: mirror_kernel(*refs, inner=inner), out_shape...  2.13 us
    pallas_call x1, Pallas kernels, shards(): pl.pallas_call(far_kernel, out_shape=shaped((devices, 3, 4, 128), f32), i...  1.66 us
    pallas_call x1, Pallas kernels, shards(): pl.pallas_call(lambda *refs: pack_kernel(*refs, inner=inner), out_shape=[...  1.6 us
    ppermute x1, waiting for transfers between devices, shards(): got = lax.ppermute(give, 'col', swap)  0.91 us
    ppermute x1, waiting for transfers between devices, shards(): every_other = lax.ppermute(every, 'col', swap)  0.91 us
  transfers between devices with their start and end apart: 6, of which 6 were waited for; matrix products, arithmetic and copies ran while one was open for 0% of the time, Pallas kernels for 19%

profile of v5, /device:TPU:0, one launch (start us, length us, event | category | flops | bytes accessed | tf_op | source)
XLA Modules:
  0.0 29.1 jit_solution(126244492099243024)
XLA Ops:
  0.0 1.6 %pack.1 = (bf16[16,2,8,128]{3,2,1,0:T(8,128)(2,1)}, bf16[8,256]{1,0:T(8,128)(2,1)S(1)}, s32[2,1,128]{2,1,0:T(1,128)S(1)}, bf16[128,1024]{1,0:T(8,128)(2,1)S(1)}, bf16[48,128,128]{2,1,0:T(8,128)(2,1)S(1)}) custom-call(bf16[8,256]{1,0:T(8,128)(2,1)} %refs_0_.1, bf16[2,32,128]{2,1,0:T(8,128)(2,1)} %refs_3_.5, s32[1,128]{1,0:T(1,128)} %bitcast.11, ...), custom_call_target="tpu_custom_call" | custom-call | tf_op jit(solution)/shard_map/pack/pallas_call | solution.py:335
  1.6 7.4 %all-to-all-start = ((bf16[16,2,8,128]{3,2,1,0:T(8,128)(2,1)}), bf16[16,2,8,128]{3,2,1,0:T(8,128)(2,1)S(1)}, u32[]{:S(2)}, u32[]{:S(2)}) async-start(bf16[16,2,8,128]{3,2,1,0:T(8,128)(2,1)} %get-tuple-element.16), calls=%async_computation | async-start | bytes 131072 | tf_op jit(solution)/shard_map/all_to_all | solution.py:325
  9.0 0.4 %collective-permute-start = (bf16[8,256]{1,0:T(8,128)(2,1)S(1)}, bf16[8,256]{1,0:T(8,128)(2,1)S(1)}, u32[]{:S(2)}, u32[]{:S(2)}) collective-permute-start(bf16[8,256]{1,0:T(8,128)(2,1)S(1)} %get-tuple-element.20.refs_7_), channel_id=1, source_target_pairs={{0,1},{1,0},{2,3},{3,2},{4,5},{5,4},{6,7},{7,6},{8,9},{9,8},{10,11... | collective-permute-start | bytes 12296 | tf_op jit(solution)/shard_map/ppermute | solution.py:356
  9.4 0.8 %collective-permute-done.refs_8_ = bf16[8,256]{1,0:T(8,128)(2,1)S(1)} collective-permute-done((bf16[8,256]{1,0:T(8,128)(2,1)S(1)}, bf16[8,256]{1,0:T(8,128)(2,1)S(1)}, u32[]{:S(2)}, u32[]{:S(2)}) %collective-permute-start) | collective-permute-done | bytes 4128 | tf_op jit(solution)/shard_map/ppermute | solution.py:356
  10.2 2.1 %mirror.1 = (f32[1024,128]{1,0:T(8,128)S(1)}, f32[1024,128]{1,0:T(8,128)S(1)}, bf16[128,512]{1,0:T(8,128)(2,1)S(1)}, bf16[512,64]{1,0:T(8,128)(2,1)S(1)}, f32[16...) custom-call(s32[1,96]{1,0:T(1,128)} %bitcast.5, s32[1,96]{1,0:T(1,128)} %bitcast.7, s32[1,96]{1,0:T(1,128)} %bitcast.9, ...), custom_call_target="tpu_custom_call" | custom-call | flops 25165824 | bytes 10000000 | tf_op jit(solution)/shard_map/mirror/pallas_call | solution.py:358
  12.4 0.0 copy-start
  12.4 0.4 %collective-permute-start.1 = (f32[16,2,4,128]{3,2,1,0:T(4,128)S(1)}, f32[16,2,4,128]{3,2,1,0:T(4,128)S(1)}, u32[]{:S(2)}, u32[]{:S(2)}) collective-permute-start(f32[16,2,4,128]{3,2,1,0:T(4,128)S(1)} %get-tuple-element.26), channel_id=1, source_target_pairs={{0,1},{1,0},{2,3},{3,2},{4,5},{5,4},{6,7},{7,6},{8,9},{9,8},{10,11... | collective-permute-start | bytes 196616 | tf_op jit(solution)/shard_map/ppermute | solution.py:381
  12.8 0.9 %collective-permute-done.1.got_ref = f32[16,2,4,128]{3,2,1,0:T(4,128)S(1)} collective-permute-done((f32[16,2,4,128]{3,2,1,0:T(4,128)S(1)}, f32[16,2,4,128]{3,2,1,0:T(4,128)S(1)}, u32[]{:S(2)}, u32[]{:S(2)}) %collective-permute-start.1) | collective-permute-done | bytes 65568 | tf_op jit(solution)/shard_map/ppermute | solution.py:381
  13.7 1.9 %all-to-all-done.every_ref.refs_4_ = bf16[16,2,8,128]{3,2,1,0:T(8,128)(2,1)S(1)} async-done(((bf16[16,2,8,128]{3,2,1,0:T(8,128)(2,1)}), bf16[16,2,8,128]{3,2,1,0:T(8,128)(2,1)S(1)}, u32[]{:S(2)}, u32[]{:S(2)}) %all-to-all-start) | async-done | bytes 65568 | tf_op jit(solution)/shard_map/all_to_all | solution.py:325
  15.6 1.7 %far.1 = f32[16,3,4,128]{3,2,1,0:T(4,128)} custom-call(bf16[16,2,8,128]{3,2,1,0:T(8,128)(2,1)S(1)} %all-to-all-done.every_ref.refs_4_, bf16[128,512]{1,0:T(8,128)(2,1)S(1)} %get-tuple-element.21.gather_ref, bf16[512,64]{1,0:T(8,128)(2,1)S(1)} %get-tuple-element.22.spread_ref, f32[1024,128]{1,0:T(8,128)S(1)} %get-tuple-element.23.by_row_ref, ...), custom_call_target="tpu_custom_call" | custom-call | tf_op jit(solution)/shard_map/far/pallas_call | solution.py:382
  17.3 4.0 %all-to-all-start.1 = ((f32[16,3,4,128]{3,2,1,0:T(4,128)}), f32[16,3,4,128]{3,2,1,0:T(4,128)S(1)}, u32[]{:S(2)}, u32[]{:S(2)}) async-start(f32[16,3,4,128]{3,2,1,0:T(4,128)} %far.1), calls=%async_computation.1 | async-start | bytes 196608 | tf_op jit(solution)/shard_map/all_to_all | solution.py:325
  21.3 0.4 %collective-permute-start.2 = (bf16[16,2,8,128]{3,2,1,0:T(8,128)(2,1)S(1)}, bf16[16,2,8,128]{3,2,1,0:T(8,128)(2,1)S(1)}, u32[]{:S(2)}, u32[]{:S(2)}) collective-permute-start(bf16[16,2,8,128]{3,2,1,0:T(8,128)(2,1)S(1)} %all-to-all-done.every_ref.refs_4_), channel_id=1, source_target_pairs={{0,1},{1,0},{2,3},{3,2},{4,5},{5,4},{6,7},{7,6},{8,9},{9,8},{10,11... | collective-permute-start | bytes 196616 | tf_op jit(solution)/shard_map/ppermute | solution.py:398
  21.7 0.9 %collective-permute-done.2.refs_5_ = bf16[16,2,8,128]{3,2,1,0:T(8,128)(2,1)S(1)} collective-permute-done((bf16[16,2,8,128]{3,2,1,0:T(8,128)(2,1)S(1)}, bf16[16,2,8,128]{3,2,1,0:T(8,128)(2,1)S(1)}, u32[]{:S(2)}, u32[]{:S(2)}) %collective-permute-start.2) | collective-permute-done | bytes 65568 | tf_op jit(solution)/shard_map/ppermute | solution.py:398
  22.6 3.3 %direct.1.refs_1_ = f32[4,8,128]{2,1,0:T(8,128)S(1)} custom-call(s32[1,96]{1,0:T(1,128)} %bitcast.6, s32[1,96]{1,0:T(1,128)} %bitcast.8, s32[1,96]{1,0:T(1,128)} %bitcast.10, bf16[96,128,128]{2,1,0:T(8,128)(2,1)} %refs_3_.4, bf16[16,2,8,128]{3,2,1,0:T(8,128)(2,1)S(1)} %all-to-all-done.every_ref.refs_4_, ...), custom_call_target="tpu_custom_call" | custom-call | flops 25165824 | bytes 10000000 | tf_op jit(solution)/shard_map/direct/pallas_call | solution.py:399
  26.0 0.4 %collective-permute-start.3 = (f32[4,8,128]{2,1,0:T(8,128)S(1)}, f32[4,8,128]{2,1,0:T(8,128)S(1)}, u32[]{:S(2)}, u32[]{:S(2)}) collective-permute-start(f32[4,8,128]{2,1,0:T(8,128)S(1)} %direct.1.refs_1_), channel_id=1, source_target_pairs={{0,1},{1,0},{2,3},{3,2},{4,5},{5,4},{6,7},{7,6},{8,9},{9,8},{10,11... | collective-permute-start | bytes 49160 | tf_op jit(solution)/shard_map/ppermute | solution.py:414
  26.4 0.8 %collective-permute-done.3.refs_2_ = f32[4,8,128]{2,1,0:T(8,128)S(1)} collective-permute-done((f32[4,8,128]{2,1,0:T(8,128)S(1)}, f32[4,8,128]{2,1,0:T(8,128)S(1)}, u32[]{:S(2)}, u32[]{:S(2)}) %collective-permute-start.3) | collective-permute-done | bytes 16416 | tf_op jit(solution)/shard_map/ppermute | solution.py:414
  27.2 1.1 %all-to-all-done.1.refs_0_ = f32[16,3,4,128]{3,2,1,0:T(4,128)S(1)} async-done(((f32[16,3,4,128]{3,2,1,0:T(4,128)}), f32[16,3,4,128]{3,2,1,0:T(4,128)S(1)}, u32[]{:S(2)}, u32[]{:S(2)}) %all-to-all-start.1) | async-done | bytes 98336 | tf_op jit(solution)/shard_map/all_to_all | solution.py:325
  28.3 0.0 copy-done
  28.3 0.8 %finish.1 = f32[8,256]{1,0:T(8,128)} custom-call(f32[16,3,4,128]{3,2,1,0:T(4,128)S(1)} %all-to-all-done.1.refs_0_, f32[4,8,128]{2,1,0:T(8,128)S(1)} %direct.1.refs_1_, f32[4,8,128]{2,1,0:T(8,128)S(1)} %collective-permute-done.3.refs_2_, bf16[2,32,128]{2,1,0:T(8,128)(2,1)S(1)} %copy-done), custom_call_target="tpu_custom_call" | custom-call | tf_op jit(solution)/shard_map/finish/pallas_call | solution.py:415
Async XLA Ops:
  1.6 14.0 %all-to-all-start = ((bf16[16,2,8,128]{3,2,1,0:T(8,128)(2,1)}), bf16[16,2,8,128]{3,2,1,0:T(8,128)(2,1)S(1)}, u32[]{:S(2)}, u32[]{:S(2)}) async-start(bf16[16,2,8,128]{3,2,1,0:T(8,128)(2,1)} %get-tuple-element.16), calls=%async_computation | async-start | bytes 131072 | tf_op jit(solution)/shard_map/all_to_all | solution.py:325
  9.0 1.2 %collective-permute-start = (bf16[8,256]{1,0:T(8,128)(2,1)S(1)}, bf16[8,256]{1,0:T(8,128)(2,1)S(1)}, u32[]{:S(2)}, u32[]{:S(2)}) collective-permute-start(bf16[8,256]{1,0:T(8,128)(2,1)S(1)} %get-tuple-element.20.refs_7_), channel_id=1, source_target_pairs={{0,1},{1,0},{2,3},{3,2},{4,5},{5,4},{6,7},{7,6},{8,9},{9,8},{10,11... | collective-permute-start | bytes 12296 | tf_op jit(solution)/shard_map/ppermute | solution.py:356
  12.4 16.0 %copy-start = (bf16[2,32,128]{2,1,0:T(8,128)(2,1)S(1)}, bf16[2,32,128]{2,1,0:T(8,128)(2,1)}, u32[]{:S(2)}) copy-start(bf16[2,32,128]{2,1,0:T(8,128)(2,1)} %refs_3_.5) | copy-start | bytes 49156
  12.4 1.3 %collective-permute-start.1 = (f32[16,2,4,128]{3,2,1,0:T(4,128)S(1)}, f32[16,2,4,128]{3,2,1,0:T(4,128)S(1)}, u32[]{:S(2)}, u32[]{:S(2)}) collective-permute-start(f32[16,2,4,128]{3,2,1,0:T(4,128)S(1)} %get-tuple-element.26), channel_id=1, source_target_pairs={{0,1},{1,0},{2,3},{3,2},{4,5},{5,4},{6,7},{7,6},{8,9},{9,8},{10,11... | collective-permute-start | bytes 196616 | tf_op jit(solution)/shard_map/ppermute | solution.py:381
  17.3 11.0 %all-to-all-start.1 = ((f32[16,3,4,128]{3,2,1,0:T(4,128)}), f32[16,3,4,128]{3,2,1,0:T(4,128)S(1)}, u32[]{:S(2)}, u32[]{:S(2)}) async-start(f32[16,3,4,128]{3,2,1,0:T(4,128)} %far.1), calls=%async_computation.1 | async-start | bytes 196608 | tf_op jit(solution)/shard_map/all_to_all | solution.py:325
  21.3 1.3 %collective-permute-start.2 = (bf16[16,2,8,128]{3,2,1,0:T(8,128)(2,1)S(1)}, bf16[16,2,8,128]{3,2,1,0:T(8,128)(2,1)S(1)}, u32[]{:S(2)}, u32[]{:S(2)}) collective-permute-start(bf16[16,2,8,128]{3,2,1,0:T(8,128)(2,1)S(1)} %all-to-all-done.every_ref.refs_4_), channel_id=1, source_target_pairs={{0,1},{1,0},{2,3},{3,2},{4,5},{5,4},{6,7},{7,6},{8,9},{9,8},{10,11... | collective-permute-start | bytes 196616 | tf_op jit(solution)/shard_map/ppermute | solution.py:398
  26.0 1.3 %collective-permute-start.3 = (f32[4,8,128]{2,1,0:T(8,128)S(1)}, f32[4,8,128]{2,1,0:T(8,128)S(1)}, u32[]{:S(2)}, u32[]{:S(2)}) collective-permute-start(f32[4,8,128]{2,1,0:T(8,128)S(1)} %direct.1.refs_1_), channel_id=1, source_target_pairs={{0,1},{1,0},{2,3},{3,2},{4,5},{5,4},{6,7},{7,6},{8,9},{9,8},{10,11... | collective-permute-start | bytes 49160 | tf_op jit(solution)/shard_map/ppermute | solution.py:414

commit v6 on v5

--- a/solution.py
+++ b/solution.py
@@ -12,9 +12,8 @@
 FIRST = (((0,), (0,)), ((), ()))
 HBM = pl.BlockSpec(memory_space=pltpu.HBM)
 VMEM = pl.BlockSpec(memory_space=pltpu.VMEM)
-CHUNKS = 4
-UNROLL = 24
-EARLY = 2
+EARLY, LATER = 1, 1
+UNROLL = 48
 GROUP = ("x", "col", "z")
 
 
@@ -108,50 +107,38 @@
         copy.wait()
 
 
-def near_copies(blocks_hbm, blocks_ref, sems, first, chunks):
-    size = blocks_hbm.shape[0] // CHUNKS
-    skipped = CHUNKS - chunks
+def start_indices(owner_hbm, col_hbm, row_hbm, owner, col, row, sems):
     return [
-        start(
-            blocks_hbm.at[pl.ds((skipped + c) * size, size)],
-            blocks_ref.at[pl.ds(c * size, size)],
-            sems.at[first + c],
-        )
-        for c in range(chunks)
-    ]
-
-
-def near_loop(first, size, body):
-    def group(g, _):
-        body([first + g * UNROLL + u for u in range(UNROLL)])
-        return 0
-
-    lax.fori_loop(0, size // UNROLL, group, 0)
-
-
-def mirror_kernel(
-    owner_hbm, col_hbm, row_hbm, blocks_hbm, far, coupling_ref, early_ref, mine_ref, other_ref,
-    by_row_ref, by_col_ref, gather_ref, spread_ref, keep_ref, give_ref,
-    owner, col, row, blocks_ref, cells_ref, sums_ref, sems, *, inner,
-):
-    small = [
         start(owner_hbm, owner, sems.at[0]),
         start(col_hbm, col, sems.at[1]),
         start(row_hbm, row, sems.at[2]),
     ]
-    copies = near_copies(blocks_hbm, blocks_ref, sems, 3, CHUNKS - EARLY)
+
+
+def near_copies(blocks_hbm, first, blocks_ref, chunks, sems):
+    size = blocks_ref.shape[0] // chunks
+    return [
+        start(blocks_hbm.at[pl.ds(first + c * size, size)], blocks_ref.at[pl.ds(c * size, size)], sems.at[3 + c])
+        for c in range(chunks)
+    ]
+
+
+def near_loop(first, size, body):
+    unroll = min(UNROLL, size)
+
+    def group(g, _):
+        body([first + g * unroll + u for u in range(unroll)])
+        return 0
+
+    lax.fori_loop(0, size // unroll, group, 0)
+
+
+def turn_kernel(
+    far, coupling_ref, by_row_ref, by_col_ref, gather_ref, spread_ref, *, inner
+):
     count, size = coupling_ref.shape
     rank = round(size**0.5)
-    devices = keep_ref.shape[0]
-    early, width, _ = early_ref.shape
-    chunk = early // EARLY
-    row_clusters = cells_ref.shape[0]
-    me = lax.axis_index("col")
-    for k in range(2):
-        cells_ref[2 * me + k] = mine_ref[:, k * width : (k + 1) * width].astype(f32)
-        cells_ref[2 - 2 * me + k] = other_ref[:, k * width : (k + 1) * width].astype(f32)
-    sums_ref[...] = jnp.zeros(sums_ref.shape, f32)
-
+    devices = gather_ref.shape[0] // 8
     source = lax.broadcasted_iota(jnp.int32, (8 * devices, count), 0)
     target = lax.broadcasted_iota(jnp.int32, (4 * devices, count), 0)
     for n in range(2):
@@ -171,24 +158,43 @@
     for k in range(rank):
         by_col_ref[k * rank : (k + 1) * rank, :] = by_row_ref[pl.ds(k, rank, stride=rank), :]
 
+
+def mirror_kernel(
+    owner_hbm, col_hbm, row_hbm, blocks_hbm, early_ref, mine_ref, other_ref,
+    keep_ref, give_ref,
+    owner, col, row, later_ref, cells_ref, sums_ref, sems, *, inner,
+):
+    early, width, _ = early_ref.shape
+    chunk = early // EARLY
+    indices = start_indices(owner_hbm, col_hbm, row_hbm, owner, col, row, sems)
+    copies = near_copies(blocks_hbm, early, later_ref, LATER, sems)
+    devices = keep_ref.shape[0]
+    row_clusters = cells_ref.shape[0]
+    me = lax.axis_index("col")
+    for k in range(2):
+        cells_ref[2 * me + k] = mine_ref[:, k * width : (k + 1) * width].astype(f32)
+        cells_ref[2 - 2 * me + k] = other_ref[:, k * width : (k + 1) * width].astype(f32)
+    sums_ref[...] = jnp.zeros(sums_ref.shape, f32)
+
     def multiply(source_ref, first):
         def body(group):
             done = []
             for p in group:
                 j = owner[0, p] * row_clusters + col[0, p]
                 at = 2 * slot_of(j, inner) + (j & 1)
-                done.append((at, dot(cells_ref[row[0, p]].astype(bf16), source_ref[p - first], PLAIN)))
+                cells = cells_ref[row[0, p]].astype(bf16)
+                done.append((at, dot(cells, source_ref[p - first], PLAIN)))
             for at, mirrored in done:
                 sums_ref[at] += mirrored
 
         return body
 
-    for copy in small:
+    for copy in indices:
         copy.wait()
     near_loop(0, early, multiply(early_ref, 0))
     for c, copy in enumerate(copies):
         copy.wait()
-        near_loop(early + c * chunk, chunk, multiply(blocks_ref, early))
+        near_loop(early + c * chunk, chunk, multiply(later_ref, early))
 
     def store(d):
         for k in range(2):
@@ -244,13 +250,9 @@
     owner_hbm, col_hbm, row_hbm, blocks_hbm, every_ref, others_ref,
     out_ref, owner, col, row, blocks_ref, cells_ref, sems, *, inner,
 ):
-    small = [
-        start(owner_hbm, owner, sems.at[0]),
-        start(col_hbm, col, sems.at[1]),
-        start(row_hbm, row, sems.at[2]),
-    ]
-    copies = near_copies(blocks_hbm, blocks_ref, sems, 3, CHUNKS)
-    chunk = blocks_ref.shape[0] // CHUNKS
+    indices = start_indices(owner_hbm, col_hbm, row_hbm, owner, col, row, sems)
+    copies = near_copies(blocks_hbm, 0, blocks_ref, EARLY + LATER, sems)
+    chunk = blocks_ref.shape[0] // (EARLY + LATER)
     row_clusters = out_ref.shape[0]
     out_ref[...] = jnp.zeros(out_ref.shape, f32)
     me = lax.axis_index("col")
@@ -262,7 +264,7 @@
             cells_ref[d, k] = jnp.concatenate([first[4 * k : 4 * k + 4], second[4 * k : 4 * k + 4]], axis=0)
 
     each(every_ref.shape[0], load)
-    for copy in small:
+    for copy in indices:
         copy.wait()
 
     def body(group):
@@ -324,6 +326,7 @@
     def exchange(blocks):
         return lax.all_to_all(blocks, GROUP, split_axis=0, concat_axis=0, tiled=True)
 
+    turn_cost = pl.CostEstimate(flops=10**6, bytes_accessed=3 * 10**6, transcendentals=0)
     near_cost = pl.CostEstimate(
         flops=2 * pairs * sides * width * width, bytes_accessed=10**7, transcendentals=0
     )
@@ -331,7 +334,9 @@
     owner, column, line = [in_hbm(a.reshape(1, pairs)) for a in (near_owner, near_col, near_row)]
     first, second = [in_hbm(a.reshape(1, count)) for a in (far_row, far_col)]
     blocks = in_hbm(near_blocks)
-    early = EARLY * (pairs // CHUNKS)
+    part = pairs // (EARLY + LATER)
+    block = near_blocks.shape[1:]
+    index_scratch = [pltpu.SMEM((1, pairs), jnp.int32)] * 3
     packed, mine, far, couplings, early_blocks = pl.pallas_call(
         lambda *refs: pack_kernel(*refs, inner=inner),
         out_shape=[
@@ -339,7 +344,7 @@
             shaped(cells.shape, bf16),
             shaped((2, 1, count), jnp.int32),
             shaped(coupling.shape, bf16),
-            shaped((early,) + near_blocks.shape[1:], bf16),
+            shaped((EARLY * part,) + block, bf16),
         ],
         in_specs=[HBM] * 6,
         out_specs=[HBM] + [VMEM] * 4,
@@ -354,30 +359,36 @@
     )(in_hbm(cells), in_hbm(basis_t), first, second, in_hbm(coupling), blocks)
     every = exchange(packed)
     other = lax.ppermute(mine, "col", swap)
-    index_scratch = [pltpu.SMEM((1, pairs), jnp.int32)] * 3
-    by_row, by_col, gather, spread, keep, give = pl.pallas_call(
-        lambda *refs: mirror_kernel(*refs, inner=inner),
+    by_row, by_col, gather, spread = pl.pallas_call(
+        lambda *refs: turn_kernel(*refs, inner=inner),
         out_shape=[
             shaped((rank * rank, count), f32),
             shaped((rank * rank, count), f32),
             shaped((8 * devices, 4 * count), bf16),
             shaped((4 * count, 4 * devices), bf16),
-            shaped((devices, 2, 4, 128), f32),
-            shaped((devices, 2, 4, 128), f32),
-        ],
-        in_specs=[HBM] * 4 + [VMEM] * 5,
-        out_specs=[VMEM] * 6,
+        ],
+        in_specs=[VMEM] * 2,
+        out_specs=[VMEM] * 4,
+        compiler_params=params,
+        cost_estimate=turn_cost,
+        name="turn",
+    )(far, couplings)
+    keep, give = pl.pallas_call(
+        lambda *refs: mirror_kernel(*refs, inner=inner),
+        out_shape=[shaped((devices, 2, 4, 128), f32)] * 2,
+        in_specs=[HBM] * 4 + [VMEM] * 3,
+        out_specs=[VMEM] * 2,
         scratch_shapes=index_scratch
         + [
-            pltpu.VMEM((pairs - early,) + near_blocks.shape[1:], bf16),
+            pltpu.VMEM((LATER * part,) + block, bf16),
             pltpu.VMEM((row_clusters, sides, width), f32),
             pltpu.VMEM((2 * devices, sides, width), f32),
-            pltpu.SemaphoreType.DMA((3 + CHUNKS,)),
+            pltpu.SemaphoreType.DMA((3 + LATER,)),
         ],
         compiler_params=params,
         cost_estimate=near_cost,
         name="mirror",
-    )(owner, column, line, blocks, far, couplings, early_blocks, mine, other)
+    )(owner, column, line, blocks, early_blocks, mine, other)
     got = lax.ppermute(give, "col", swap)
     partial = pl.pallas_call(
         far_kernel,
@@ -405,7 +416,7 @@
         + [
             pltpu.VMEM(near_blocks.shape, bf16),
             pltpu.VMEM(payload.shape, f32),
-            pltpu.SemaphoreType.DMA((3 + CHUNKS,)),
+            pltpu.SemaphoreType.DMA((3 + EARLY + LATER,)),
         ],
         compiler_params=params,
         cost_estimate=near_cost,

time: 29.4 us -> 29.3 us (level)
  waiting for transfers between devices: 6.53 us -> 6.16 us
  Pallas kernels: 9.45 us -> 9.8 us
    ppermute x1, waiting for transfers between devices: 0.91 us -> 0.44 us  [shards(): got = lax.ppermute(give, 'col', swap)]
    pallas_call x0 -> x1, Pallas kernels: none -> 0.46 us  [shards(): pl.pallas_call(lambda *refs: turn_kernel(*refs, inner=inner), out_shape=[...]
  transfers between devices with their start and end apart: 6 -> 6, of which waited for: 6 -> 6; matrix products, arithmetic and copies ran while one was open for 0% -> 0% of each run, Pallas kernels for 19% -> 20%
where the time goes in v6:
time: 29.3 us; the launch traced here: 29 us
  starting transfers between devices  12.9 us (44%)
  Pallas kernels  9.8 us (33%)
  waiting for transfers between devices  6.16 us (21%)
    all_to_all x2, starting transfers between devices, exchange(): lax.all_to_all(blocks, GROUP, split_axis=0, concat_axis=0, tiled=True)  11.3 us
    pallas_call x1, Pallas kernels, shards(): pl.pallas_call(lambda *refs: direct_kernel(*refs, inner=inner), out_shape...  3.34 us
    all_to_all x2, waiting for transfers between devices, exchange(): lax.all_to_all(blocks, GROUP, split_axis=0, concat_axis=0, tiled=True)  3.15 us
    pallas_call x1, Pallas kernels, shards(): pl.pallas_call(lambda *refs: mirror_kernel(*refs, inner=inner), out_shape...  2 us
    pallas_call x1, Pallas kernels, shards(): pl.pallas_call(far_kernel, out_shape=shaped((devices, 3, 4, 128), f32), i...  1.64 us
    pallas_call x1, Pallas kernels, shards(): pl.pallas_call(lambda *refs: pack_kernel(*refs, inner=inner), out_shape=[...  1.6 us
    ppermute x1, waiting for transfers between devices, shards(): every_other = lax.ppermute(every, 'col', swap)  0.91 us
    ppermute x1, waiting for transfers between devices, shards(): others = lax.ppermute(direct, 'col', swap)  0.84 us
  transfers between devices with their start and end apart: 6, of which 6 were waited for; matrix products, arithmetic and copies ran while one was open for 0% of the time, Pallas kernels for 20%

profile of v6, /device:TPU:0, one launch (start us, length us, event | category | flops | bytes accessed | tf_op | source)
XLA Modules:
  0.0 29.0 jit_solution(638388961748680972)
XLA Ops:
  0.0 1.6 %pack.1 = (bf16[16,2,8,128]{3,2,1,0:T(8,128)(2,1)}, bf16[8,256]{1,0:T(8,128)(2,1)S(1)}, s32[2,1,128]{2,1,0:T(1,128)S(1)}, bf16[128,1024]{1,0:T(8,128)(2,1)S(1)}, bf16[48,128,128]{2,1,0:T(8,128)(2,1)S(1)}) custom-call(bf16[8,256]{1,0:T(8,128)(2,1)} %refs_0_.1, bf16[2,32,128]{2,1,0:T(8,128)(2,1)} %refs_3_.5, s32[1,128]{1,0:T(1,128)} %bitcast.11, ...), custom_call_target="tpu_custom_call" | custom-call | tf_op jit(solution)/shard_map/pack/pallas_call | solution.py:340
  1.6 7.4 %all-to-all-start = ((bf16[16,2,8,128]{3,2,1,0:T(8,128)(2,1)}), bf16[16,2,8,128]{3,2,1,0:T(8,128)(2,1)S(1)}, u32[]{:S(2)}, u32[]{:S(2)}) async-start(bf16[16,2,8,128]{3,2,1,0:T(8,128)(2,1)} %get-tuple-element.16), calls=%async_computation | async-start | bytes 131072 | tf_op jit(solution)/shard_map/all_to_all | solution.py:327
  9.0 0.4 %collective-permute-start = (bf16[8,256]{1,0:T(8,128)(2,1)S(1)}, bf16[8,256]{1,0:T(8,128)(2,1)S(1)}, u32[]{:S(2)}, u32[]{:S(2)}) collective-permute-start(bf16[8,256]{1,0:T(8,128)(2,1)S(1)} %get-tuple-element.24.refs_5_), channel_id=1, source_target_pairs={{0,1},{1,0},{2,3},{3,2},{4,5},{5,4},{6,7},{7,6},{8,9},{9,8},{10,11... | collective-permute-start | bytes 12296 | tf_op jit(solution)/shard_map/ppermute | solution.py:361
  9.4 0.8 %collective-permute-done.refs_6_ = bf16[8,256]{1,0:T(8,128)(2,1)S(1)} collective-permute-done((bf16[8,256]{1,0:T(8,128)(2,1)S(1)}, bf16[8,256]{1,0:T(8,128)(2,1)S(1)}, u32[]{:S(2)}, u32[]{:S(2)}) %collective-permute-start) | collective-permute-done | bytes 4128 | tf_op jit(solution)/shard_map/ppermute | solution.py:361
  10.2 2.0 %mirror.1 = (f32[16,2,4,128]{3,2,1,0:T(4,128)S(1)}, f32[16,2,4,128]{3,2,1,0:T(4,128)S(1)}) custom-call(s32[1,96]{1,0:T(1,128)} %bitcast.5, s32[1,96]{1,0:T(1,128)} %bitcast.7, s32[1,96]{1,0:T(1,128)} %bitcast.9, bf16[96,128,128]{2,1,0:T(8,128)(2,1)} %refs_3_.4, bf16[48,128,128]{2,1,0:T(8,128)(2,1)S(1)} %get-tuple-element.23.refs_4_, ...), custom_call_target="tpu_custom_call" | custom-call | flops 25165824 | bytes 10000000 | tf_op jit(solution)/shard_map/mirror/pallas_call | solution.py:376
  12.2 0.0 copy-start
  12.2 0.4 %collective-permute-start.1 = (f32[16,2,4,128]{3,2,1,0:T(4,128)S(1)}, f32[16,2,4,128]{3,2,1,0:T(4,128)S(1)}, u32[]{:S(2)}, u32[]{:S(2)}) collective-permute-start(f32[16,2,4,128]{3,2,1,0:T(4,128)S(1)} %get-tuple-element.26), channel_id=1, source_target_pairs={{0,1},{1,0},{2,3},{3,2},{4,5},{5,4},{6,7},{7,6},{8,9},{9,8},{10,11... | collective-permute-start | bytes 196616 | tf_op jit(solution)/shard_map/ppermute | solution.py:392
  12.7 0.5 %turn.1 = (f32[1024,128]{1,0:T(8,128)S(1)}, f32[1024,128]{1,0:T(8,128)S(1)}, bf16[128,512]{1,0:T(8,128)(2,1)S(1)}, bf16[512,64]{1,0:T(8,128)(2,1)S(1)}) custom-call(s32[2,1,128]{2,1,0:T(1,128)S(1)} %get-tuple-element.17.refs_0_, bf16[128,1024]{1,0:T(8,128)(2,1)S(1)} %get-tuple-element.18.refs_1_), custom_call_target="tpu_custom_call" | custom-call | flops 1000000 | bytes 3000000 | tf_op jit(solution)/shard_map/turn/pallas_call | solution.py:362
  13.1 0.4 %collective-permute-done.1.got_ref = f32[16,2,4,128]{3,2,1,0:T(4,128)S(1)} collective-permute-done((f32[16,2,4,128]{3,2,1,0:T(4,128)S(1)}, f32[16,2,4,128]{3,2,1,0:T(4,128)S(1)}, u32[]{:S(2)}, u32[]{:S(2)}) %collective-permute-start.1) | collective-permute-done | bytes 65568 | tf_op jit(solution)/shard_map/ppermute | solution.py:392
  13.6 2.1 %all-to-all-done.every_ref.refs_4_ = bf16[16,2,8,128]{3,2,1,0:T(8,128)(2,1)S(1)} async-done(((bf16[16,2,8,128]{3,2,1,0:T(8,128)(2,1)}), bf16[16,2,8,128]{3,2,1,0:T(8,128)(2,1)S(1)}, u32[]{:S(2)}, u32[]{:S(2)}) %all-to-all-start) | async-done | bytes 65568 | tf_op jit(solution)/shard_map/all_to_all | solution.py:327
  15.6 1.6 %far.1 = f32[16,3,4,128]{3,2,1,0:T(4,128)} custom-call(bf16[16,2,8,128]{3,2,1,0:T(8,128)(2,1)S(1)} %all-to-all-done.every_ref.refs_4_, bf16[128,512]{1,0:T(8,128)(2,1)S(1)} %get-tuple-element.19.gather_ref, bf16[512,64]{1,0:T(8,128)(2,1)S(1)} %get-tuple-element.20.spread_ref, f32[1024,128]{1,0:T(8,128)S(1)} %get-tuple-element.21.by_row_ref, ...), custom_call_target="tpu_custom_call" | custom-call | tf_op jit(solution)/shard_map/far/pallas_call | solution.py:393
  17.3 3.9 %all-to-all-start.1 = ((f32[16,3,4,128]{3,2,1,0:T(4,128)}), f32[16,3,4,128]{3,2,1,0:T(4,128)S(1)}, u32[]{:S(2)}, u32[]{:S(2)}) async-start(f32[16,3,4,128]{3,2,1,0:T(4,128)} %far.1), calls=%async_computation.1 | async-start | bytes 196608 | tf_op jit(solution)/shard_map/all_to_all | solution.py:327
  21.2 0.4 %collective-permute-start.2 = (bf16[16,2,8,128]{3,2,1,0:T(8,128)(2,1)S(1)}, bf16[16,2,8,128]{3,2,1,0:T(8,128)(2,1)S(1)}, u32[]{:S(2)}, u32[]{:S(2)}) collective-permute-start(bf16[16,2,8,128]{3,2,1,0:T(8,128)(2,1)S(1)} %all-to-all-done.every_ref.refs_4_), channel_id=1, source_target_pairs={{0,1},{1,0},{2,3},{3,2},{4,5},{5,4},{6,7},{7,6},{8,9},{9,8},{10,11... | collective-permute-start | bytes 196616 | tf_op jit(solution)/shard_map/ppermute | solution.py:409
  21.6 0.9 %collective-permute-done.2.refs_5_ = bf16[16,2,8,128]{3,2,1,0:T(8,128)(2,1)S(1)} collective-permute-done((bf16[16,2,8,128]{3,2,1,0:T(8,128)(2,1)S(1)}, bf16[16,2,8,128]{3,2,1,0:T(8,128)(2,1)S(1)}, u32[]{:S(2)}, u32[]{:S(2)}) %collective-permute-start.2) | collective-permute-done | bytes 65568 | tf_op jit(solution)/shard_map/ppermute | solution.py:409
  22.5 3.3 %direct.1.refs_1_ = f32[4,8,128]{2,1,0:T(8,128)S(1)} custom-call(s32[1,96]{1,0:T(1,128)} %bitcast.6, s32[1,96]{1,0:T(1,128)} %bitcast.8, s32[1,96]{1,0:T(1,128)} %bitcast.10, bf16[96,128,128]{2,1,0:T(8,128)(2,1)} %refs_3_.4, bf16[16,2,8,128]{3,2,1,0:T(8,128)(2,1)S(1)} %all-to-all-done.every_ref.refs_4_, ...), custom_call_target="tpu_custom_call" | custom-call | flops 25165824 | bytes 10000000 | tf_op jit(solution)/shard_map/direct/pallas_call | solution.py:410
  25.8 0.4 %collective-permute-start.3 = (f32[4,8,128]{2,1,0:T(8,128)S(1)}, f32[4,8,128]{2,1,0:T(8,128)S(1)}, u32[]{:S(2)}, u32[]{:S(2)}) collective-permute-start(f32[4,8,128]{2,1,0:T(8,128)S(1)} %direct.1.refs_1_), channel_id=1, source_target_pairs={{0,1},{1,0},{2,3},{3,2},{4,5},{5,4},{6,7},{7,6},{8,9},{9,8},{10,11... | collective-permute-start | bytes 49160 | tf_op jit(solution)/shard_map/ppermute | solution.py:425
  26.3 0.8 %collective-permute-done.3.refs_2_ = f32[4,8,128]{2,1,0:T(8,128)S(1)} collective-permute-done((f32[4,8,128]{2,1,0:T(8,128)S(1)}, f32[4,8,128]{2,1,0:T(8,128)S(1)}, u32[]{:S(2)}, u32[]{:S(2)}) %collective-permute-start.3) | collective-permute-done | bytes 16416 | tf_op jit(solution)/shard_map/ppermute | solution.py:425
  27.1 1.1 %all-to-all-done.1.refs_0_ = f32[16,3,4,128]{3,2,1,0:T(4,128)S(1)} async-done(((f32[16,3,4,128]{3,2,1,0:T(4,128)}), f32[16,3,4,128]{3,2,1,0:T(4,128)S(1)}, u32[]{:S(2)}, u32[]{:S(2)}) %all-to-all-start.1) | async-done | bytes 98336 | tf_op jit(solution)/shard_map/all_to_all | solution.py:327
  28.2 0.0 copy-done
  28.2 0.8 %finish.1 = f32[8,256]{1,0:T(8,128)} custom-call(f32[16,3,4,128]{3,2,1,0:T(4,128)S(1)} %all-to-all-done.1.refs_0_, f32[4,8,128]{2,1,0:T(8,128)S(1)} %direct.1.refs_1_, f32[4,8,128]{2,1,0:T(8,128)S(1)} %collective-permute-done.3.refs_2_, bf16[2,32,128]{2,1,0:T(8,128)(2,1)S(1)} %copy-done), custom_call_target="tpu_custom_call" | custom-call | tf_op jit(solution)/shard_map/finish/pallas_call | solution.py:426
Async XLA Ops:
  1.6 14.0 %all-to-all-start = ((bf16[16,2,8,128]{3,2,1,0:T(8,128)(2,1)}), bf16[16,2,8,128]{3,2,1,0:T(8,128)(2,1)S(1)}, u32[]{:S(2)}, u32[]{:S(2)}) async-start(bf16[16,2,8,128]{3,2,1,0:T(8,128)(2,1)} %get-tuple-element.16), calls=%async_computation | async-start | bytes 131072 | tf_op jit(solution)/shard_map/all_to_all | solution.py:327
  9.0 1.2 %collective-permute-start = (bf16[8,256]{1,0:T(8,128)(2,1)S(1)}, bf16[8,256]{1,0:T(8,128)(2,1)S(1)}, u32[]{:S(2)}, u32[]{:S(2)}) collective-permute-start(bf16[8,256]{1,0:T(8,128)(2,1)S(1)} %get-tuple-element.24.refs_5_), channel_id=1, source_target_pairs={{0,1},{1,0},{2,3},{3,2},{4,5},{5,4},{6,7},{7,6},{8,9},{9,8},{10,11... | collective-permute-start | bytes 12296 | tf_op jit(solution)/shard_map/ppermute | solution.py:361
  12.2 16.0 %copy-start = (bf16[2,32,128]{2,1,0:T(8,128)(2,1)S(1)}, bf16[2,32,128]{2,1,0:T(8,128)(2,1)}, u32[]{:S(2)}) copy-start(bf16[2,32,128]{2,1,0:T(8,128)(2,1)} %refs_3_.5) | copy-start | bytes 49156
  12.2 1.3 %collective-permute-start.1 = (f32[16,2,4,128]{3,2,1,0:T(4,128)S(1)}, f32[16,2,4,128]{3,2,1,0:T(4,128)S(1)}, u32[]{:S(2)}, u32[]{:S(2)}) collective-permute-start(f32[16,2,4,128]{3,2,1,0:T(4,128)S(1)} %get-tuple-element.26), channel_id=1, source_target_pairs={{0,1},{1,0},{2,3},{3,2},{4,5},{5,4},{6,7},{7,6},{8,9},{9,8},{10,11... | collective-permute-start | bytes 196616 | tf_op jit(solution)/shard_map/ppermute | solution.py:392
  17.3 10.9 %all-to-all-start.1 = ((f32[16,3,4,128]{3,2,1,0:T(4,128)}), f32[16,3,4,128]{3,2,1,0:T(4,128)S(1)}, u32[]{:S(2)}, u32[]{:S(2)}) async-start(f32[16,3,4,128]{3,2,1,0:T(4,128)} %far.1), calls=%async_computation.1 | async-start | bytes 196608 | tf_op jit(solution)/shard_map/all_to_all | solution.py:327
  21.2 1.3 %collective-permute-start.2 = (bf16[16,2,8,128]{3,2,1,0:T(8,128)(2,1)S(1)}, bf16[16,2,8,128]{3,2,1,0:T(8,128)(2,1)S(1)}, u32[]{:S(2)}, u32[]{:S(2)}) collective-permute-start(bf16[16,2,8,128]{3,2,1,0:T(8,128)(2,1)S(1)} %all-to-all-done.every_ref.refs_4_), channel_id=1, source_target_pairs={{0,1},{1,0},{2,3},{3,2},{4,5},{5,4},{6,7},{7,6},{8,9},{9,8},{10,11... | collective-permute-start | bytes 196616 | tf_op jit(solution)/shard_map/ppermute | solution.py:409
  25.8 1.3 %collective-permute-start.3 = (f32[4,8,128]{2,1,0:T(8,128)S(1)}, f32[4,8,128]{2,1,0:T(8,128)S(1)}, u32[]{:S(2)}, u32[]{:S(2)}) collective-permute-start(f32[4,8,128]{2,1,0:T(8,128)S(1)} %direct.1.refs_1_), channel_id=1, source_target_pairs={{0,1},{1,0},{2,3},{3,2},{4,5},{5,4},{6,7},{7,6},{8,9},{9,8},{10,11... | collective-permute-start | bytes 49160 | tf_op jit(solution)/shard_map/ppermute | solution.py:425

commit v7 on v6

--- a/solution.py
+++ b/solution.py
@@ -205,11 +205,9 @@
 
 
 def far_kernel(
-    every_ref, gather_ref, spread_ref, by_row_ref, by_col_ref, keep_ref, got_ref,
-    out_hbm, near_ref, left_ref, right_ref, lines_ref, far_ref, sems,
+    every_ref, gather_ref, spread_ref, by_row_ref, by_col_ref,
+    far_ref, left_ref, right_ref, lines_ref,
 ):
-    near_ref[...] = keep_ref[...] + got_ref[...]
-    near = start(near_ref, out_hbm.at[:, pl.ds(0, 2)], sems.at[0])
     devices = every_ref.shape[0]
     size, count = left_ref.shape
     sides = 8
@@ -241,9 +239,13 @@
         far_ref[d, 0] = lines_ref[pl.ds(4 * d, 4), :]
 
     each(devices, store)
-    far = start(far_ref, out_hbm.at[:, pl.ds(2, 1)], sems.at[1])
+
+def join_kernel(far_ref, keep_ref, got_ref, out_hbm, near_ref, sems):
+    far = start(far_ref, out_hbm.at[:, pl.ds(2, 1)], sems.at[0])
+    near_ref[...] = keep_ref[...] + got_ref[...]
+    near = start(near_ref, out_hbm.at[:, pl.ds(0, 2)], sems.at[1])
+    far.wait()
     near.wait()
-    far.wait()
 
 
 def direct_kernel(
@@ -390,21 +392,25 @@
         name="mirror",
     )(owner, column, line, blocks, early_blocks, mine, other)
     got = lax.ppermute(give, "col", swap)
+    coupled = pl.pallas_call(
+        far_kernel,
+        out_shape=shaped((devices, 1, 4, 128), f32),
+        in_specs=[VMEM] * 5,
+        out_specs=VMEM,
+        scratch_shapes=[pltpu.VMEM((sides * rank, count), f32)] * 2 + [pltpu.VMEM((4 * devices, 128), f32)],
+        compiler_params=params,
+        cost_estimate=turn_cost,
+        name="far",
+    )(every, gather, spread, by_row, by_col)
     partial = pl.pallas_call(
-        far_kernel,
+        join_kernel,
         out_shape=shaped((devices, 3, 4, 128), f32),
-        in_specs=[VMEM] * 7,
+        in_specs=[VMEM] * 3,
         out_specs=HBM,
-        scratch_shapes=[pltpu.VMEM(keep.shape, f32)]
-        + [pltpu.VMEM((sides * rank, count), f32)] * 2
-        + [
-            pltpu.VMEM((4 * devices, 128), f32),
-            pltpu.VMEM((devices, 1, 4, 128), f32),
-            pltpu.SemaphoreType.DMA((2,)),
-        ],
-        compiler_params=params,
-        name="far",
-    )(every, gather, spread, by_row, by_col, keep, got)
+        scratch_shapes=[pltpu.VMEM(keep.shape, f32), pltpu.SemaphoreType.DMA((2,))],
+        compiler_params=params,
+        name="join",
+    )(coupled, keep, got)
     parts = exchange(partial)
     every_other = lax.ppermute(every, "col", swap)
     direct = pl.pallas_call(

time: 29.3 us -> 28.9 us (0.986)
  starting transfers between devices: 12.9 us -> 12.3 us
    ppermute x1, waiting for transfers between devices: 0.44 us -> 0.01 us  [shards(): got = lax.ppermute(give, 'col', swap)]
    all_to_all x2, waiting for transfers between devices: 3.15 us -> 3.55 us  [exchange(): lax.all_to_all(blocks, GROUP, split_axis=0, concat_axis=0, tiled=True)]
    all_to_all x2, starting transfers between devices: 11.3 us -> 10.9 us  [exchange(): lax.all_to_all(blocks, GROUP, split_axis=0, concat_axis=0, tiled=True)]
    pallas_call x1 -> x2, Pallas kernels: 1.64 us -> 1.66 us  [the longest x1 0.99 us: shards(): pl.pallas_call(far_kernel, out_shape=shaped((devices, 1, 4, 128), f32), i...]
  transfers between devices with their start and end apart: 6 -> 6, of which waited for: 6 -> 5; matrix products, arithmetic and copies ran while one was open for 0% -> 0% of each run, Pallas kernels for 20% -> 24%
where the time goes in v7:
time: 28.9 us; the launch traced here: 28.6 us
  starting transfers between devices  12.3 us (43%)
  Pallas kernels  9.81 us (34%)
  waiting for transfers between devices  6.32 us (22%)
    all_to_all x2, starting transfers between devices, exchange(): lax.all_to_all(blocks, GROUP, split_axis=0, concat_axis=0, tiled=True)  10.9 us
    all_to_all x2, waiting for transfers between devices, exchange(): lax.all_to_all(blocks, GROUP, split_axis=0, concat_axis=0, tiled=True)  3.55 us
    pallas_call x1, Pallas kernels, shards(): pl.pallas_call(lambda *refs: direct_kernel(*refs, inner=inner), out_shape...  3.34 us
    pallas_call x1, Pallas kernels, shards(): pl.pallas_call(lambda *refs: mirror_kernel(*refs, inner=inner), out_shape...  2 us
    pallas_call x1, Pallas kernels, shards(): pl.pallas_call(lambda *refs: pack_kernel(*refs, inner=inner), out_shape=[...  1.6 us
    ppermute x1, waiting for transfers between devices, shards(): every_other = lax.ppermute(every, 'col', swap)  1.01 us
    pallas_call x1, Pallas kernels, shards(): pl.pallas_call(far_kernel, out_shape=shaped((devices, 1, 4, 128), f32), i...  0.99 us
    ppermute x1, waiting for transfers between devices, shards(): others = lax.ppermute(direct, 'col', swap)  0.94 us
  transfers between devices with their start and end apart: 6, of which 5 were waited for; matrix products, arithmetic and copies ran while one was open for 0% of the time, Pallas kernels for 24%

profile of v7, /device:TPU:0, one launch (start us, length us, event | category | flops | bytes accessed | tf_op | source)
XLA Modules:
  0.0 28.6 jit_solution(2341517372483124909)
XLA Ops:
  0.0 1.6 %pack.1 = (bf16[16,2,8,128]{3,2,1,0:T(8,128)(2,1)}, bf16[8,256]{1,0:T(8,128)(2,1)S(1)}, s32[2,1,128]{2,1,0:T(1,128)S(1)}, bf16[128,1024]{1,0:T(8,128)(2,1)S(1)}, bf16[48,128,128]{2,1,0:T(8,128)(2,1)S(1)}) custom-call(bf16[8,256]{1,0:T(8,128)(2,1)} %refs_0_.1, bf16[2,32,128]{2,1,0:T(8,128)(2,1)} %refs_3_.5, s32[1,128]{1,0:T(1,128)} %bitcast.11, ...), custom_call_target="tpu_custom_call" | custom-call | tf_op jit(solution)/shard_map/pack/pallas_call | solution.py:342
  1.6 7.4 %all-to-all-start = ((bf16[16,2,8,128]{3,2,1,0:T(8,128)(2,1)}), bf16[16,2,8,128]{3,2,1,0:T(8,128)(2,1)S(1)}, u32[]{:S(2)}, u32[]{:S(2)}) async-start(bf16[16,2,8,128]{3,2,1,0:T(8,128)(2,1)} %get-tuple-element.16), calls=%async_computation | async-start | bytes 131072 | tf_op jit(solution)/shard_map/all_to_all | solution.py:329
  9.0 0.4 %collective-permute-start = (bf16[8,256]{1,0:T(8,128)(2,1)S(1)}, bf16[8,256]{1,0:T(8,128)(2,1)S(1)}, u32[]{:S(2)}, u32[]{:S(2)}) collective-permute-start(bf16[8,256]{1,0:T(8,128)(2,1)S(1)} %get-tuple-element.24.refs_5_), channel_id=1, source_target_pairs={{0,1},{1,0},{2,3},{3,2},{4,5},{5,4},{6,7},{7,6},{8,9},{9,8},{10,11... | collective-permute-start | bytes 12296 | tf_op jit(solution)/shard_map/ppermute | solution.py:363
  9.4 0.8 %collective-permute-done.refs_6_ = bf16[8,256]{1,0:T(8,128)(2,1)S(1)} collective-permute-done((bf16[8,256]{1,0:T(8,128)(2,1)S(1)}, bf16[8,256]{1,0:T(8,128)(2,1)S(1)}, u32[]{:S(2)}, u32[]{:S(2)}) %collective-permute-start) | collective-permute-done | bytes 4128 | tf_op jit(solution)/shard_map/ppermute | solution.py:363
  10.2 2.0 %mirror.1 = (f32[16,2,4,128]{3,2,1,0:T(4,128)S(1)}, f32[16,2,4,128]{3,2,1,0:T(4,128)S(1)}) custom-call(s32[1,96]{1,0:T(1,128)} %bitcast.5, s32[1,96]{1,0:T(1,128)} %bitcast.7, s32[1,96]{1,0:T(1,128)} %bitcast.9, bf16[96,128,128]{2,1,0:T(8,128)(2,1)} %refs_3_.4, bf16[48,128,128]{2,1,0:T(8,128)(2,1)S(1)} %get-tuple-element.23.refs_4_, ...), custom_call_target="tpu_custom_call" | custom-call | flops 25165824 | bytes 10000000 | tf_op jit(solution)/shard_map/mirror/pallas_call | solution.py:378
  12.2 0.0 copy-start
  12.2 0.4 %collective-permute-start.1 = (f32[16,2,4,128]{3,2,1,0:T(4,128)S(1)}, f32[16,2,4,128]{3,2,1,0:T(4,128)S(1)}, u32[]{:S(2)}, u32[]{:S(2)}) collective-permute-start(f32[16,2,4,128]{3,2,1,0:T(4,128)S(1)} %get-tuple-element.26), channel_id=1, source_target_pairs={{0,1},{1,0},{2,3},{3,2},{4,5},{5,4},{6,7},{7,6},{8,9},{9,8},{10,11... | collective-permute-start | bytes 196616 | tf_op jit(solution)/shard_map/ppermute | solution.py:394
  12.7 0.5 %turn.1 = (f32[1024,128]{1,0:T(8,128)S(1)}, f32[1024,128]{1,0:T(8,128)S(1)}, bf16[128,512]{1,0:T(8,128)(2,1)S(1)}, bf16[512,64]{1,0:T(8,128)(2,1)S(1)}) custom-call(s32[2,1,128]{2,1,0:T(1,128)S(1)} %get-tuple-element.17.refs_0_, bf16[128,1024]{1,0:T(8,128)(2,1)S(1)} %get-tuple-element.18.refs_1_), custom_call_target="tpu_custom_call" | custom-call | flops 1000000 | bytes 3000000 | tf_op jit(solution)/shard_map/turn/pallas_call | solution.py:364
  13.1 2.5 %all-to-all-done.every_ref.refs_4_ = bf16[16,2,8,128]{3,2,1,0:T(8,128)(2,1)S(1)} async-done(((bf16[16,2,8,128]{3,2,1,0:T(8,128)(2,1)}), bf16[16,2,8,128]{3,2,1,0:T(8,128)(2,1)S(1)}, u32[]{:S(2)}, u32[]{:S(2)}) %all-to-all-start) | async-done | bytes 65568 | tf_op jit(solution)/shard_map/all_to_all | solution.py:329
  15.6 1.0 %far.1.far_ref = f32[16,1,4,128]{3,2,1,0:T(4,128)S(1)} custom-call(bf16[16,2,8,128]{3,2,1,0:T(8,128)(2,1)S(1)} %all-to-all-done.every_ref.refs_4_, bf16[128,512]{1,0:T(8,128)(2,1)S(1)} %get-tuple-element.19.gather_ref, bf16[512,64]{1,0:T(8,128)(2,1)S(1)} %get-tuple-element.20.spread_ref, f32[1024,128]{1,0:T(8,128)S(1)} %get-tuple-element.21.by_row_ref, ...), custom_call_target="tpu_custom_call" | custom-call | flops 1000000 | bytes 3000000 | tf_op jit(solution)/shard_map/far/pallas_call | solution.py:395
  16.6 0.0 collective-permute-done.1.got_ref
  16.6 0.7 %join.1 = f32[16,3,4,128]{3,2,1,0:T(4,128)} custom-call(f32[16,1,4,128]{3,2,1,0:T(4,128)S(1)} %far.1.far_ref, f32[16,2,4,128]{3,2,1,0:T(4,128)S(1)} %get-tuple-element.25.keep_ref, f32[16,2,4,128]{3,2,1,0:T(4,128)S(1)} %collective-permute-done.1.got_ref), custom_call_target="tpu_custom_call" | custom-call | tf_op jit(solution)/shard_map/join/pallas_call | solution.py:405
  17.3 3.5 %all-to-all-start.1 = ((f32[16,3,4,128]{3,2,1,0:T(4,128)}), f32[16,3,4,128]{3,2,1,0:T(4,128)S(1)}, u32[]{:S(2)}, u32[]{:S(2)}) async-start(f32[16,3,4,128]{3,2,1,0:T(4,128)} %join.1), calls=%async_computation.1 | async-start | bytes 196608 | tf_op jit(solution)/shard_map/all_to_all | solution.py:329
  20.8 0.3 %collective-permute-start.2 = (bf16[16,2,8,128]{3,2,1,0:T(8,128)(2,1)S(1)}, bf16[16,2,8,128]{3,2,1,0:T(8,128)(2,1)S(1)}, u32[]{:S(2)}, u32[]{:S(2)}) collective-permute-start(bf16[16,2,8,128]{3,2,1,0:T(8,128)(2,1)S(1)} %all-to-all-done.every_ref.refs_4_), channel_id=1, source_target_pairs={{0,1},{1,0},{2,3},{3,2},{4,5},{5,4},{6,7},{7,6},{8,9},{9,8},{10,11... | collective-permute-start | bytes 196616 | tf_op jit(solution)/shard_map/ppermute | solution.py:415
  21.1 1.0 %collective-permute-done.2.refs_5_ = bf16[16,2,8,128]{3,2,1,0:T(8,128)(2,1)S(1)} collective-permute-done((bf16[16,2,8,128]{3,2,1,0:T(8,128)(2,1)S(1)}, bf16[16,2,8,128]{3,2,1,0:T(8,128)(2,1)S(1)}, u32[]{:S(2)}, u32[]{:S(2)}) %collective-permute-start.2) | collective-permute-done | bytes 65568 | tf_op jit(solution)/shard_map/ppermute | solution.py:415
  22.2 3.3 %direct.1.refs_1_ = f32[4,8,128]{2,1,0:T(8,128)S(1)} custom-call(s32[1,96]{1,0:T(1,128)} %bitcast.6, s32[1,96]{1,0:T(1,128)} %bitcast.8, s32[1,96]{1,0:T(1,128)} %bitcast.10, bf16[96,128,128]{2,1,0:T(8,128)(2,1)} %refs_3_.4, bf16[16,2,8,128]{3,2,1,0:T(8,128)(2,1)S(1)} %all-to-all-done.every_ref.refs_4_, ...), custom_call_target="tpu_custom_call" | custom-call | flops 25165824 | bytes 10000000 | tf_op jit(solution)/shard_map/direct/pallas_call | solution.py:416
  25.5 0.3 %collective-permute-start.3 = (f32[4,8,128]{2,1,0:T(8,128)S(1)}, f32[4,8,128]{2,1,0:T(8,128)S(1)}, u32[]{:S(2)}, u32[]{:S(2)}) collective-permute-start(f32[4,8,128]{2,1,0:T(8,128)S(1)} %direct.1.refs_1_), channel_id=1, source_target_pairs={{0,1},{1,0},{2,3},{3,2},{4,5},{5,4},{6,7},{7,6},{8,9},{9,8},{10,11... | collective-permute-start | bytes 49160 | tf_op jit(solution)/shard_map/ppermute | solution.py:431
  25.8 0.9 %collective-permute-done.3.refs_2_ = f32[4,8,128]{2,1,0:T(8,128)S(1)} collective-permute-done((f32[4,8,128]{2,1,0:T(8,128)S(1)}, f32[4,8,128]{2,1,0:T(8,128)S(1)}, u32[]{:S(2)}, u32[]{:S(2)}) %collective-permute-start.3) | collective-permute-done | bytes 16416 | tf_op jit(solution)/shard_map/ppermute | solution.py:431
  26.8 1.0 %all-to-all-done.1.refs_0_ = f32[16,3,4,128]{3,2,1,0:T(4,128)S(1)} async-done(((f32[16,3,4,128]{3,2,1,0:T(4,128)}), f32[16,3,4,128]{3,2,1,0:T(4,128)S(1)}, u32[]{:S(2)}, u32[]{:S(2)}) %all-to-all-start.1) | async-done | bytes 98336 | tf_op jit(solution)/shard_map/all_to_all | solution.py:329
  27.8 0.0 copy-done
  27.8 0.8 %finish.1 = f32[8,256]{1,0:T(8,128)} custom-call(f32[16,3,4,128]{3,2,1,0:T(4,128)S(1)} %all-to-all-done.1.refs_0_, f32[4,8,128]{2,1,0:T(8,128)S(1)} %direct.1.refs_1_, f32[4,8,128]{2,1,0:T(8,128)S(1)} %collective-permute-done.3.refs_2_, bf16[2,32,128]{2,1,0:T(8,128)(2,1)S(1)} %copy-done), custom_call_target="tpu_custom_call" | custom-call | tf_op jit(solution)/shard_map/finish/pallas_call | solution.py:432
Async XLA Ops:
  1.6 14.0 %all-to-all-start = ((bf16[16,2,8,128]{3,2,1,0:T(8,128)(2,1)}), bf16[16,2,8,128]{3,2,1,0:T(8,128)(2,1)S(1)}, u32[]{:S(2)}, u32[]{:S(2)}) async-start(bf16[16,2,8,128]{3,2,1,0:T(8,128)(2,1)} %get-tuple-element.16), calls=%async_computation | async-start | bytes 131072 | tf_op jit(solution)/shard_map/all_to_all | solution.py:329
  9.0 1.2 %collective-permute-start = (bf16[8,256]{1,0:T(8,128)(2,1)S(1)}, bf16[8,256]{1,0:T(8,128)(2,1)S(1)}, u32[]{:S(2)}, u32[]{:S(2)}) collective-permute-start(bf16[8,256]{1,0:T(8,128)(2,1)S(1)} %get-tuple-element.24.refs_5_), channel_id=1, source_target_pairs={{0,1},{1,0},{2,3},{3,2},{4,5},{5,4},{6,7},{7,6},{8,9},{9,8},{10,11... | collective-permute-start | bytes 12296 | tf_op jit(solution)/shard_map/ppermute | solution.py:363
  12.2 15.6 %copy-start = (bf16[2,32,128]{2,1,0:T(8,128)(2,1)S(1)}, bf16[2,32,128]{2,1,0:T(8,128)(2,1)}, u32[]{:S(2)}) copy-start(bf16[2,32,128]{2,1,0:T(8,128)(2,1)} %refs_3_.5) | copy-start | bytes 49156
  12.2 4.4 %collective-permute-start.1 = (f32[16,2,4,128]{3,2,1,0:T(4,128)S(1)}, f32[16,2,4,128]{3,2,1,0:T(4,128)S(1)}, u32[]{:S(2)}, u32[]{:S(2)}) collective-permute-start(f32[16,2,4,128]{3,2,1,0:T(4,128)S(1)} %get-tuple-element.26), channel_id=1, source_target_pairs={{0,1},{1,0},{2,3},{3,2},{4,5},{5,4},{6,7},{7,6},{8,9},{9,8},{10,11... | collective-permute-start | bytes 196616 | tf_op jit(solution)/shard_map/ppermute | solution.py:394
  17.3 10.5 %all-to-all-start.1 = ((f32[16,3,4,128]{3,2,1,0:T(4,128)}), f32[16,3,4,128]{3,2,1,0:T(4,128)S(1)}, u32[]{:S(2)}, u32[]{:S(2)}) async-start(f32[16,3,4,128]{3,2,1,0:T(4,128)} %join.1), calls=%async_computation.1 | async-start | bytes 196608 | tf_op jit(solution)/shard_map/all_to_all | solution.py:329
  20.8 1.3 %collective-permute-start.2 = (bf16[16,2,8,128]{3,2,1,0:T(8,128)(2,1)S(1)}, bf16[16,2,8,128]{3,2,1,0:T(8,128)(2,1)S(1)}, u32[]{:S(2)}, u32[]{:S(2)}) collective-permute-start(bf16[16,2,8,128]{3,2,1,0:T(8,128)(2,1)S(1)} %all-to-all-done.every_ref.refs_4_), channel_id=1, source_target_pairs={{0,1},{1,0},{2,3},{3,2},{4,5},{5,4},{6,7},{7,6},{8,9},{9,8},{10,11... | collective-permute-start | bytes 196616 | tf_op jit(solution)/shard_map/ppermute | solution.py:415
  25.5 1.2 %collective-permute-start.3 = (f32[4,8,128]{2,1,0:T(8,128)S(1)}, f32[4,8,128]{2,1,0:T(8,128)S(1)}, u32[]{:S(2)}, u32[]{:S(2)}) collective-permute-start(f32[4,8,128]{2,1,0:T(8,128)S(1)} %direct.1.refs_1_), channel_id=1, source_target_pairs={{0,1},{1,0},{2,3},{3,2},{4,5},{5,4},{6,7},{7,6},{8,9},{9,8},{10,11... | collective-permute-start | bytes 49160 | tf_op jit(solution)/shard_map/ppermute | solution.py:431

commit v8 on v7

--- a/solution.py
+++ b/solution.py
@@ -61,8 +61,8 @@
 
 
 def pack_kernel(
-    cells_hbm, basis_hbm, first_hbm, second_hbm, coupling_hbm, blocks_hbm,
-    out_hbm, mine_ref, far_ref, coupling_ref, early_ref,
+    cells_hbm, basis_hbm, first_hbm, second_hbm, blocks_hbm,
+    out_hbm, mine_ref, far_ref, early_ref,
     cells_ref, basis_ref, out_ref, sems, *, inner,
 ):
     copies = [
@@ -72,7 +72,6 @@
     ahead = [
         start(first_hbm, far_ref.at[0], sems.at[2]),
         start(second_hbm, far_ref.at[1], sems.at[3]),
-        start(coupling_hbm, coupling_ref, sems.at[4]),
         start(blocks_hbm.at[pl.ds(0, early_ref.shape[0])], early_ref, sems.at[5]),
     ]
     sides = cells_ref.shape[0]
@@ -134,8 +133,9 @@
 
 
 def turn_kernel(
-    far, coupling_ref, by_row_ref, by_col_ref, gather_ref, spread_ref, *, inner
+    far, coupling_hbm, by_row_ref, by_col_ref, gather_ref, spread_ref, coupling_ref, sem, *, inner
 ):
+    copy = start(coupling_hbm, coupling_ref, sem)
     count, size = coupling_ref.shape
     rank = round(size**0.5)
     devices = gather_ref.shape[0] // 8
@@ -153,6 +153,7 @@
         spread_ref[2 * n * count : (2 * n + 1) * count, :] = hot
         spread_ref[(2 * n + 1) * count : (2 * n + 2) * count, :] = hot
 
+    copy.wait()
     for t in range(0, size, 128):
         by_row_ref[t : t + 128, :] = coupling_ref[:, t : t + 128].astype(f32).T
     for k in range(rank):
@@ -160,7 +161,7 @@
 
 
 def mirror_kernel(
-    owner_hbm, col_hbm, row_hbm, blocks_hbm, early_ref, mine_ref, other_ref,
+    owner_hbm, col_hbm, row_hbm, blocks_hbm, early_ref, mine_ref, other_ref, _,
     keep_ref, give_ref,
     owner, col, row, later_ref, cells_ref, sums_ref, sems, *, inner,
 ):
@@ -339,17 +340,16 @@
     part = pairs // (EARLY + LATER)
     block = near_blocks.shape[1:]
     index_scratch = [pltpu.SMEM((1, pairs), jnp.int32)] * 3
-    packed, mine, far, couplings, early_blocks = pl.pallas_call(
+    packed, mine, far, early_blocks = pl.pallas_call(
         lambda *refs: pack_kernel(*refs, inner=inner),
         out_shape=[
             payload,
             shaped(cells.shape, bf16),
             shaped((2, 1, count), jnp.int32),
-            shaped(coupling.shape, bf16),
             shaped((EARLY * part,) + block, bf16),
         ],
-        in_specs=[HBM] * 6,
-        out_specs=[HBM] + [VMEM] * 4,
+        in_specs=[HBM] * 5,
+        out_specs=[HBM] + [VMEM] * 3,
         scratch_shapes=[
             pltpu.VMEM(cells.shape, bf16),
             pltpu.VMEM(basis_t.shape, bf16),
@@ -358,7 +358,7 @@
         ],
         compiler_params=params,
         name="pack",
-    )(in_hbm(cells), in_hbm(basis_t), first, second, in_hbm(coupling), blocks)
+    )(in_hbm(cells), in_hbm(basis_t), first, second, blocks)
     every = exchange(packed)
     other = lax.ppermute(mine, "col", swap)
     by_row, by_col, gather, spread = pl.pallas_call(
@@ -369,16 +369,17 @@
             shaped((8 * devices, 4 * count), bf16),
             shaped((4 * count, 4 * devices), bf16),
         ],
-        in_specs=[VMEM] * 2,
+        in_specs=[VMEM, HBM],
         out_specs=[VMEM] * 4,
+        scratch_shapes=[pltpu.VMEM(coupling.shape, bf16), pltpu.SemaphoreType.DMA],
         compiler_params=params,
         cost_estimate=turn_cost,
         name="turn",
-    )(far, couplings)
+    )(far, in_hbm(coupling))
     keep, give = pl.pallas_call(
         lambda *refs: mirror_kernel(*refs, inner=inner),
         out_shape=[shaped((devices, 2, 4, 128), f32)] * 2,
-        in_specs=[HBM] * 4 + [VMEM] * 3,
+        in_specs=[HBM] * 4 + [VMEM] * 4,
         out_specs=[VMEM] * 2,
         scratch_shapes=index_scratch
         + [
@@ -390,7 +391,7 @@
         compiler_params=params,
         cost_estimate=near_cost,
         name="mirror",
-    )(owner, column, line, blocks, early_blocks, mine, other)
+    )(owner, column, line, blocks, early_blocks, mine, other, spread)
     got = lax.ppermute(give, "col", swap)
     coupled = pl.pallas_call(
         far_kernel,

time: 28.9 us -> 28.9 us (level)
  Pallas kernels: 9.81 us -> 10.8 us
  waiting for transfers between devices: 6.32 us -> 5.48 us
    pallas_call x1, Pallas kernels: 0.46 us -> 1.43 us  [shards(): pl.pallas_call(lambda *refs: turn_kernel(*refs, inner=inner), out_shape=[...]
    ppermute x1, waiting for transfers between devices: 0.82 us -> 0.01 us  [shards(): other = lax.ppermute(mine, 'col', swap)]
  transfers between devices with their start and end apart: 6 -> 6, of which waited for: 5 -> 4; matrix products, arithmetic and copies ran while one was open for 0% -> 0% of each run, Pallas kernels for 24% -> 27%
where the time goes in v8:
time: 28.9 us; the launch traced here: 28.5 us
  starting transfers between devices  12.2 us (42%)
  Pallas kernels  10.8 us (37%)
  waiting for transfers between devices  5.48 us (19%)
    all_to_all x2, starting transfers between devices, exchange(): lax.all_to_all(blocks, GROUP, split_axis=0, concat_axis=0, tiled=True)  10.9 us
    all_to_all x2, waiting for transfers between devices, exchange(): lax.all_to_all(blocks, GROUP, split_axis=0, concat_axis=0, tiled=True)  3.57 us
    pallas_call x1, Pallas kernels, shards(): pl.pallas_call(lambda *refs: direct_kernel(*refs, inner=inner), out_shape...  3.33 us
    pallas_call x1, Pallas kernels, shards(): pl.pallas_call(lambda *refs: mirror_kernel(*refs, inner=inner), out_shape...  2 us
    pallas_call x1, Pallas kernels, shards(): pl.pallas_call(lambda *refs: pack_kernel(*refs, inner=inner), out_shape=[...  1.57 us
    pallas_call x1, Pallas kernels, shards(): pl.pallas_call(lambda *refs: turn_kernel(*refs, inner=inner), out_shape=[...  1.43 us
    pallas_call x1, Pallas kernels, shards(): pl.pallas_call(far_kernel, out_shape=shaped((devices, 1, 4, 128), f32), i...  0.99 us
    ppermute x1, waiting for transfers between devices, shards(): every_other = lax.ppermute(every, 'col', swap)  0.98 us
  transfers between devices with their start and end apart: 6, of which 4 were waited for; matrix products, arithmetic and copies ran while one was open for 0% of the time, Pallas kernels for 27%

profile of v8, /device:TPU:0, one launch (start us, length us, event | category | flops | bytes accessed | tf_op | source)
XLA Modules:
  0.0 28.5 jit_solution(4484705997972313433)
XLA Ops:
  0.0 1.6 %pack.1 = (bf16[16,2,8,128]{3,2,1,0:T(8,128)(2,1)}, bf16[8,256]{1,0:T(8,128)(2,1)S(1)}, s32[2,1,128]{2,1,0:T(1,128)S(1)}, bf16[48,128,128]{2,1,0:T(8,128)(2,1)S(1)}) custom-call(bf16[8,256]{1,0:T(8,128)(2,1)} %refs_0_.1, bf16[2,32,128]{2,1,0:T(8,128)(2,1)} %refs_3_.5, s32[1,128]{1,0:T(1,128)} %bitcast.11, s32[1,128]{1,0:T(1,128)} %bitcast.12, ...), custom_call_target="tpu_custom_call" | custom-call | tf_op jit(solution)/shard_map/pack/pallas_call | solution.py:343
  1.6 7.4 %all-to-all-start = ((bf16[16,2,8,128]{3,2,1,0:T(8,128)(2,1)}), bf16[16,2,8,128]{3,2,1,0:T(8,128)(2,1)S(1)}, u32[]{:S(2)}, u32[]{:S(2)}) async-start(bf16[16,2,8,128]{3,2,1,0:T(8,128)(2,1)} %get-tuple-element.15), calls=%async_computation | async-start | bytes 131072 | tf_op jit(solution)/shard_map/all_to_all | solution.py:330
  9.0 0.4 %collective-permute-start = (bf16[8,256]{1,0:T(8,128)(2,1)S(1)}, bf16[8,256]{1,0:T(8,128)(2,1)S(1)}, u32[]{:S(2)}, u32[]{:S(2)}) collective-permute-start(bf16[8,256]{1,0:T(8,128)(2,1)S(1)} %get-tuple-element.22.refs_5_), channel_id=1, source_target_pairs={{0,1},{1,0},{2,3},{3,2},{4,5},{5,4},{6,7},{7,6},{8,9},{9,8},{10,11... | collective-permute-start | bytes 12296 | tf_op jit(solution)/shard_map/ppermute | solution.py:363
  9.4 1.4 %turn.1 = (f32[1024,128]{1,0:T(8,128)S(1)}, f32[1024,128]{1,0:T(8,128)S(1)}, bf16[128,512]{1,0:T(8,128)(2,1)S(1)}, bf16[512,64]{1,0:T(8,128)(2,1)S(1)}) custom-call(s32[2,1,128]{2,1,0:T(1,128)S(1)} %get-tuple-element.16.refs_0_, bf16[128,1024]{1,0:T(8,128)(2,1)} %refs_1_.3), custom_call_target="tpu_custom_call" | custom-call | flops 1000000 | bytes 3000000 | tf_op jit(solution)/shard_map/turn/pallas_call | solution.py:364
  10.8 0.0 collective-permute-done.refs_6_
  10.8 2.0 %mirror.1 = (f32[16,2,4,128]{3,2,1,0:T(4,128)S(1)}, f32[16,2,4,128]{3,2,1,0:T(4,128)S(1)}) custom-call(s32[1,96]{1,0:T(1,128)} %bitcast.5, s32[1,96]{1,0:T(1,128)} %bitcast.7, s32[1,96]{1,0:T(1,128)} %bitcast.9, bf16[96,128,128]{2,1,0:T(8,128)(2,1)} %refs_3_.4, bf16[48,128,128]{2,1,0:T(8,128)(2,1)S(1)} %get-tuple-element.21.refs_4_, ...), custom_call_target="tpu_custom_call" | custom-call | flops 25165824 | bytes 10000000 | tf_op jit(solution)/shard_map/mirror/pallas_call | solution.py:379
  12.8 0.0 copy-start
  12.8 0.2 collective-permute-start.1
  13.1 2.5 %all-to-all-done.every_ref.refs_4_ = bf16[16,2,8,128]{3,2,1,0:T(8,128)(2,1)S(1)} async-done(((bf16[16,2,8,128]{3,2,1,0:T(8,128)(2,1)}), bf16[16,2,8,128]{3,2,1,0:T(8,128)(2,1)S(1)}, u32[]{:S(2)}, u32[]{:S(2)}) %all-to-all-start) | async-done | bytes 65568 | tf_op jit(solution)/shard_map/all_to_all | solution.py:330
  15.6 1.0 %far.1.far_ref = f32[16,1,4,128]{3,2,1,0:T(4,128)S(1)} custom-call(bf16[16,2,8,128]{3,2,1,0:T(8,128)(2,1)S(1)} %all-to-all-done.every_ref.refs_4_, bf16[128,512]{1,0:T(8,128)(2,1)S(1)} %get-tuple-element.17.gather_ref, bf16[512,64]{1,0:T(8,128)(2,1)S(1)} %get-tuple-element.18.spread_ref.refs_7_, f32[1024,128]{1,0:T(8,128)S(1)} %get-tuple-element.19.by_row_ref, ...), custom_call_target="tpu_custom_call" | custom-call | flops 1000000 | bytes 3000000 | tf_op jit(solution)/shard_map/far/pallas_call | solution.py:396
  16.6 0.0 collective-permute-done.1.got_ref
  16.6 0.7 %join.1 = f32[16,3,4,128]{3,2,1,0:T(4,128)} custom-call(f32[16,1,4,128]{3,2,1,0:T(4,128)S(1)} %far.1.far_ref, f32[16,2,4,128]{3,2,1,0:T(4,128)S(1)} %get-tuple-element.23.keep_ref, f32[16,2,4,128]{3,2,1,0:T(4,128)S(1)} %collective-permute-done.1.got_ref), custom_call_target="tpu_custom_call" | custom-call | tf_op jit(solution)/shard_map/join/pallas_call | solution.py:406
  17.3 3.5 %all-to-all-start.1 = ((f32[16,3,4,128]{3,2,1,0:T(4,128)}), f32[16,3,4,128]{3,2,1,0:T(4,128)S(1)}, u32[]{:S(2)}, u32[]{:S(2)}) async-start(f32[16,3,4,128]{3,2,1,0:T(4,128)} %join.1), calls=%async_computation.1 | async-start | bytes 196608 | tf_op jit(solution)/shard_map/all_to_all | solution.py:330
  20.8 0.3 %collective-permute-start.2 = (bf16[16,2,8,128]{3,2,1,0:T(8,128)(2,1)S(1)}, bf16[16,2,8,128]{3,2,1,0:T(8,128)(2,1)S(1)}, u32[]{:S(2)}, u32[]{:S(2)}) collective-permute-start(bf16[16,2,8,128]{3,2,1,0:T(8,128)(2,1)S(1)} %all-to-all-done.every_ref.refs_4_), channel_id=1, source_target_pairs={{0,1},{1,0},{2,3},{3,2},{4,5},{5,4},{6,7},{7,6},{8,9},{9,8},{10,11... | collective-permute-start | bytes 196616 | tf_op jit(solution)/shard_map/ppermute | solution.py:416
  21.1 1.0 %collective-permute-done.2.refs_5_ = bf16[16,2,8,128]{3,2,1,0:T(8,128)(2,1)S(1)} collective-permute-done((bf16[16,2,8,128]{3,2,1,0:T(8,128)(2,1)S(1)}, bf16[16,2,8,128]{3,2,1,0:T(8,128)(2,1)S(1)}, u32[]{:S(2)}, u32[]{:S(2)}) %collective-permute-start.2) | collective-permute-done | bytes 65568 | tf_op jit(solution)/shard_map/ppermute | solution.py:416
  22.1 3.3 %direct.1.refs_1_ = f32[4,8,128]{2,1,0:T(8,128)S(1)} custom-call(s32[1,96]{1,0:T(1,128)} %bitcast.6, s32[1,96]{1,0:T(1,128)} %bitcast.8, s32[1,96]{1,0:T(1,128)} %bitcast.10, bf16[96,128,128]{2,1,0:T(8,128)(2,1)} %refs_3_.4, bf16[16,2,8,128]{3,2,1,0:T(8,128)(2,1)S(1)} %all-to-all-done.every_ref.refs_4_, ...), custom_call_target="tpu_custom_call" | custom-call | flops 25165824 | bytes 10000000 | tf_op jit(solution)/shard_map/direct/pallas_call | solution.py:417
  25.5 0.3 %collective-permute-start.3 = (f32[4,8,128]{2,1,0:T(8,128)S(1)}, f32[4,8,128]{2,1,0:T(8,128)S(1)}, u32[]{:S(2)}, u32[]{:S(2)}) collective-permute-start(f32[4,8,128]{2,1,0:T(8,128)S(1)} %direct.1.refs_1_), channel_id=1, source_target_pairs={{0,1},{1,0},{2,3},{3,2},{4,5},{5,4},{6,7},{7,6},{8,9},{9,8},{10,11... | collective-permute-start | bytes 49160 | tf_op jit(solution)/shard_map/ppermute | solution.py:432
  25.8 0.9 %collective-permute-done.3.refs_2_ = f32[4,8,128]{2,1,0:T(8,128)S(1)} collective-permute-done((f32[4,8,128]{2,1,0:T(8,128)S(1)}, f32[4,8,128]{2,1,0:T(8,128)S(1)}, u32[]{:S(2)}, u32[]{:S(2)}) %collective-permute-start.3) | collective-permute-done | bytes 16416 | tf_op jit(solution)/shard_map/ppermute | solution.py:432
  26.7 1.1 %all-to-all-done.1.refs_0_ = f32[16,3,4,128]{3,2,1,0:T(4,128)S(1)} async-done(((f32[16,3,4,128]{3,2,1,0:T(4,128)}), f32[16,3,4,128]{3,2,1,0:T(4,128)S(1)}, u32[]{:S(2)}, u32[]{:S(2)}) %all-to-all-start.1) | async-done | bytes 98336 | tf_op jit(solution)/shard_map/all_to_all | solution.py:330
  27.8 0.0 copy-done
  27.8 0.8 %finish.1 = f32[8,256]{1,0:T(8,128)} custom-call(f32[16,3,4,128]{3,2,1,0:T(4,128)S(1)} %all-to-all-done.1.refs_0_, f32[4,8,128]{2,1,0:T(8,128)S(1)} %direct.1.refs_1_, f32[4,8,128]{2,1,0:T(8,128)S(1)} %collective-permute-done.3.refs_2_, bf16[2,32,128]{2,1,0:T(8,128)(2,1)S(1)} %copy-done), custom_call_target="tpu_custom_call" | custom-call | tf_op jit(solution)/shard_map/finish/pallas_call | solution.py:433
Async XLA Ops:
  1.6 14.0 %all-to-all-start = ((bf16[16,2,8,128]{3,2,1,0:T(8,128)(2,1)}), bf16[16,2,8,128]{3,2,1,0:T(8,128)(2,1)S(1)}, u32[]{:S(2)}, u32[]{:S(2)}) async-start(bf16[16,2,8,128]{3,2,1,0:T(8,128)(2,1)} %get-tuple-element.15), calls=%async_computation | async-start | bytes 131072 | tf_op jit(solution)/shard_map/all_to_all | solution.py:330
  9.0 1.9 %collective-permute-start = (bf16[8,256]{1,0:T(8,128)(2,1)S(1)}, bf16[8,256]{1,0:T(8,128)(2,1)S(1)}, u32[]{:S(2)}, u32[]{:S(2)}) collective-permute-start(bf16[8,256]{1,0:T(8,128)(2,1)S(1)} %get-tuple-element.22.refs_5_), channel_id=1, source_target_pairs={{0,1},{1,0},{2,3},{3,2},{4,5},{5,4},{6,7},{7,6},{8,9},{9,8},{10,11... | collective-permute-start | bytes 12296 | tf_op jit(solution)/shard_map/ppermute | solution.py:363
  12.8 14.9 %copy-start = (bf16[2,32,128]{2,1,0:T(8,128)(2,1)S(1)}, bf16[2,32,128]{2,1,0:T(8,128)(2,1)}, u32[]{:S(2)}) copy-start(bf16[2,32,128]{2,1,0:T(8,128)(2,1)} %refs_3_.5) | copy-start | bytes 49156
  12.8 3.8 %collective-permute-start.1 = (f32[16,2,4,128]{3,2,1,0:T(4,128)S(1)}, f32[16,2,4,128]{3,2,1,0:T(4,128)S(1)}, u32[]{:S(2)}, u32[]{:S(2)}) collective-permute-start(f32[16,2,4,128]{3,2,1,0:T(4,128)S(1)} %get-tuple-element.24), channel_id=1, source_target_pairs={{0,1},{1,0},{2,3},{3,2},{4,5},{5,4},{6,7},{7,6},{8,9},{9,8},{10,11... | collective-permute-start | bytes 196616 | tf_op jit(solution)/shard_map/ppermute | solution.py:395
  17.3 10.5 %all-to-all-start.1 = ((f32[16,3,4,128]{3,2,1,0:T(4,128)}), f32[16,3,4,128]{3,2,1,0:T(4,128)S(1)}, u32[]{:S(2)}, u32[]{:S(2)}) async-start(f32[16,3,4,128]{3,2,1,0:T(4,128)} %join.1), calls=%async_computation.1 | async-start | bytes 196608 | tf_op jit(solution)/shard_map/all_to_all | solution.py:330
  20.8 1.3 %collective-permute-start.2 = (bf16[16,2,8,128]{3,2,1,0:T(8,128)(2,1)S(1)}, bf16[16,2,8,128]{3,2,1,0:T(8,128)(2,1)S(1)}, u32[]{:S(2)}, u32[]{:S(2)}) collective-permute-start(bf16[16,2,8,128]{3,2,1,0:T(8,128)(2,1)S(1)} %all-to-all-done.every_ref.refs_4_), channel_id=1, source_target_pairs={{0,1},{1,0},{2,3},{3,2},{4,5},{5,4},{6,7},{7,6},{8,9},{9,8},{10,11... | collective-permute-start | bytes 196616 | tf_op jit(solution)/shard_map/ppermute | solution.py:416
  25.5 1.2 %collective-permute-start.3 = (f32[4,8,128]{2,1,0:T(8,128)S(1)}, f32[4,8,128]{2,1,0:T(8,128)S(1)}, u32[]{:S(2)}, u32[]{:S(2)}) collective-permute-start(f32[4,8,128]{2,1,0:T(8,128)S(1)} %direct.1.refs_1_), channel_id=1, source_target_pairs={{0,1},{1,0},{2,3},{3,2},{4,5},{5,4},{6,7},{7,6},{8,9},{9,8},{10,11... | collective-permute-start | bytes 49160 | tf_op jit(solution)/shard_map/ppermute | solution.py:432

commit v9 on v7

--- a/solution.py
+++ b/solution.py
@@ -213,7 +213,7 @@
     sides = 8
     rank = size // sides
 
-    lines = every_ref[:, 1].astype(f32).reshape(8 * devices, 128).astype(bf16)
+    lines = every_ref[:, 1].reshape(8 * devices, 128)
     moments = dot(lines, gather_ref[...], FIRST)
     for h in range(2):
         left_ref[h * 128 : (h + 1) * 128, :] = moments[:, h * count : (h + 1) * count]
@@ -306,7 +306,8 @@
         flat = jnp.concatenate([far[2 * k : 2 * k + 1], far[2 * k + 1 : 2 * k + 2]], axis=1)
         high, low = halves(jnp.where(mask, flat, 0.0))
         tiled = jnp.concatenate([basis_ref[k]] * sides, axis=0)
-        total = total + (dot(high, tiled, PLAIN) + dot(low, tiled, PLAIN))
+        both = dot(jnp.concatenate([high, low], axis=0), tiled, PLAIN)
+        total = total + (both[:sides] + both[sides:])
         out_ref[:, k * width : (k + 1) * width] = total
 
 
@@ -320,7 +321,7 @@
     pairs = near_blocks.shape[0]
     count = coupling.shape[0]
     swap = [(0, 1), (1, 0)]
-    params = pltpu.CompilerParams(vmem_limit_bytes=24 * 1024 * 1024)
+    params = pltpu.CompilerParams(vmem_limit_bytes=12 * 1024 * 1024)
 
     def shaped(shape, dtype):
         return jax.ShapeDtypeStruct(shape, dtype)

time: 28.9 us -> 28.9 us (level)
  no operation moved by 1% of the time
where the time goes in v9:
time: 28.9 us; the launch traced here: 28.5 us
  starting transfers between devices  12.3 us (43%)
  Pallas kernels  9.8 us (34%)
  waiting for transfers between devices  6.32 us (22%)
    all_to_all x2, starting transfers between devices, exchange(): lax.all_to_all(blocks, GROUP, split_axis=0, concat_axis=0, tiled=True)  10.9 us
    all_to_all x2, waiting for transfers between devices, exchange(): lax.all_to_all(blocks, GROUP, split_axis=0, concat_axis=0, tiled=True)  3.55 us
    pallas_call x1, Pallas kernels, shards(): pl.pallas_call(lambda *refs: direct_kernel(*refs, inner=inner), out_shape...  3.34 us
    pallas_call x1, Pallas kernels, shards(): pl.pallas_call(lambda *refs: mirror_kernel(*refs, inner=inner), out_shape...  1.99 us
    pallas_call x1, Pallas kernels, shards(): pl.pallas_call(lambda *refs: pack_kernel(*refs, inner=inner), out_shape=[...  1.6 us
    ppermute x1, waiting for transfers between devices, shards(): every_other = lax.ppermute(every, 'col', swap)  1.01 us
    pallas_call x1, Pallas kernels, shards(): pl.pallas_call(far_kernel, out_shape=shaped((devices, 1, 4, 128), f32), i...  0.99 us
    ppermute x1, waiting for transfers between devices, shards(): others = lax.ppermute(direct, 'col', swap)  0.93 us
  transfers between devices with their start and end apart: 6, of which 5 were waited for; matrix products, arithmetic and copies ran while one was open for 0% of the time, Pallas kernels for 24%

profile of v9, /device:TPU:0, one launch (start us, length us, event | category | flops | bytes accessed | tf_op | source)
XLA Modules:
  0.0 28.5 jit_solution(7590484205120169739)
XLA Ops:
  0.0 1.6 %pack.1 = (bf16[16,2,8,128]{3,2,1,0:T(8,128)(2,1)}, bf16[8,256]{1,0:T(8,128)(2,1)S(1)}, s32[2,1,128]{2,1,0:T(1,128)S(1)}, bf16[128,1024]{1,0:T(8,128)(2,1)S(1)}, bf16[48,128,128]{2,1,0:T(8,128)(2,1)S(1)}) custom-call(bf16[8,256]{1,0:T(8,128)(2,1)} %refs_0_.1, bf16[2,32,128]{2,1,0:T(8,128)(2,1)} %refs_3_.5, s32[1,128]{1,0:T(1,128)} %bitcast.11, ...), custom_call_target="tpu_custom_call" | custom-call | tf_op jit(solution)/shard_map/pack/pallas_call | solution.py:343
  1.6 7.4 %all-to-all-start = ((bf16[16,2,8,128]{3,2,1,0:T(8,128)(2,1)}), bf16[16,2,8,128]{3,2,1,0:T(8,128)(2,1)S(1)}, u32[]{:S(2)}, u32[]{:S(2)}) async-start(bf16[16,2,8,128]{3,2,1,0:T(8,128)(2,1)} %get-tuple-element.16), calls=%async_computation | async-start | bytes 131072 | tf_op jit(solution)/shard_map/all_to_all | solution.py:330
  9.0 0.4 %collective-permute-start = (bf16[8,256]{1,0:T(8,128)(2,1)S(1)}, bf16[8,256]{1,0:T(8,128)(2,1)S(1)}, u32[]{:S(2)}, u32[]{:S(2)}) collective-permute-start(bf16[8,256]{1,0:T(8,128)(2,1)S(1)} %get-tuple-element.24.refs_5_), channel_id=1, source_target_pairs={{0,1},{1,0},{2,3},{3,2},{4,5},{5,4},{6,7},{7,6},{8,9},{9,8},{10,11... | collective-permute-start | bytes 12296 | tf_op jit(solution)/shard_map/ppermute | solution.py:364
  9.4 0.8 %collective-permute-done.refs_6_ = bf16[8,256]{1,0:T(8,128)(2,1)S(1)} collective-permute-done((bf16[8,256]{1,0:T(8,128)(2,1)S(1)}, bf16[8,256]{1,0:T(8,128)(2,1)S(1)}, u32[]{:S(2)}, u32[]{:S(2)}) %collective-permute-start) | collective-permute-done | bytes 4128 | tf_op jit(solution)/shard_map/ppermute | solution.py:364
  10.2 2.0 %mirror.1 = (f32[16,2,4,128]{3,2,1,0:T(4,128)S(1)}, f32[16,2,4,128]{3,2,1,0:T(4,128)S(1)}) custom-call(s32[1,96]{1,0:T(1,128)} %bitcast.5, s32[1,96]{1,0:T(1,128)} %bitcast.7, s32[1,96]{1,0:T(1,128)} %bitcast.9, bf16[96,128,128]{2,1,0:T(8,128)(2,1)} %refs_3_.4, bf16[48,128,128]{2,1,0:T(8,128)(2,1)S(1)} %get-tuple-element.23.refs_4_, ...), custom_call_target="tpu_custom_call" | custom-call | flops 25165824 | bytes 10000000 | tf_op jit(solution)/shard_map/mirror/pallas_call | solution.py:379
  12.2 0.0 copy-start
  12.2 0.4 %collective-permute-start.1 = (f32[16,2,4,128]{3,2,1,0:T(4,128)S(1)}, f32[16,2,4,128]{3,2,1,0:T(4,128)S(1)}, u32[]{:S(2)}, u32[]{:S(2)}) collective-permute-start(f32[16,2,4,128]{3,2,1,0:T(4,128)S(1)} %get-tuple-element.26), channel_id=1, source_target_pairs={{0,1},{1,0},{2,3},{3,2},{4,5},{5,4},{6,7},{7,6},{8,9},{9,8},{10,11... | collective-permute-start | bytes 196616 | tf_op jit(solution)/shard_map/ppermute | solution.py:395
  12.7 0.5 %turn.1 = (f32[1024,128]{1,0:T(8,128)S(1)}, f32[1024,128]{1,0:T(8,128)S(1)}, bf16[128,512]{1,0:T(8,128)(2,1)S(1)}, bf16[512,64]{1,0:T(8,128)(2,1)S(1)}) custom-call(s32[2,1,128]{2,1,0:T(1,128)S(1)} %get-tuple-element.17.refs_0_, bf16[128,1024]{1,0:T(8,128)(2,1)S(1)} %get-tuple-element.18.refs_1_), custom_call_target="tpu_custom_call" | custom-call | flops 1000000 | bytes 3000000 | tf_op jit(solution)/shard_map/turn/pallas_call | solution.py:365
  13.1 2.5 %all-to-all-done.every_ref.refs_4_ = bf16[16,2,8,128]{3,2,1,0:T(8,128)(2,1)S(1)} async-done(((bf16[16,2,8,128]{3,2,1,0:T(8,128)(2,1)}), bf16[16,2,8,128]{3,2,1,0:T(8,128)(2,1)S(1)}, u32[]{:S(2)}, u32[]{:S(2)}) %all-to-all-start) | async-done | bytes 65568 | tf_op jit(solution)/shard_map/all_to_all | solution.py:330
  15.6 1.0 %far.1.far_ref = f32[16,1,4,128]{3,2,1,0:T(4,128)S(1)} custom-call(bf16[16,2,8,128]{3,2,1,0:T(8,128)(2,1)S(1)} %all-to-all-done.every_ref.refs_4_, bf16[128,512]{1,0:T(8,128)(2,1)S(1)} %get-tuple-element.19.gather_ref, bf16[512,64]{1,0:T(8,128)(2,1)S(1)} %get-tuple-element.20.spread_ref, f32[1024,128]{1,0:T(8,128)S(1)} %get-tuple-element.21.by_row_ref, ...), custom_call_target="tpu_custom_call" | custom-call | flops 1000000 | bytes 3000000 | tf_op jit(solution)/shard_map/far/pallas_call | solution.py:396
  16.6 0.0 collective-permute-done.1.got_ref
  16.6 0.7 %join.1 = f32[16,3,4,128]{3,2,1,0:T(4,128)} custom-call(f32[16,1,4,128]{3,2,1,0:T(4,128)S(1)} %far.1.far_ref, f32[16,2,4,128]{3,2,1,0:T(4,128)S(1)} %get-tuple-element.25.keep_ref, f32[16,2,4,128]{3,2,1,0:T(4,128)S(1)} %collective-permute-done.1.got_ref), custom_call_target="tpu_custom_call" | custom-call | tf_op jit(solution)/shard_map/join/pallas_call | solution.py:406
  17.3 3.5 %all-to-all-start.1 = ((f32[16,3,4,128]{3,2,1,0:T(4,128)}), f32[16,3,4,128]{3,2,1,0:T(4,128)S(1)}, u32[]{:S(2)}, u32[]{:S(2)}) async-start(f32[16,3,4,128]{3,2,1,0:T(4,128)} %join.1), calls=%async_computation.1 | async-start | bytes 196608 | tf_op jit(solution)/shard_map/all_to_all | solution.py:330
  20.8 0.3 %collective-permute-start.2 = (bf16[16,2,8,128]{3,2,1,0:T(8,128)(2,1)S(1)}, bf16[16,2,8,128]{3,2,1,0:T(8,128)(2,1)S(1)}, u32[]{:S(2)}, u32[]{:S(2)}) collective-permute-start(bf16[16,2,8,128]{3,2,1,0:T(8,128)(2,1)S(1)} %all-to-all-done.every_ref.refs_4_), channel_id=1, source_target_pairs={{0,1},{1,0},{2,3},{3,2},{4,5},{5,4},{6,7},{7,6},{8,9},{9,8},{10,11... | collective-permute-start | bytes 196616 | tf_op jit(solution)/shard_map/ppermute | solution.py:416
  21.1 1.0 %collective-permute-done.2.refs_5_ = bf16[16,2,8,128]{3,2,1,0:T(8,128)(2,1)S(1)} collective-permute-done((bf16[16,2,8,128]{3,2,1,0:T(8,128)(2,1)S(1)}, bf16[16,2,8,128]{3,2,1,0:T(8,128)(2,1)S(1)}, u32[]{:S(2)}, u32[]{:S(2)}) %collective-permute-start.2) | collective-permute-done | bytes 65568 | tf_op jit(solution)/shard_map/ppermute | solution.py:416
  22.2 3.3 %direct.1.refs_1_ = f32[4,8,128]{2,1,0:T(8,128)S(1)} custom-call(s32[1,96]{1,0:T(1,128)} %bitcast.6, s32[1,96]{1,0:T(1,128)} %bitcast.8, s32[1,96]{1,0:T(1,128)} %bitcast.10, bf16[96,128,128]{2,1,0:T(8,128)(2,1)} %refs_3_.4, bf16[16,2,8,128]{3,2,1,0:T(8,128)(2,1)S(1)} %all-to-all-done.every_ref.refs_4_, ...), custom_call_target="tpu_custom_call" | custom-call | flops 25165824 | bytes 10000000 | tf_op jit(solution)/shard_map/direct/pallas_call | solution.py:417
  25.5 0.3 %collective-permute-start.3 = (f32[4,8,128]{2,1,0:T(8,128)S(1)}, f32[4,8,128]{2,1,0:T(8,128)S(1)}, u32[]{:S(2)}, u32[]{:S(2)}) collective-permute-start(f32[4,8,128]{2,1,0:T(8,128)S(1)} %direct.1.refs_1_), channel_id=1, source_target_pairs={{0,1},{1,0},{2,3},{3,2},{4,5},{5,4},{6,7},{7,6},{8,9},{9,8},{10,11... | collective-permute-start | bytes 49160 | tf_op jit(solution)/shard_map/ppermute | solution.py:432
  25.8 0.9 %collective-permute-done.3.refs_2_ = f32[4,8,128]{2,1,0:T(8,128)S(1)} collective-permute-done((f32[4,8,128]{2,1,0:T(8,128)S(1)}, f32[4,8,128]{2,1,0:T(8,128)S(1)}, u32[]{:S(2)}, u32[]{:S(2)}) %collective-permute-start.3) | collective-permute-done | bytes 16416 | tf_op jit(solution)/shard_map/ppermute | solution.py:432
  26.8 1.1 %all-to-all-done.1.refs_0_ = f32[16,3,4,128]{3,2,1,0:T(4,128)S(1)} async-done(((f32[16,3,4,128]{3,2,1,0:T(4,128)}), f32[16,3,4,128]{3,2,1,0:T(4,128)S(1)}, u32[]{:S(2)}, u32[]{:S(2)}) %all-to-all-start.1) | async-done | bytes 98336 | tf_op jit(solution)/shard_map/all_to_all | solution.py:330
  27.8 0.0 copy-done
  27.8 0.7 %finish.1 = f32[8,256]{1,0:T(8,128)} custom-call(f32[16,3,4,128]{3,2,1,0:T(4,128)S(1)} %all-to-all-done.1.refs_0_, f32[4,8,128]{2,1,0:T(8,128)S(1)} %direct.1.refs_1_, f32[4,8,128]{2,1,0:T(8,128)S(1)} %collective-permute-done.3.refs_2_, bf16[2,32,128]{2,1,0:T(8,128)(2,1)S(1)} %copy-done), custom_call_target="tpu_custom_call" | custom-call | tf_op jit(solution)/shard_map/finish/pallas_call | solution.py:433
Async XLA Ops:
  1.6 14.0 %all-to-all-start = ((bf16[16,2,8,128]{3,2,1,0:T(8,128)(2,1)}), bf16[16,2,8,128]{3,2,1,0:T(8,128)(2,1)S(1)}, u32[]{:S(2)}, u32[]{:S(2)}) async-start(bf16[16,2,8,128]{3,2,1,0:T(8,128)(2,1)} %get-tuple-element.16), calls=%async_computation | async-start | bytes 131072 | tf_op jit(solution)/shard_map/all_to_all | solution.py:330
  9.0 1.2 %collective-permute-start = (bf16[8,256]{1,0:T(8,128)(2,1)S(1)}, bf16[8,256]{1,0:T(8,128)(2,1)S(1)}, u32[]{:S(2)}, u32[]{:S(2)}) collective-permute-start(bf16[8,256]{1,0:T(8,128)(2,1)S(1)} %get-tuple-element.24.refs_5_), channel_id=1, source_target_pairs={{0,1},{1,0},{2,3},{3,2},{4,5},{5,4},{6,7},{7,6},{8,9},{9,8},{10,11... | collective-permute-start | bytes 12296 | tf_op jit(solution)/shard_map/ppermute | solution.py:364
  12.2 15.6 %copy-start = (bf16[2,32,128]{2,1,0:T(8,128)(2,1)S(1)}, bf16[2,32,128]{2,1,0:T(8,128)(2,1)}, u32[]{:S(2)}) copy-start(bf16[2,32,128]{2,1,0:T(8,128)(2,1)} %refs_3_.5) | copy-start | bytes 49156
  12.2 4.4 %collective-permute-start.1 = (f32[16,2,4,128]{3,2,1,0:T(4,128)S(1)}, f32[16,2,4,128]{3,2,1,0:T(4,128)S(1)}, u32[]{:S(2)}, u32[]{:S(2)}) collective-permute-start(f32[16,2,4,128]{3,2,1,0:T(4,128)S(1)} %get-tuple-element.26), channel_id=1, source_target_pairs={{0,1},{1,0},{2,3},{3,2},{4,5},{5,4},{6,7},{7,6},{8,9},{9,8},{10,11... | collective-permute-start | bytes 196616 | tf_op jit(solution)/shard_map/ppermute | solution.py:395
  17.3 10.5 %all-to-all-start.1 = ((f32[16,3,4,128]{3,2,1,0:T(4,128)}), f32[16,3,4,128]{3,2,1,0:T(4,128)S(1)}, u32[]{:S(2)}, u32[]{:S(2)}) async-start(f32[16,3,4,128]{3,2,1,0:T(4,128)} %join.1), calls=%async_computation.1 | async-start | bytes 196608 | tf_op jit(solution)/shard_map/all_to_all | solution.py:330
  20.8 1.3 %collective-permute-start.2 = (bf16[16,2,8,128]{3,2,1,0:T(8,128)(2,1)S(1)}, bf16[16,2,8,128]{3,2,1,0:T(8,128)(2,1)S(1)}, u32[]{:S(2)}, u32[]{:S(2)}) collective-permute-start(bf16[16,2,8,128]{3,2,1,0:T(8,128)(2,1)S(1)} %all-to-all-done.every_ref.refs_4_), channel_id=1, source_target_pairs={{0,1},{1,0},{2,3},{3,2},{4,5},{5,4},{6,7},{7,6},{8,9},{9,8},{10,11... | collective-permute-start | bytes 196616 | tf_op jit(solution)/shard_map/ppermute | solution.py:416
  25.5 1.2 %collective-permute-start.3 = (f32[4,8,128]{2,1,0:T(8,128)S(1)}, f32[4,8,128]{2,1,0:T(8,128)S(1)}, u32[]{:S(2)}, u32[]{:S(2)}) collective-permute-start(f32[4,8,128]{2,1,0:T(8,128)S(1)} %direct.1.refs_1_), channel_id=1, source_target_pairs={{0,1},{1,0},{2,3},{3,2},{4,5},{5,4},{6,7},{7,6},{8,9},{9,8},{10,11... | collective-permute-start | bytes 49160 | tf_op jit(solution)/shard_map/ppermute | solution.py:432

commit v10 on v7

--- a/solution.py
+++ b/solution.py
@@ -14,7 +14,7 @@
 VMEM = pl.BlockSpec(memory_space=pltpu.VMEM)
 EARLY, LATER = 1, 1
 UNROLL = 48
-GROUP = ("x", "col", "z")
+GROUP = ('w', 'x', 'col', 'z')
 
 
 def dot(left, right, dims):
@@ -47,9 +47,12 @@
 
 
 def slot_of(cluster, inner):
-    depth, width = inner
+    depth, _, width, depth_z, depth_w = inner
     device = cluster >> 1
-    return lax.rem(device, 2 * width) * depth + lax.div(device, 2 * width)
+    c, device = device & 1, device >> 1
+    x, device = lax.rem(device, width), lax.div(device, width)
+    z, w = lax.rem(device, depth_z), lax.div(device, depth_z)
+    return (((w) * width + x) * 2 + c) * depth + (z)
 
 
 def each(count, body):
@@ -312,7 +315,7 @@
 
 def shards(cells, basis_t, near_blocks, near_owner, near_col, near_row, far_row, far_col, coupling):
     depth = lax.axis_size("z")
-    inner = (depth, lax.axis_size("x"))
+    inner = (depth, lax.axis_size("w") * lax.axis_size("x"), lax.axis_size("x"), lax.axis_size("z"), lax.axis_size("w"))
     devices = 2 * depth * inner[1]
     sides, lanes = cells.shape
     owned, rank, width = basis_t.shape
@@ -442,8 +445,9 @@
 def solution(mesh):
     parts, rows, cols = mesh.devices.shape
     x = 2 if rows % 2 == 0 else 1
-    mesh = Mesh(mesh.devices.reshape(parts, rows // x, x, cols), ("parts", "z", "x", "col"))
-    split = ("parts", "z", "x", "col")
+    w = 2 if rows // x % 2 == 0 else 1
+    mesh = Mesh(mesh.devices.reshape(parts, w, rows // x // w, x, cols), ("parts", "w", "z", "x", "col"))
+    split = ("parts", "w", "z", "x", "col")
     return jax.shard_map(
         shards,
         mesh=mesh,

time: 28.9 us -> 28.9 us (level)
  no operation moved by 1% of the time
where the time goes in v10:
time: 28.9 us; the launch traced here: 28.6 us
  starting transfers between devices  12.3 us (43%)
  Pallas kernels  9.85 us (34%)
  waiting for transfers between devices  6.32 us (22%)
    all_to_all x2, starting transfers between devices, exchange(): lax.all_to_all(blocks, GROUP, split_axis=0, concat_axis=0, tiled=True)  10.9 us
    all_to_all x2, waiting for transfers between devices, exchange(): lax.all_to_all(blocks, GROUP, split_axis=0, concat_axis=0, tiled=True)  3.52 us
    pallas_call x1, Pallas kernels, shards(): pl.pallas_call(lambda *refs: direct_kernel(*refs, inner=inner), out_shape...  3.35 us
    pallas_call x1, Pallas kernels, shards(): pl.pallas_call(lambda *refs: mirror_kernel(*refs, inner=inner), out_shape...  2.01 us
    pallas_call x1, Pallas kernels, shards(): pl.pallas_call(lambda *refs: pack_kernel(*refs, inner=inner), out_shape=[...  1.6 us
    ppermute x1, waiting for transfers between devices, shards(): every_other = lax.ppermute(every, 'col', swap)  1.02 us
    pallas_call x1, Pallas kernels, shards(): pl.pallas_call(far_kernel, out_shape=shaped((devices, 1, 4, 128), f32), i...  0.99 us
    ppermute x1, waiting for transfers between devices, shards(): others = lax.ppermute(direct, 'col', swap)  0.96 us
  transfers between devices with their start and end apart: 6, of which 5 were waited for; matrix products, arithmetic and copies ran while one was open for 0% of the time, Pallas kernels for 24%

profile of v10, /device:TPU:0, one launch (start us, length us, event | category | flops | bytes accessed | tf_op | source)
XLA Modules:
  0.0 28.6 jit_solution(10598863038014574017)
XLA Ops:
  0.0 1.6 %pack.1 = (bf16[16,2,8,128]{3,2,1,0:T(8,128)(2,1)}, bf16[8,256]{1,0:T(8,128)(2,1)S(1)}, s32[2,1,128]{2,1,0:T(1,128)S(1)}, bf16[128,1024]{1,0:T(8,128)(2,1)S(1)}, bf16[48,128,128]{2,1,0:T(8,128)(2,1)S(1)}) custom-call(bf16[8,256]{1,0:T(8,128)(2,1)} %refs_0_.1, bf16[2,32,128]{2,1,0:T(8,128)(2,1)} %refs_3_.5, s32[1,128]{1,0:T(1,128)} %bitcast.11, ...), custom_call_target="tpu_custom_call" | custom-call | tf_op jit(solution)/shard_map/pack/pallas_call | solution.py:345
  1.6 7.4 %all-to-all-start = ((bf16[16,2,8,128]{3,2,1,0:T(8,128)(2,1)}), bf16[16,2,8,128]{3,2,1,0:T(8,128)(2,1)S(1)}, u32[]{:S(2)}, u32[]{:S(2)}) async-start(bf16[16,2,8,128]{3,2,1,0:T(8,128)(2,1)} %get-tuple-element.16), calls=%async_computation | async-start | bytes 131072 | tf_op jit(solution)/shard_map/all_to_all | solution.py:332
  9.0 0.4 %collective-permute-start = (bf16[8,256]{1,0:T(8,128)(2,1)S(1)}, bf16[8,256]{1,0:T(8,128)(2,1)S(1)}, u32[]{:S(2)}, u32[]{:S(2)}) collective-permute-start(bf16[8,256]{1,0:T(8,128)(2,1)S(1)} %get-tuple-element.24.refs_5_), channel_id=1, source_target_pairs={{0,1},{1,0},{2,3},{3,2},{4,5},{5,4},{6,7},{7,6},{8,9},{9,8},{10,11... | collective-permute-start | bytes 12296 | tf_op jit(solution)/shard_map/ppermute | solution.py:366
  9.4 0.8 %collective-permute-done.refs_6_ = bf16[8,256]{1,0:T(8,128)(2,1)S(1)} collective-permute-done((bf16[8,256]{1,0:T(8,128)(2,1)S(1)}, bf16[8,256]{1,0:T(8,128)(2,1)S(1)}, u32[]{:S(2)}, u32[]{:S(2)}) %collective-permute-start) | collective-permute-done | bytes 4128 | tf_op jit(solution)/shard_map/ppermute | solution.py:366
  10.2 2.0 %mirror.1 = (f32[16,2,4,128]{3,2,1,0:T(4,128)S(1)}, f32[16,2,4,128]{3,2,1,0:T(4,128)S(1)}) custom-call(s32[1,96]{1,0:T(1,128)} %bitcast.5, s32[1,96]{1,0:T(1,128)} %bitcast.7, s32[1,96]{1,0:T(1,128)} %bitcast.9, bf16[96,128,128]{2,1,0:T(8,128)(2,1)} %refs_3_.4, bf16[48,128,128]{2,1,0:T(8,128)(2,1)S(1)} %get-tuple-element.23.refs_4_, ...), custom_call_target="tpu_custom_call" | custom-call | flops 25165824 | bytes 10000000 | tf_op jit(solution)/shard_map/mirror/pallas_call | solution.py:381
  12.2 0.0 copy-start
  12.3 0.4 %collective-permute-start.1 = (f32[16,2,4,128]{3,2,1,0:T(4,128)S(1)}, f32[16,2,4,128]{3,2,1,0:T(4,128)S(1)}, u32[]{:S(2)}, u32[]{:S(2)}) collective-permute-start(f32[16,2,4,128]{3,2,1,0:T(4,128)S(1)} %get-tuple-element.26), channel_id=1, source_target_pairs={{0,1},{1,0},{2,3},{3,2},{4,5},{5,4},{6,7},{7,6},{8,9},{9,8},{10,11... | collective-permute-start | bytes 196616 | tf_op jit(solution)/shard_map/ppermute | solution.py:397
  12.7 0.5 %turn.1 = (f32[1024,128]{1,0:T(8,128)S(1)}, f32[1024,128]{1,0:T(8,128)S(1)}, bf16[128,512]{1,0:T(8,128)(2,1)S(1)}, bf16[512,64]{1,0:T(8,128)(2,1)S(1)}) custom-call(s32[2,1,128]{2,1,0:T(1,128)S(1)} %get-tuple-element.17.refs_0_, bf16[128,1024]{1,0:T(8,128)(2,1)S(1)} %get-tuple-element.18.refs_1_), custom_call_target="tpu_custom_call" | custom-call | flops 1000000 | bytes 3000000 | tf_op jit(solution)/shard_map/turn/pallas_call | solution.py:367
  13.1 2.5 %all-to-all-done.every_ref.refs_4_ = bf16[16,2,8,128]{3,2,1,0:T(8,128)(2,1)S(1)} async-done(((bf16[16,2,8,128]{3,2,1,0:T(8,128)(2,1)}), bf16[16,2,8,128]{3,2,1,0:T(8,128)(2,1)S(1)}, u32[]{:S(2)}, u32[]{:S(2)}) %all-to-all-start) | async-done | bytes 65568 | tf_op jit(solution)/shard_map/all_to_all | solution.py:332
  15.6 1.0 %far.1.far_ref = f32[16,1,4,128]{3,2,1,0:T(4,128)S(1)} custom-call(bf16[16,2,8,128]{3,2,1,0:T(8,128)(2,1)S(1)} %all-to-all-done.every_ref.refs_4_, bf16[128,512]{1,0:T(8,128)(2,1)S(1)} %get-tuple-element.19.gather_ref, bf16[512,64]{1,0:T(8,128)(2,1)S(1)} %get-tuple-element.20.spread_ref, f32[1024,128]{1,0:T(8,128)S(1)} %get-tuple-element.21.by_row_ref, ...), custom_call_target="tpu_custom_call" | custom-call | flops 1000000 | bytes 3000000 | tf_op jit(solution)/shard_map/far/pallas_call | solution.py:398
  16.6 0.0 collective-permute-done.1.got_ref
  16.6 0.7 %join.1 = f32[16,3,4,128]{3,2,1,0:T(4,128)} custom-call(f32[16,1,4,128]{3,2,1,0:T(4,128)S(1)} %far.1.far_ref, f32[16,2,4,128]{3,2,1,0:T(4,128)S(1)} %get-tuple-element.25.keep_ref, f32[16,2,4,128]{3,2,1,0:T(4,128)S(1)} %collective-permute-done.1.got_ref), custom_call_target="tpu_custom_call" | custom-call | tf_op jit(solution)/shard_map/join/pallas_call | solution.py:408
  17.3 3.5 %all-to-all-start.1 = ((f32[16,3,4,128]{3,2,1,0:T(4,128)}), f32[16,3,4,128]{3,2,1,0:T(4,128)S(1)}, u32[]{:S(2)}, u32[]{:S(2)}) async-start(f32[16,3,4,128]{3,2,1,0:T(4,128)} %join.1), calls=%async_computation.1 | async-start | bytes 196608 | tf_op jit(solution)/shard_map/all_to_all | solution.py:332
  20.8 0.3 %collective-permute-start.2 = (bf16[16,2,8,128]{3,2,1,0:T(8,128)(2,1)S(1)}, bf16[16,2,8,128]{3,2,1,0:T(8,128)(2,1)S(1)}, u32[]{:S(2)}, u32[]{:S(2)}) collective-permute-start(bf16[16,2,8,128]{3,2,1,0:T(8,128)(2,1)S(1)} %all-to-all-done.every_ref.refs_4_), channel_id=1, source_target_pairs={{0,1},{1,0},{2,3},{3,2},{4,5},{5,4},{6,7},{7,6},{8,9},{9,8},{10,11... | collective-permute-start | bytes 196616 | tf_op jit(solution)/shard_map/ppermute | solution.py:418
  21.1 1.0 %collective-permute-done.2.refs_5_ = bf16[16,2,8,128]{3,2,1,0:T(8,128)(2,1)S(1)} collective-permute-done((bf16[16,2,8,128]{3,2,1,0:T(8,128)(2,1)S(1)}, bf16[16,2,8,128]{3,2,1,0:T(8,128)(2,1)S(1)}, u32[]{:S(2)}, u32[]{:S(2)}) %collective-permute-start.2) | collective-permute-done | bytes 65568 | tf_op jit(solution)/shard_map/ppermute | solution.py:418
  22.2 3.4 %direct.1.refs_1_ = f32[4,8,128]{2,1,0:T(8,128)S(1)} custom-call(s32[1,96]{1,0:T(1,128)} %bitcast.6, s32[1,96]{1,0:T(1,128)} %bitcast.8, s32[1,96]{1,0:T(1,128)} %bitcast.10, bf16[96,128,128]{2,1,0:T(8,128)(2,1)} %refs_3_.4, bf16[16,2,8,128]{3,2,1,0:T(8,128)(2,1)S(1)} %all-to-all-done.every_ref.refs_4_, ...), custom_call_target="tpu_custom_call" | custom-call | flops 25165824 | bytes 10000000 | tf_op jit(solution)/shard_map/direct/pallas_call | solution.py:419
  25.5 0.3 %collective-permute-start.3 = (f32[4,8,128]{2,1,0:T(8,128)S(1)}, f32[4,8,128]{2,1,0:T(8,128)S(1)}, u32[]{:S(2)}, u32[]{:S(2)}) collective-permute-start(f32[4,8,128]{2,1,0:T(8,128)S(1)} %direct.1.refs_1_), channel_id=1, source_target_pairs={{0,1},{1,0},{2,3},{3,2},{4,5},{5,4},{6,7},{7,6},{8,9},{9,8},{10,11... | collective-permute-start | bytes 49160 | tf_op jit(solution)/shard_map/ppermute | solution.py:434
  25.8 1.0 %collective-permute-done.3.refs_2_ = f32[4,8,128]{2,1,0:T(8,128)S(1)} collective-permute-done((f32[4,8,128]{2,1,0:T(8,128)S(1)}, f32[4,8,128]{2,1,0:T(8,128)S(1)}, u32[]{:S(2)}, u32[]{:S(2)}) %collective-permute-start.3) | collective-permute-done | bytes 16416 | tf_op jit(solution)/shard_map/ppermute | solution.py:434
  26.8 1.0 %all-to-all-done.1.refs_0_ = f32[16,3,4,128]{3,2,1,0:T(4,128)S(1)} async-done(((f32[16,3,4,128]{3,2,1,0:T(4,128)}), f32[16,3,4,128]{3,2,1,0:T(4,128)S(1)}, u32[]{:S(2)}, u32[]{:S(2)}) %all-to-all-start.1) | async-done | bytes 98336 | tf_op jit(solution)/shard_map/all_to_all | solution.py:332
  27.8 0.0 copy-done
  27.8 0.8 %finish.1 = f32[8,256]{1,0:T(8,128)} custom-call(f32[16,3,4,128]{3,2,1,0:T(4,128)S(1)} %all-to-all-done.1.refs_0_, f32[4,8,128]{2,1,0:T(8,128)S(1)} %direct.1.refs_1_, f32[4,8,128]{2,1,0:T(8,128)S(1)} %collective-permute-done.3.refs_2_, bf16[2,32,128]{2,1,0:T(8,128)(2,1)S(1)} %copy-done), custom_call_target="tpu_custom_call" | custom-call | tf_op jit(solution)/shard_map/finish/pallas_call | solution.py:435
Async XLA Ops:
  1.6 14.0 %all-to-all-start = ((bf16[16,2,8,128]{3,2,1,0:T(8,128)(2,1)}), bf16[16,2,8,128]{3,2,1,0:T(8,128)(2,1)S(1)}, u32[]{:S(2)}, u32[]{:S(2)}) async-start(bf16[16,2,8,128]{3,2,1,0:T(8,128)(2,1)} %get-tuple-element.16), calls=%async_computation | async-start | bytes 131072 | tf_op jit(solution)/shard_map/all_to_all | solution.py:332
  9.0 1.2 %collective-permute-start = (bf16[8,256]{1,0:T(8,128)(2,1)S(1)}, bf16[8,256]{1,0:T(8,128)(2,1)S(1)}, u32[]{:S(2)}, u32[]{:S(2)}) collective-permute-start(bf16[8,256]{1,0:T(8,128)(2,1)S(1)} %get-tuple-element.24.refs_5_), channel_id=1, source_target_pairs={{0,1},{1,0},{2,3},{3,2},{4,5},{5,4},{6,7},{7,6},{8,9},{9,8},{10,11... | collective-permute-start | bytes 12296 | tf_op jit(solution)/shard_map/ppermute | solution.py:366
  12.2 15.6 %copy-start = (bf16[2,32,128]{2,1,0:T(8,128)(2,1)S(1)}, bf16[2,32,128]{2,1,0:T(8,128)(2,1)}, u32[]{:S(2)}) copy-start(bf16[2,32,128]{2,1,0:T(8,128)(2,1)} %refs_3_.5) | copy-start | bytes 49156
  12.3 4.4 %collective-permute-start.1 = (f32[16,2,4,128]{3,2,1,0:T(4,128)S(1)}, f32[16,2,4,128]{3,2,1,0:T(4,128)S(1)}, u32[]{:S(2)}, u32[]{:S(2)}) collective-permute-start(f32[16,2,4,128]{3,2,1,0:T(4,128)S(1)} %get-tuple-element.26), channel_id=1, source_target_pairs={{0,1},{1,0},{2,3},{3,2},{4,5},{5,4},{6,7},{7,6},{8,9},{9,8},{10,11... | collective-permute-start | bytes 196616 | tf_op jit(solution)/shard_map/ppermute | solution.py:397
  17.3 10.5 %all-to-all-start.1 = ((f32[16,3,4,128]{3,2,1,0:T(4,128)}), f32[16,3,4,128]{3,2,1,0:T(4,128)S(1)}, u32[]{:S(2)}, u32[]{:S(2)}) async-start(f32[16,3,4,128]{3,2,1,0:T(4,128)} %join.1), calls=%async_computation.1 | async-start | bytes 196608 | tf_op jit(solution)/shard_map/all_to_all | solution.py:332
  20.8 1.3 %collective-permute-start.2 = (bf16[16,2,8,128]{3,2,1,0:T(8,128)(2,1)S(1)}, bf16[16,2,8,128]{3,2,1,0:T(8,128)(2,1)S(1)}, u32[]{:S(2)}, u32[]{:S(2)}) collective-permute-start(bf16[16,2,8,128]{3,2,1,0:T(8,128)(2,1)S(1)} %all-to-all-done.every_ref.refs_4_), channel_id=1, source_target_pairs={{0,1},{1,0},{2,3},{3,2},{4,5},{5,4},{6,7},{7,6},{8,9},{9,8},{10,11... | collective-permute-start | bytes 196616 | tf_op jit(solution)/shard_map/ppermute | solution.py:418
  25.5 1.2 %collective-permute-start.3 = (f32[4,8,128]{2,1,0:T(8,128)S(1)}, f32[4,8,128]{2,1,0:T(8,128)S(1)}, u32[]{:S(2)}, u32[]{:S(2)}) collective-permute-start(f32[4,8,128]{2,1,0:T(8,128)S(1)} %direct.1.refs_1_), channel_id=1, source_target_pairs={{0,1},{1,0},{2,3},{3,2},{4,5},{5,4},{6,7},{7,6},{8,9},{9,8},{10,11... | collective-permute-start | bytes 49160 | tf_op jit(solution)/shard_map/ppermute | solution.py:434

commit v11 on v7

--- a/solution.py
+++ b/solution.py
@@ -36,9 +36,9 @@
     return lane // rank == row
 
 
-def start(source, target, sem):
+def start(source, target, sem, priority=0):
     copy = pltpu.make_async_copy(source, target, sem)
-    copy.start()
+    copy.start(priority=priority)
     return copy
 
 
@@ -72,8 +72,8 @@
     ahead = [
         start(first_hbm, far_ref.at[0], sems.at[2]),
         start(second_hbm, far_ref.at[1], sems.at[3]),
-        start(coupling_hbm, coupling_ref, sems.at[4]),
-        start(blocks_hbm.at[pl.ds(0, early_ref.shape[0])], early_ref, sems.at[5]),
+        start(coupling_hbm, coupling_ref, sems.at[4], 1),
+        start(blocks_hbm.at[pl.ds(0, early_ref.shape[0])], early_ref, sems.at[5], 1),
     ]
     sides = cells_ref.shape[0]
     owned, rank, width = basis_ref.shape

time: 28.9 us -> 28.9 us (level)
  no operation moved by 1% of the time
where the time goes in v11:
time: 28.9 us; the launch traced here: 28.6 us
  starting transfers between devices  12.3 us (43%)
  Pallas kernels  9.81 us (34%)
  waiting for transfers between devices  6.33 us (22%)
    all_to_all x2, starting transfers between devices, exchange(): lax.all_to_all(blocks, GROUP, split_axis=0, concat_axis=0, tiled=True)  10.9 us
    all_to_all x2, waiting for transfers between devices, exchange(): lax.all_to_all(blocks, GROUP, split_axis=0, concat_axis=0, tiled=True)  3.56 us
    pallas_call x1, Pallas kernels, shards(): pl.pallas_call(lambda *refs: direct_kernel(*refs, inner=inner), out_shape...  3.33 us
    pallas_call x1, Pallas kernels, shards(): pl.pallas_call(lambda *refs: mirror_kernel(*refs, inner=inner), out_shape...  2 us
    pallas_call x1, Pallas kernels, shards(): pl.pallas_call(lambda *refs: pack_kernel(*refs, inner=inner), out_shape=[...  1.6 us
    ppermute x1, waiting for transfers between devices, shards(): every_other = lax.ppermute(every, 'col', swap)  1.01 us
    pallas_call x1, Pallas kernels, shards(): pl.pallas_call(far_kernel, out_shape=shaped((devices, 1, 4, 128), f32), i...  0.99 us
    ppermute x1, waiting for transfers between devices, shards(): others = lax.ppermute(direct, 'col', swap)  0.93 us
  transfers between devices with their start and end apart: 6, of which 5 were waited for; matrix products, arithmetic and copies ran while one was open for 0% of the time, Pallas kernels for 24%

profile of v11, /device:TPU:0, one launch (start us, length us, event | category | flops | bytes accessed | tf_op | source)
XLA Modules:
  0.0 28.6 jit_solution(4093918354004990954)
XLA Ops:
  0.0 1.6 %pack.1 = (bf16[16,2,8,128]{3,2,1,0:T(8,128)(2,1)}, bf16[8,256]{1,0:T(8,128)(2,1)S(1)}, s32[2,1,128]{2,1,0:T(1,128)S(1)}, bf16[128,1024]{1,0:T(8,128)(2,1)S(1)}, bf16[48,128,128]{2,1,0:T(8,128)(2,1)S(1)}) custom-call(bf16[8,256]{1,0:T(8,128)(2,1)} %refs_0_.1, bf16[2,32,128]{2,1,0:T(8,128)(2,1)} %refs_3_.5, s32[1,128]{1,0:T(1,128)} %bitcast.11, ...), custom_call_target="tpu_custom_call" | custom-call | tf_op jit(solution)/shard_map/pack/pallas_call | solution.py:342
  1.6 7.4 %all-to-all-start = ((bf16[16,2,8,128]{3,2,1,0:T(8,128)(2,1)}), bf16[16,2,8,128]{3,2,1,0:T(8,128)(2,1)S(1)}, u32[]{:S(2)}, u32[]{:S(2)}) async-start(bf16[16,2,8,128]{3,2,1,0:T(8,128)(2,1)} %get-tuple-element.16), calls=%async_computation | async-start | bytes 131072 | tf_op jit(solution)/shard_map/all_to_all | solution.py:329
  9.0 0.4 %collective-permute-start = (bf16[8,256]{1,0:T(8,128)(2,1)S(1)}, bf16[8,256]{1,0:T(8,128)(2,1)S(1)}, u32[]{:S(2)}, u32[]{:S(2)}) collective-permute-start(bf16[8,256]{1,0:T(8,128)(2,1)S(1)} %get-tuple-element.24.refs_5_), channel_id=1, source_target_pairs={{0,1},{1,0},{2,3},{3,2},{4,5},{5,4},{6,7},{7,6},{8,9},{9,8},{10,11... | collective-permute-start | bytes 12296 | tf_op jit(solution)/shard_map/ppermute | solution.py:363
  9.4 0.8 %collective-permute-done.refs_6_ = bf16[8,256]{1,0:T(8,128)(2,1)S(1)} collective-permute-done((bf16[8,256]{1,0:T(8,128)(2,1)S(1)}, bf16[8,256]{1,0:T(8,128)(2,1)S(1)}, u32[]{:S(2)}, u32[]{:S(2)}) %collective-permute-start) | collective-permute-done | bytes 4128 | tf_op jit(solution)/shard_map/ppermute | solution.py:363
  10.2 2.0 %mirror.1 = (f32[16,2,4,128]{3,2,1,0:T(4,128)S(1)}, f32[16,2,4,128]{3,2,1,0:T(4,128)S(1)}) custom-call(s32[1,96]{1,0:T(1,128)} %bitcast.5, s32[1,96]{1,0:T(1,128)} %bitcast.7, s32[1,96]{1,0:T(1,128)} %bitcast.9, bf16[96,128,128]{2,1,0:T(8,128)(2,1)} %refs_3_.4, bf16[48,128,128]{2,1,0:T(8,128)(2,1)S(1)} %get-tuple-element.23.refs_4_, ...), custom_call_target="tpu_custom_call" | custom-call | flops 25165824 | bytes 10000000 | tf_op jit(solution)/shard_map/mirror/pallas_call | solution.py:378
  12.2 0.0 copy-start
  12.2 0.4 %collective-permute-start.1 = (f32[16,2,4,128]{3,2,1,0:T(4,128)S(1)}, f32[16,2,4,128]{3,2,1,0:T(4,128)S(1)}, u32[]{:S(2)}, u32[]{:S(2)}) collective-permute-start(f32[16,2,4,128]{3,2,1,0:T(4,128)S(1)} %get-tuple-element.26), channel_id=1, source_target_pairs={{0,1},{1,0},{2,3},{3,2},{4,5},{5,4},{6,7},{7,6},{8,9},{9,8},{10,11... | collective-permute-start | bytes 196616 | tf_op jit(solution)/shard_map/ppermute | solution.py:394
  12.7 0.5 %turn.1 = (f32[1024,128]{1,0:T(8,128)S(1)}, f32[1024,128]{1,0:T(8,128)S(1)}, bf16[128,512]{1,0:T(8,128)(2,1)S(1)}, bf16[512,64]{1,0:T(8,128)(2,1)S(1)}) custom-call(s32[2,1,128]{2,1,0:T(1,128)S(1)} %get-tuple-element.17.refs_0_, bf16[128,1024]{1,0:T(8,128)(2,1)S(1)} %get-tuple-element.18.refs_1_), custom_call_target="tpu_custom_call" | custom-call | flops 1000000 | bytes 3000000 | tf_op jit(solution)/shard_map/turn/pallas_call | solution.py:364
  13.1 2.5 %all-to-all-done.every_ref.refs_4_ = bf16[16,2,8,128]{3,2,1,0:T(8,128)(2,1)S(1)} async-done(((bf16[16,2,8,128]{3,2,1,0:T(8,128)(2,1)}), bf16[16,2,8,128]{3,2,1,0:T(8,128)(2,1)S(1)}, u32[]{:S(2)}, u32[]{:S(2)}) %all-to-all-start) | async-done | bytes 65568 | tf_op jit(solution)/shard_map/all_to_all | solution.py:329
  15.6 1.0 %far.1.far_ref = f32[16,1,4,128]{3,2,1,0:T(4,128)S(1)} custom-call(bf16[16,2,8,128]{3,2,1,0:T(8,128)(2,1)S(1)} %all-to-all-done.every_ref.refs_4_, bf16[128,512]{1,0:T(8,128)(2,1)S(1)} %get-tuple-element.19.gather_ref, bf16[512,64]{1,0:T(8,128)(2,1)S(1)} %get-tuple-element.20.spread_ref, f32[1024,128]{1,0:T(8,128)S(1)} %get-tuple-element.21.by_row_ref, ...), custom_call_target="tpu_custom_call" | custom-call | flops 1000000 | bytes 3000000 | tf_op jit(solution)/shard_map/far/pallas_call | solution.py:395
  16.6 0.0 collective-permute-done.1.got_ref
  16.6 0.7 %join.1 = f32[16,3,4,128]{3,2,1,0:T(4,128)} custom-call(f32[16,1,4,128]{3,2,1,0:T(4,128)S(1)} %far.1.far_ref, f32[16,2,4,128]{3,2,1,0:T(4,128)S(1)} %get-tuple-element.25.keep_ref, f32[16,2,4,128]{3,2,1,0:T(4,128)S(1)} %collective-permute-done.1.got_ref), custom_call_target="tpu_custom_call" | custom-call | tf_op jit(solution)/shard_map/join/pallas_call | solution.py:405
  17.3 3.5 %all-to-all-start.1 = ((f32[16,3,4,128]{3,2,1,0:T(4,128)}), f32[16,3,4,128]{3,2,1,0:T(4,128)S(1)}, u32[]{:S(2)}, u32[]{:S(2)}) async-start(f32[16,3,4,128]{3,2,1,0:T(4,128)} %join.1), calls=%async_computation.1 | async-start | bytes 196608 | tf_op jit(solution)/shard_map/all_to_all | solution.py:329
  20.8 0.3 %collective-permute-start.2 = (bf16[16,2,8,128]{3,2,1,0:T(8,128)(2,1)S(1)}, bf16[16,2,8,128]{3,2,1,0:T(8,128)(2,1)S(1)}, u32[]{:S(2)}, u32[]{:S(2)}) collective-permute-start(bf16[16,2,8,128]{3,2,1,0:T(8,128)(2,1)S(1)} %all-to-all-done.every_ref.refs_4_), channel_id=1, source_target_pairs={{0,1},{1,0},{2,3},{3,2},{4,5},{5,4},{6,7},{7,6},{8,9},{9,8},{10,11... | collective-permute-start | bytes 196616 | tf_op jit(solution)/shard_map/ppermute | solution.py:415
  21.1 1.0 %collective-permute-done.2.refs_5_ = bf16[16,2,8,128]{3,2,1,0:T(8,128)(2,1)S(1)} collective-permute-done((bf16[16,2,8,128]{3,2,1,0:T(8,128)(2,1)S(1)}, bf16[16,2,8,128]{3,2,1,0:T(8,128)(2,1)S(1)}, u32[]{:S(2)}, u32[]{:S(2)}) %collective-permute-start.2) | collective-permute-done | bytes 65568 | tf_op jit(solution)/shard_map/ppermute | solution.py:415
  22.2 3.3 %direct.1.refs_1_ = f32[4,8,128]{2,1,0:T(8,128)S(1)} custom-call(s32[1,96]{1,0:T(1,128)} %bitcast.6, s32[1,96]{1,0:T(1,128)} %bitcast.8, s32[1,96]{1,0:T(1,128)} %bitcast.10, bf16[96,128,128]{2,1,0:T(8,128)(2,1)} %refs_3_.4, bf16[16,2,8,128]{3,2,1,0:T(8,128)(2,1)S(1)} %all-to-all-done.every_ref.refs_4_, ...), custom_call_target="tpu_custom_call" | custom-call | flops 25165824 | bytes 10000000 | tf_op jit(solution)/shard_map/direct/pallas_call | solution.py:416
  25.5 0.3 %collective-permute-start.3 = (f32[4,8,128]{2,1,0:T(8,128)S(1)}, f32[4,8,128]{2,1,0:T(8,128)S(1)}, u32[]{:S(2)}, u32[]{:S(2)}) collective-permute-start(f32[4,8,128]{2,1,0:T(8,128)S(1)} %direct.1.refs_1_), channel_id=1, source_target_pairs={{0,1},{1,0},{2,3},{3,2},{4,5},{5,4},{6,7},{7,6},{8,9},{9,8},{10,11... | collective-permute-start | bytes 49160 | tf_op jit(solution)/shard_map/ppermute | solution.py:431
  25.8 0.9 %collective-permute-done.3.refs_2_ = f32[4,8,128]{2,1,0:T(8,128)S(1)} collective-permute-done((f32[4,8,128]{2,1,0:T(8,128)S(1)}, f32[4,8,128]{2,1,0:T(8,128)S(1)}, u32[]{:S(2)}, u32[]{:S(2)}) %collective-permute-start.3) | collective-permute-done | bytes 16416 | tf_op jit(solution)/shard_map/ppermute | solution.py:431
  26.7 1.1 %all-to-all-done.1.refs_0_ = f32[16,3,4,128]{3,2,1,0:T(4,128)S(1)} async-done(((f32[16,3,4,128]{3,2,1,0:T(4,128)}), f32[16,3,4,128]{3,2,1,0:T(4,128)S(1)}, u32[]{:S(2)}, u32[]{:S(2)}) %all-to-all-start.1) | async-done | bytes 98336 | tf_op jit(solution)/shard_map/all_to_all | solution.py:329
  27.8 0.0 copy-done
  27.8 0.8 %finish.1 = f32[8,256]{1,0:T(8,128)} custom-call(f32[16,3,4,128]{3,2,1,0:T(4,128)S(1)} %all-to-all-done.1.refs_0_, f32[4,8,128]{2,1,0:T(8,128)S(1)} %direct.1.refs_1_, f32[4,8,128]{2,1,0:T(8,128)S(1)} %collective-permute-done.3.refs_2_, bf16[2,32,128]{2,1,0:T(8,128)(2,1)S(1)} %copy-done), custom_call_target="tpu_custom_call" | custom-call | tf_op jit(solution)/shard_map/finish/pallas_call | solution.py:432
Async XLA Ops:
  1.6 14.0 %all-to-all-start = ((bf16[16,2,8,128]{3,2,1,0:T(8,128)(2,1)}), bf16[16,2,8,128]{3,2,1,0:T(8,128)(2,1)S(1)}, u32[]{:S(2)}, u32[]{:S(2)}) async-start(bf16[16,2,8,128]{3,2,1,0:T(8,128)(2,1)} %get-tuple-element.16), calls=%async_computation | async-start | bytes 131072 | tf_op jit(solution)/shard_map/all_to_all | solution.py:329
  9.0 1.2 %collective-permute-start = (bf16[8,256]{1,0:T(8,128)(2,1)S(1)}, bf16[8,256]{1,0:T(8,128)(2,1)S(1)}, u32[]{:S(2)}, u32[]{:S(2)}) collective-permute-start(bf16[8,256]{1,0:T(8,128)(2,1)S(1)} %get-tuple-element.24.refs_5_), channel_id=1, source_target_pairs={{0,1},{1,0},{2,3},{3,2},{4,5},{5,4},{6,7},{7,6},{8,9},{9,8},{10,11... | collective-permute-start | bytes 12296 | tf_op jit(solution)/shard_map/ppermute | solution.py:363
  12.2 15.6 %copy-start = (bf16[2,32,128]{2,1,0:T(8,128)(2,1)S(1)}, bf16[2,32,128]{2,1,0:T(8,128)(2,1)}, u32[]{:S(2)}) copy-start(bf16[2,32,128]{2,1,0:T(8,128)(2,1)} %refs_3_.5) | copy-start | bytes 49156
  12.2 4.4 %collective-permute-start.1 = (f32[16,2,4,128]{3,2,1,0:T(4,128)S(1)}, f32[16,2,4,128]{3,2,1,0:T(4,128)S(1)}, u32[]{:S(2)}, u32[]{:S(2)}) collective-permute-start(f32[16,2,4,128]{3,2,1,0:T(4,128)S(1)} %get-tuple-element.26), channel_id=1, source_target_pairs={{0,1},{1,0},{2,3},{3,2},{4,5},{5,4},{6,7},{7,6},{8,9},{9,8},{10,11... | collective-permute-start | bytes 196616 | tf_op jit(solution)/shard_map/ppermute | solution.py:394
  17.3 10.5 %all-to-all-start.1 = ((f32[16,3,4,128]{3,2,1,0:T(4,128)}), f32[16,3,4,128]{3,2,1,0:T(4,128)S(1)}, u32[]{:S(2)}, u32[]{:S(2)}) async-start(f32[16,3,4,128]{3,2,1,0:T(4,128)} %join.1), calls=%async_computation.1 | async-start | bytes 196608 | tf_op jit(solution)/shard_map/all_to_all | solution.py:329
  20.8 1.3 %collective-permute-start.2 = (bf16[16,2,8,128]{3,2,1,0:T(8,128)(2,1)S(1)}, bf16[16,2,8,128]{3,2,1,0:T(8,128)(2,1)S(1)}, u32[]{:S(2)}, u32[]{:S(2)}) collective-permute-start(bf16[16,2,8,128]{3,2,1,0:T(8,128)(2,1)S(1)} %all-to-all-done.every_ref.refs_4_), channel_id=1, source_target_pairs={{0,1},{1,0},{2,3},{3,2},{4,5},{5,4},{6,7},{7,6},{8,9},{9,8},{10,11... | collective-permute-start | bytes 196616 | tf_op jit(solution)/shard_map/ppermute | solution.py:415
  25.5 1.2 %collective-permute-start.3 = (f32[4,8,128]{2,1,0:T(8,128)S(1)}, f32[4,8,128]{2,1,0:T(8,128)S(1)}, u32[]{:S(2)}, u32[]{:S(2)}) collective-permute-start(f32[4,8,128]{2,1,0:T(8,128)S(1)} %direct.1.refs_1_), channel_id=1, source_target_pairs={{0,1},{1,0},{2,3},{3,2},{4,5},{5,4},{6,7},{7,6},{8,9},{9,8},{10,11... | collective-permute-start | bytes 49160 | tf_op jit(solution)/shard_map/ppermute | solution.py:431
